TPU v7x, 32 devices: a whole 2x2x4 slice. The times are simulated.
32 devices in a mesh: range: 2 (over y), radial: 16 (over z, x, core).
Axes of the slice: x: 2, y: 2, z: 4, core: 2. Of those that a mesh axis runs over, the one named last changes fastest.
Arguments:
- field_start: bfloat16 [2, 1024, 1024], P(None, 'radial'), may hold values from -6 to 6
- phase_table: float32 [16, 1024], replicated, may hold values from -1.5 to 1.5
- profile_index: int32 [2, 2], replicated, may hold values from 0 to 15
- group_power: float32 [2], replicated, may hold values from 0.3 to 3
- group_slot: int32 [2], replicated, may hold values from 0 to 1, each once
- source_shift: int32 [2, 16], P('range'), may hold values from 0 to 15
- slot_sub: int32 [2, 16, 16], P('range'), may hold values from 0 to 3
- tile_count: int32 [2, 16], P('range'), may hold values from 1 to 16, as said below
- row_weights: bfloat16 [2, 16, 16, 16, 256], P('range', 'radial'), may hold values from -0.375 to 0.375
- col_weights: bfloat16 [2, 16, 16, 256, 256], P('range', 'radial'), may hold values from -0.375 to 0.375
Outputs:
- interference: float32 [2, 16, 256, 256], P('range', 'radial')
Inputs may be any that keep to these rules, and one draw needn't show every extreme that they name: `tile_count`: in every slab some tile uses all 16 slots.
All inputs are finite; a program needn't handle non-finite values.
Results may differ from a plain program's by a relative error of at most 0.04.
Values may be sent and summed in bfloat16 or wider, within the bound.
No kernel may reach another device: no remote copies, remote signals or barrier semaphores. Data moves between devices by JAX's collectives and lax.ppermute only.
A program may use at most 64 MiB of HBM per device.

v0:
```python
import math

import jax
import jax.numpy as jnp
from jax import lax
from jax.sharding import PartitionSpec as P

VB = 128
SUB = 16
K_MAX = 16
CAP = 2
GROUP_RADIALS = 512


spread_angle = 6.0
absorb_rate = 0.5


def dft_tables(height):
    block_rows = height // 8
    column_ids = jnp.arange(height, dtype=jnp.int32)
    factor = 1.0 / math.sqrt(height)

    def table_block(block_index):
        row_ids = block_index * block_rows + jnp.arange(block_rows, dtype=jnp.int32)
        product = row_ids[:, None] * column_ids[None, :] % height
        angle = 2.0 * math.pi / height * product.astype(jnp.float32)
        return (
            (jnp.cos(angle) * factor).astype(jnp.bfloat16),
            (jnp.sin(angle) * factor).astype(jnp.bfloat16),
        )

    cos_blocks, sin_blocks = lax.map(table_block, jnp.arange(8, dtype=jnp.int32))
    return (cos_blocks.reshape(height, height), sin_blocks.reshape(height, height))


def spectral_phase(height):
    index_row = jnp.arange(height, dtype=jnp.int32)
    folded = jnp.minimum(index_row, height - index_row).astype(jnp.float32)
    theta = -spread_angle * (2.0 * folded / height) ** 2
    return (jnp.cos(theta), jnp.sin(theta))


def absorber_profile(height):
    level = jnp.arange(height, dtype=jnp.int32).astype(jnp.float32)
    depth = jnp.maximum(0.0, (level - 0.9375 * height) / (0.0625 * height))
    return jnp.exp(-absorb_rate * depth * depth)


def march_slab(
    field, radial_gain, phases, cosine_table, sine_table, spectral_cos, spectral_sin, absorber, band
):
    real_part = field[0]
    imag_part = field[1]
    row_total = real_part.shape[0]
    bands = []
    for step_index in range(phases.shape[0]):
        phase_cos = jnp.cos(phases[step_index])
        phase_sin = jnp.sin(phases[step_index])
        real_wide = real_part.astype(jnp.float32)
        imag_wide = imag_part.astype(jnp.float32)
        screened = jnp.concatenate(
            [
                real_wide * phase_cos - imag_wide * phase_sin,
                real_wide * phase_sin + imag_wide * phase_cos,
            ],
            0,
        ).astype(jnp.bfloat16)
        with_cos = jnp.dot(screened, cosine_table, preferred_element_type=jnp.float32)
        with_sin = jnp.dot(screened, sine_table, preferred_element_type=jnp.float32)
        spec_real = with_cos[:row_total] + with_sin[row_total:]
        spec_imag = with_cos[row_total:] - with_sin[:row_total]
        moved = jnp.concatenate(
            [
                spec_real * spectral_cos - spec_imag * spectral_sin,
                spec_real * spectral_sin + spec_imag * spectral_cos,
            ],
            0,
        ).astype(jnp.bfloat16)
        back_cos = jnp.dot(moved, cosine_table, preferred_element_type=jnp.float32)
        back_sin = jnp.dot(moved, sine_table, preferred_element_type=jnp.float32)
        real_part = ((back_cos[:row_total] - back_sin[row_total:]) * absorber).astype(jnp.bfloat16)
        imag_part = ((back_cos[row_total:] + back_sin[:row_total]) * absorber).astype(jnp.bfloat16)
        real_low = real_part.astype(jnp.float32)[:, :band]
        imag_low = imag_part.astype(jnp.float32)[:, :band]
        bands.append(
            (radial_gain[:, None] * (real_low * real_low + imag_low * imag_low)).astype(
                jnp.bfloat16
            )
        )
    return (jnp.stack([real_part, imag_part]), jnp.concatenate(bands, axis=1))


def per_device(
    field_start,
    phase_table,
    profile_index,
    group_power,
    group_slot,
    source_shift,
    slot_sub,
    tile_count,
    row_weights,
    col_weights,
):
    radial_size = lax.axis_size("radial")
    range_size = lax.axis_size("range")
    slab_index = lax.axis_index("range")
    radial_index = lax.axis_index("radial")
    height = field_start.shape[2]
    local_rows = field_start.shape[1]
    group_total = group_power.shape[0]
    cosine_table, sine_table = dft_tables(height)
    spectral_cos, spectral_sin = spectral_phase(height)
    absorber = absorber_profile(height)
    profile_count = phase_table.shape[0]
    selector = (
        profile_index[:, :, None, None]
        == jnp.arange(profile_count, dtype=jnp.int32)[None, None, :, None]
    )
    all_phases = jnp.sum(
        jnp.where(
            selector, phase_table[None, None, :, :], jnp.zeros_like(phase_table)[None, None, :, :]
        ),
        axis=2,
    )
    global_radial = radial_index * local_rows + jnp.arange(local_rows, dtype=jnp.int32)
    group_place = global_radial // GROUP_RADIALS
    group_range = jnp.arange(group_total, dtype=jnp.int32)
    group_ids = jnp.sum(
        jnp.where(group_place[:, None] == group_range[None, :], group_slot[None, :], 0), axis=1
    )
    radial_gain = jnp.sum(
        jnp.where(
            group_ids[:, None] == group_range[None, :],
            group_power[None, :],
            jnp.zeros_like(group_power)[None, :],
        ),
        axis=1,
    )
    channels = all_phases.shape[1] * VB
    share_rows = local_rows // range_size
    share_start = slab_index * share_rows
    field = lax.dynamic_slice_in_dim(field_start, share_start, share_rows, 1)
    share_gain = lax.dynamic_slice_in_dim(radial_gain, share_start, share_rows, 0)
    slab_bands = []
    for slab_number in range(range_size):
        field, bands = march_slab(
            field,
            share_gain,
            all_phases[slab_number],
            cosine_table,
            sine_table,
            spectral_cos,
            spectral_sin,
            absorber,
            VB,
        )
        slab_bands.append(bands)
    stacked = jnp.stack(slab_bands)
    arrived = lax.all_to_all(stacked, "range", split_axis=0, concat_axis=0, tiled=True)
    polar = arrived.reshape(local_rows, channels)
    slot_ids = jnp.arange(K_MAX, dtype=jnp.int32)
    own_shift = source_shift[0, radial_index]
    own_count = tile_count[0, radial_index]
    own_subs = slot_sub[0, radial_index]
    source = (radial_index + own_shift + slot_ids // CAP) % radial_size
    every_block = lax.all_gather(polar, "radial", axis=0, tiled=True)
    row_index = (
        source[:, None] * local_rows
        + own_subs[:, None] * SUB
        + jnp.arange(SUB, dtype=jnp.int32)[None, :]
    )
    pieces = every_block[row_index]
    is_live = slot_ids < own_count
    pieces = jnp.where(is_live[:, None, None], pieces, jnp.zeros_like(pieces))
    mixed = jnp.einsum(
        "ksc,kcp->ksp", pieces, col_weights[0, 0], preferred_element_type=jnp.float32
    ).astype(jnp.bfloat16)
    tile_value = jnp.einsum(
        "ksp,ksq->pq", row_weights[0, 0], mixed, preferred_element_type=jnp.float32
    )
    return tile_value.reshape(1, 1, tile_value.shape[0], tile_value.shape[1])


def solution(mesh):
    return jax.shard_map(
        per_device,
        mesh=mesh,
        in_specs=(
            P(None, "radial", None),
            P(),
            P(),
            P(),
            P(),
            P("range", None),
            P("range", None, None),
            P("range", None),
            P("range", "radial", None, None, None),
            P("range", "radial", None, None, None),
        ),
        out_specs=P("range", "radial", None, None),
        check_vma=False,
    )
```

profile of v0, /device:TPU:0, one launch (start us, length us, event | category | flops | bytes accessed | tf_op | source)
XLA Modules:
  0.0 86.9 jit_solution(122945805446404835)
XLA Ops:
  0.1 0.9 %iota_compare_fusion = pred[2,2,16]{2,1,0:T(4,128)(4,1)S(1)} fusion(s32[2,2]{1,0:T(2,128)} %param.14), kind=kLoop, calls=%fused_computation.152 | loop fusion | flops 64 | bytes 80 | tf_op jit(solution)/shard_map/eq | solution.py:118
  1.0 1.0 %select_reduce_fusion = f32[2,2,1024]{2,1,0:T(2,128)S(1)} fusion(f32[16,1024]{1,0:T(8,128)} %param.13, pred[2,2,16]{2,1,0:T(4,128)(4,1)S(1)} %iota_compare_fusion), kind=kLoop, calls=%fused_computation.21 | loop fusion | flops 126976 | bytes 81984 | tf_op jit(solution)/shard_map/reduce_sum | solution.py:121
  2.4 36.4 %while.15 = (s32[]{:T(128)}, bf16[8,128,1024]{2,1,0:T(8,128)(2,1)}, bf16[8,128,1024]{2,1,0:T(8,128)(2,1)}, s32[8]{0:T(128)S(1)}, s32[]{:T(128)}, /*index=5*/s32[1]{0:T(128)}) while((s32[]{:T(128)}, bf16[8,128,1024]{2,1,0:T(8,128)(2,1)}, bf16[8,128,1024]{2,1,0:T(8,128)(2,1)}, s32[8]{0:T(128)S(1)}, s32[]{:T(128)}, ...), condition=%wide.region_4.5_spmd.clone, body=%wide.region_3.4_spmd.clone.sunk | while | flops 2359427 | bytes 525421 | solution.py:33
  2.5 0.7 dynamic_slice.38
  3.8 3.2 %fusion.133 = (bf16[8,128,1024]{2,1,0:T(8,128)(2,1)}, bf16[8,128,1024]{2,1,0:T(8,128)(2,1)}) fusion(bf16[8,128,1024]{2,1,0:T(8,128)(2,1)} %get-tuple-element.170, s32[]{:T(128)S(6)} %copy.19, s32[128]{0:T(128)S(1)} %iota_add_fusion.2, bf16[8,128,1024]{2,1,0:T(8,128)(2,1)} %get-tuple-element.169), kind=kLoop, calls=%fused_computation.15.clone.1 | loop fusion | flops 2359296 | bytes 524804 | tf_op jit(solution)/shard_map/while/body/jit(dynamic_update_index_in_dim)/dynamic_update_slice | solution.py:33
  7.0 0.7 dynamic_slice.38
  8.4 3.2 %fusion.133 = (bf16[8,128,1024]{2,1,0:T(8,128)(2,1)}, bf16[8,128,1024]{2,1,0:T(8,128)(2,1)}) fusion(bf16[8,128,1024]{2,1,0:T(8,128)(2,1)} %get-tuple-element.170, s32[]{:T(128)S(6)} %copy.19, s32[128]{0:T(128)S(1)} %iota_add_fusion.2, bf16[8,128,1024]{2,1,0:T(8,128)(2,1)} %get-tuple-element.169), kind=kLoop, calls=%fused_computation.15.clone.1 | loop fusion | flops 2359296 | bytes 524804 | tf_op jit(solution)/shard_map/while/body/jit(dynamic_update_index_in_dim)/dynamic_update_slice | solution.py:33
  11.5 0.7 dynamic_slice.38
  12.9 3.2 %fusion.133 = (bf16[8,128,1024]{2,1,0:T(8,128)(2,1)}, bf16[8,128,1024]{2,1,0:T(8,128)(2,1)}) fusion(bf16[8,128,1024]{2,1,0:T(8,128)(2,1)} %get-tuple-element.170, s32[]{:T(128)S(6)} %copy.19, s32[128]{0:T(128)S(1)} %iota_add_fusion.2, bf16[8,128,1024]{2,1,0:T(8,128)(2,1)} %get-tuple-element.169), kind=kLoop, calls=%fused_computation.15.clone.1 | loop fusion | flops 2359296 | bytes 524804 | tf_op jit(solution)/shard_map/while/body/jit(dynamic_update_index_in_dim)/dynamic_update_slice | solution.py:33
  16.1 0.7 dynamic_slice.38
  17.5 3.2 %fusion.133 = (bf16[8,128,1024]{2,1,0:T(8,128)(2,1)}, bf16[8,128,1024]{2,1,0:T(8,128)(2,1)}) fusion(bf16[8,128,1024]{2,1,0:T(8,128)(2,1)} %get-tuple-element.170, s32[]{:T(128)S(6)} %copy.19, s32[128]{0:T(128)S(1)} %iota_add_fusion.2, bf16[8,128,1024]{2,1,0:T(8,128)(2,1)} %get-tuple-element.169), kind=kLoop, calls=%fused_computation.15.clone.1 | loop fusion | flops 2359296 | bytes 524804 | tf_op jit(solution)/shard_map/while/body/jit(dynamic_update_index_in_dim)/dynamic_update_slice | solution.py:33
  20.6 0.7 dynamic_slice.38
  22.0 3.2 %fusion.133 = (bf16[8,128,1024]{2,1,0:T(8,128)(2,1)}, bf16[8,128,1024]{2,1,0:T(8,128)(2,1)}) fusion(bf16[8,128,1024]{2,1,0:T(8,128)(2,1)} %get-tuple-element.170, s32[]{:T(128)S(6)} %copy.19, s32[128]{0:T(128)S(1)} %iota_add_fusion.2, bf16[8,128,1024]{2,1,0:T(8,128)(2,1)} %get-tuple-element.169), kind=kLoop, calls=%fused_computation.15.clone.1 | loop fusion | flops 2359296 | bytes 524804 | tf_op jit(solution)/shard_map/while/body/jit(dynamic_update_index_in_dim)/dynamic_update_slice | solution.py:33
  25.2 0.7 dynamic_slice.38
  26.5 3.2 %fusion.133 = (bf16[8,128,1024]{2,1,0:T(8,128)(2,1)}, bf16[8,128,1024]{2,1,0:T(8,128)(2,1)}) fusion(bf16[8,128,1024]{2,1,0:T(8,128)(2,1)} %get-tuple-element.170, s32[]{:T(128)S(6)} %copy.19, s32[128]{0:T(128)S(1)} %iota_add_fusion.2, bf16[8,128,1024]{2,1,0:T(8,128)(2,1)} %get-tuple-element.169), kind=kLoop, calls=%fused_computation.15.clone.1 | loop fusion | flops 2359296 | bytes 524804 | tf_op jit(solution)/shard_map/while/body/jit(dynamic_update_index_in_dim)/dynamic_update_slice | solution.py:33
  29.7 0.7 dynamic_slice.38
  31.1 3.2 %fusion.133 = (bf16[8,128,1024]{2,1,0:T(8,128)(2,1)}, bf16[8,128,1024]{2,1,0:T(8,128)(2,1)}) fusion(bf16[8,128,1024]{2,1,0:T(8,128)(2,1)} %get-tuple-element.170, s32[]{:T(128)S(6)} %copy.19, s32[128]{0:T(128)S(1)} %iota_add_fusion.2, bf16[8,128,1024]{2,1,0:T(8,128)(2,1)} %get-tuple-element.169), kind=kLoop, calls=%fused_computation.15.clone.1 | loop fusion | flops 2359296 | bytes 524804 | tf_op jit(solution)/shard_map/while/body/jit(dynamic_update_index_in_dim)/dynamic_update_slice | solution.py:33
  34.3 0.7 dynamic_slice.38
  35.6 3.2 %fusion.133 = (bf16[8,128,1024]{2,1,0:T(8,128)(2,1)}, bf16[8,128,1024]{2,1,0:T(8,128)(2,1)}) fusion(bf16[8,128,1024]{2,1,0:T(8,128)(2,1)} %get-tuple-element.170, s32[]{:T(128)S(6)} %copy.19, s32[128]{0:T(128)S(1)} %iota_add_fusion.2, bf16[8,128,1024]{2,1,0:T(8,128)(2,1)} %get-tuple-element.169), kind=kLoop, calls=%fused_computation.15.clone.1 | loop fusion | flops 2359296 | bytes 524804 | tf_op jit(solution)/shard_map/while/body/jit(dynamic_update_index_in_dim)/dynamic_update_slice | solution.py:33
  38.9 2.2 %fusion.52 = f32[64,1024]{1,0:T(8,128)S(1)} fusion(bf16[1024,1024]{1,0:T(8,128)(2,1)} %bitcast.81, bf16[32,1024]{1,0:T(8,128)(2,1)S(1)} %get-tuple-element.112, bf16[32,1024]{1,0:T(8,128)(2,1)S(1)} %get-tuple-element.111), kind=kOutput, calls=%fused_computation.95 | convolution fusion | flops 134479872 | bytes 2490368 | tf_op jit(solution)/shard_map/dot_general | solution.py:70
  41.6 1.0 %copy-done.2 = bf16[8,128,1024]{2,1,0:T(8,128)(2,1)S(1)} copy-done((bf16[8,128,1024]{2,1,0:T(8,128)(2,1)S(1)}, bf16[8,128,1024]{2,1,0:T(8,128)(2,1)}, u32[]{:S(2)}) %copy-start.2) | copy-done | bytes 2097176
  49.9 0.8 fusion.82
  50.7 0.7 fusion.83
  51.7 0.6 pad_maximum_fusion.24
  52.3 4.2 %all-to-all-start = ((bf16[2,32,256]{2,1,0:T(8,128)(2,1)}), bf16[2,32,256]{2,1,0:T(8,128)(2,1)S(1)}, u32[]{:S(2)}, u32[]{:S(2)}) async-start(bf16[2,32,256]{2,1,0:T(8,128)(2,1)} %pad_maximum_fusion.24), calls=%async_computation | async-start | bytes 65536 | tf_op jit(solution)/shard_map/all_to_all | solution.py:161
  56.5 0.6 constant_dynamic-slice_fusion.1
  57.8 0.7 fusion.87
  59.2 1.3 %all-to-all-done = bf16[2,32,256]{2,1,0:T(8,128)(2,1)S(1)} async-done(((bf16[2,32,256]{2,1,0:T(8,128)(2,1)}), bf16[2,32,256]{2,1,0:T(8,128)(2,1)S(1)}, u32[]{:S(2)}, u32[]{:S(2)}) %all-to-all-start) | async-done | bytes 32800 | tf_op jit(solution)/shard_map/all_to_all | solution.py:161
  60.5 23.7 %all_gather.3 = bf16[1024,256]{1,0:T(8,128)(2,1)S(1)} all-gather(bf16[64,256]{1,0:T(8,128)(2,1)S(1)} %bitcast.90), channel_id=1, replica_groups=mesh['range'=2,'radial'=16] {'radial'}, dimensions={0}, use_global_device_ids=true | all-gather | bytes 557056 | tf_op jit(solution)/shard_map/all_gather | solution.py:168
  84.2 1.1 %gather_fusion = bf16[256,256]{1,0:T(8,128)(2,1)S(1)} fusion(bf16[1024,256]{1,0:T(8,128)(2,1)S(1)} %all_gather.3, s32[1024]{0:T(1024)S(1)} %pad_clamp_fusion), kind=kCustom, calls=%fused_computation | custom fusion | bytes 263168 | tf_op jit(solution)/shard_map/gather | solution.py:174
  85.3 0.7 convolution_bitcast_fusion
  86.0 0.8 copy.13
  (65 shorter events, 9.1 us)
Async XLA Ops:
  0.0 85.3 %copy-start = (bf16[1,1,16,256,256]{4,3,2,1,0:T(8,128)(2,1)S(1)}, bf16[1,1,16,256,256]{4,3,2,1,0:T(8,128)(2,1)}, u32[]{:S(2)}) copy-start(bf16[1,1,16,256,256]{4,3,2,1,0:T(8,128)(2,1)} %param.21) | copy-start | bytes 6291460
  0.0 38.8 %copy-start.4 = (bf16[2,64,1024]{2,1,0:T(8,128)(2,1)S(1)}, bf16[2,64,1024]{2,1,0:T(8,128)(2,1)}, u32[]{:S(2)}) copy-start(bf16[2,64,1024]{2,1,0:T(8,128)(2,1)} %param.12) | copy-start | bytes 786436
  38.8 2.3 %copy-start.1 = (bf16[8,128,1024]{2,1,0:T(8,128)(2,1)S(1)}, bf16[8,128,1024]{2,1,0:T(8,128)(2,1)}, u32[]{:S(2)}) copy-start(bf16[8,128,1024]{2,1,0:T(8,128)(2,1)} %get-tuple-element.72) | copy-start | bytes 6291460
  41.1 1.6 %copy-start.2 = (bf16[8,128,1024]{2,1,0:T(8,128)(2,1)S(1)}, bf16[8,128,1024]{2,1,0:T(8,128)(2,1)}, u32[]{:S(2)}) copy-start(bf16[8,128,1024]{2,1,0:T(8,128)(2,1)} %get-tuple-element.73) | copy-start | bytes 6291460
  49.4 7.1 %copy-start.5 = (s32[1,16]{1,0:T(1,128)S(1)}, s32[1,16]{1,0:T(1,128)}, u32[]{:S(2)}) copy-start(s32[1,16]{1,0:T(1,128)} %param.17) | copy-start | bytes 196
  49.4 7.1 %copy-start.6 = (s32[1,16]{1,0:T(1,128)S(1)}, s32[1,16]{1,0:T(1,128)}, u32[]{:S(2)}) copy-start(s32[1,16]{1,0:T(1,128)} %param.19) | copy-start | bytes 196
  49.9 35.4 %copy-start.3 = (bf16[1,1,16,16,256]{4,3,2,1,0:T(8,128)(2,1)S(1)}, bf16[1,1,16,16,256]{4,3,2,1,0:T(8,128)(2,1)}, u32[]{:S(2)}) copy-start(bf16[1,1,16,16,256]{4,3,2,1,0:T(8,128)(2,1)} %param.20) | copy-start | bytes 393220
  52.3 8.2 %all-to-all-start = ((bf16[2,32,256]{2,1,0:T(8,128)(2,1)}), bf16[2,32,256]{2,1,0:T(8,128)(2,1)S(1)}, u32[]{:S(2)}, u32[]{:S(2)}) async-start(bf16[2,32,256]{2,1,0:T(8,128)(2,1)} %pad_maximum_fusion.24), calls=%async_computation | async-start | bytes 65536 | tf_op jit(solution)/shard_map/all_to_all | solution.py:161
where the time goes:
time: 87.3 us; the launch traced here: 86.9 us
  other arithmetic  31.4 us (36%)
  blocking collectives  23.7 us (27%)
  matrix products  10 us (11%)
  local copies, waits for them, and re-layouts  9.64 us (11%)
  loops' own time  5.63 us (6%)
  starting transfers between devices  4.23 us (5%)
  waiting for transfers between devices  1.26 us (1%)
  between operations  0.99 us (1%)
    dynamic_update_slice x8, other arithmetic, dft_tables(): lax.map(table_block, jnp.arange(8, dtype=jnp.int32))  25.4 us
    all_gather x1, blocking collectives, per_device(): every_block = lax.all_gather(polar, 'radial', axis=0, tiled=True)  23.7 us
    another operation x1, loops' own time, dft_tables(): lax.map(table_block, jnp.arange(8, dtype=jnp.int32))  5.63 us
    dynamic_slice x8, local copies, waits for them, and re-layouts, dft_tables(): lax.map(table_block, jnp.arange(8, dtype=jnp.int32))  5.31 us
    all_to_all x1, starting transfers between devices, per_device(): lax.all_to_all(stacked, 'range', split_axis=0, concat_axis=0, tiled=True)  4.23 us
    dot_general x4, matrix products, march_slab(): with_sin = jnp.dot(screened, sine_table, preferred_element_type=jnp.float32)  3.63 us
    dot_general x4, matrix products, march_slab(): back_cos = jnp.dot(moved, cosine_table, preferred_element_type=jnp.float32)  1.91 us
    dot_general x4, matrix products, march_slab(): jnp.dot(screened, cosine_table, preferred_element_type=jnp.float32)  1.91 us
  transfers between devices with their start and end apart: 1, of which 1 were waited for; matrix products, arithmetic and copies ran while one was open for 2% of the time, Pallas kernels for 0%

commit v1 on v0

v1 whole, which is shorter than its diff:
```python
import functools
import math

import jax
import jax.numpy as jnp
import numpy as np
from jax import lax
from jax.experimental import pallas as pl
from jax.experimental.pallas import tpu as pltpu
from jax.sharding import PartitionSpec as P

VB = 128
SUB = 16
K_MAX = 16
CAP = 2
GROUP_RADIALS = 512
RADIX = 4

spread_angle = 6.0
absorb_rate = 0.5


def march_constants(height):
    quarter = height // RADIX
    index = np.arange(quarter)
    angle = 2.0 * np.pi / quarter * (index[:, None] * index[None, :] % quarter)
    factor = 1.0 / math.sqrt(height)
    cosine, sine = np.cos(angle) * factor, np.sin(angle) * factor
    weights = np.block([[cosine, -sine], [sine, cosine]]).astype(jnp.bfloat16)
    turn = 2.0 * np.pi / height * (np.arange(RADIX)[:, None] * index[None, :])
    level = np.arange(height)
    folded = np.minimum(level, height - level).astype(np.float64)
    theta = -spread_angle * (2.0 * folded / height) ** 2
    theta = theta.reshape(quarter, RADIX).T
    depth = np.maximum(0.0, (level - 0.9375 * height) / (0.0625 * height))
    absorber = np.exp(-absorb_rate * depth * depth).reshape(1, height)
    waves = np.concatenate([np.cos(turn), np.sin(turn), np.cos(theta), np.sin(theta)], 0)
    return weights, waves.astype(np.float32), absorber.astype(np.float32)


def cos_sin(angle):
    square = angle * angle
    cosine = jnp.full_like(angle, 1.0 / math.factorial(14) * -1.0)
    for order in (12, 10, 8, 6, 4, 2, 0):
        cosine = cosine * square + (-1.0) ** (order // 2) / math.factorial(order)
    sine = jnp.full_like(angle, 1.0 / math.factorial(13))
    for order in (11, 9, 7, 5, 3, 1):
        sine = sine * square + (-1.0) ** (order // 2) / math.factorial(order)
    return cosine, sine * angle


def march_kernel(
    steps,
    slabs,
    profile_ref,
    power_ref,
    slot_ref,
    field_ref,
    phase_ref,
    weight_ref,
    wave_ref,
    absorb_ref,
    polar_ref,
    phase_rows,
    screen_cos,
    screen_sin,
    real_ref,
    imag_ref,
    mixed_ref,
    moved_ref,
):
    rows, height = field_ref.shape[1:]
    quarter = height // RADIX
    slab = lax.axis_index("range")
    first_radial = lax.axis_index("radial") * rows
    gain = power_ref[slot_ref[first_radial // GROUP_RADIALS]]
    total = slabs * steps
    for place in range(total):
        phase_rows[place : place + 1, :] = phase_ref[
            pl.ds(profile_ref[place // steps, place % steps], 1), :
        ]
    cosine, sine = cos_sin(phase_rows[...])
    damp = jnp.where(lax.broadcasted_iota(jnp.int32, cosine.shape, 0) == 0, 1.0, absorb_ref[...])
    cosine, sine = cosine * damp, sine * damp
    for place in range(total):
        screen_cos[place] = jnp.broadcast_to(cosine[place : place + 1, :], (16, height))
        screen_sin[place] = jnp.broadcast_to(sine[place : place + 1, :], (16, height))
    real_ref[...] = field_ref[0].astype(jnp.float32)
    imag_ref[...] = field_ref[1].astype(jnp.float32)

    def one_step(place, step):
        for row in range(0, rows, 16):
            for lane in range(0, quarter, 128):
                parts = []
                for q in range(RADIX):
                    spot = (slice(row, row + 16), slice(q * quarter + lane, q * quarter + lane + 128))
                    phase_cos = screen_cos[place, :, spot[1]]
                    phase_sin = screen_sin[place, :, spot[1]]
                    real, imag = real_ref[spot], imag_ref[spot]
                    parts.append(
                        (real * phase_cos - imag * phase_sin, real * phase_sin + imag * phase_cos)
                    )
                (r0, i0), (r1, i1), (r2, i2), (r3, i3) = parts
                sr02, si02, dr02, di02 = r0 + r2, i0 + i2, r0 - r2, i0 - i2
                sr13, si13, dr13, di13 = r1 + r3, i1 + i3, r1 - r3, i1 - i3
                forward = (
                    (sr02 + sr13, si02 + si13),
                    (dr02 + di13, di02 - dr13),
                    (sr02 - sr13, si02 - si13),
                    (dr02 - di13, di02 + dr13),
                )
                for j, (real, imag) in enumerate(forward):
                    if j:
                        turn_cos = wave_ref[j : j + 1, lane : lane + 128]
                        turn_sin = wave_ref[RADIX + j : RADIX + j + 1, lane : lane + 128]
                        real, imag = (
                            real * turn_cos + imag * turn_sin,
                            imag * turn_cos - real * turn_sin,
                        )
                    spot = slice(j * rows + row, j * rows + row + 16)
                    mixed_ref[spot, lane : lane + 128] = real.astype(jnp.bfloat16)
                    mixed_ref[spot, quarter + lane : quarter + lane + 128] = imag.astype(jnp.bfloat16)
        spectrum = jnp.dot(mixed_ref[...], weight_ref[...], preferred_element_type=jnp.float32)
        for j in range(RADIX):
            theta_cos = wave_ref[2 * RADIX + j : 2 * RADIX + j + 1, :]
            theta_sin = wave_ref[3 * RADIX + j : 3 * RADIX + j + 1, :]
            real = spectrum[j * rows : (j + 1) * rows, :quarter]
            imag = spectrum[j * rows : (j + 1) * rows, quarter:]
            spot = slice(j * rows, (j + 1) * rows)
            moved_ref[spot, quarter:] = (real * theta_cos - imag * theta_sin).astype(jnp.bfloat16)
            moved_ref[spot, :quarter] = (real * theta_sin + imag * theta_cos).astype(jnp.bfloat16)
        back = jnp.dot(moved_ref[...], weight_ref[...], preferred_element_type=jnp.float32)
        for row in range(0, rows, 16):
            for lane in range(0, quarter, 128):
                parts = []
                for j in range(RADIX):
                    spot = slice(j * rows + row, j * rows + row + 16)
                    imag = back[spot, lane : lane + 128]
                    real = back[spot, quarter + lane : quarter + lane + 128]
                    if j:
                        turn_cos = wave_ref[j : j + 1, lane : lane + 128]
                        turn_sin = wave_ref[RADIX + j : RADIX + j + 1, lane : lane + 128]
                        real, imag = (
                            real * turn_cos - imag * turn_sin,
                            imag * turn_cos + real * turn_sin,
                        )
                    parts.append((real, imag))
                (r0, i0), (r1, i1), (r2, i2), (r3, i3) = parts
                sr02, si02, dr02, di02 = r0 + r2, i0 + i2, r0 - r2, i0 - i2
                sr13, si13, dr13, di13 = r1 + r3, i1 + i3, r1 - r3, i1 - i3
                inverse = (
                    (sr02 + sr13, si02 + si13),
                    (dr02 - di13, di02 + dr13),
                    (sr02 - sr13, si02 - si13),
                    (dr02 + di13, di02 - dr13),
                )
                for q, (real, imag) in enumerate(inverse):
                    spot = (slice(row, row + 16), slice(q * quarter + lane, q * quarter + lane + 128))
                    real_ref[spot] = real
                    imag_ref[spot] = imag
                    if q == 0 and lane < VB:
                        power = gain * (real * real + imag * imag)
                        polar_ref[row : row + 16, step * VB + lane : step * VB + lane + 128] = (
                            power.astype(jnp.bfloat16)
                        )

    def one_slab(number, carry):
        for step in range(steps):
            one_step(number * steps + step, step)
        return carry

    lax.fori_loop(0, slab + 1, one_slab, 0)


def march(field, phase_table, profile_index, group_power, group_slot):
    rows, height = field.shape[1:]
    slabs, steps = profile_index.shape
    weights, waves, absorber = march_constants(height)
    padded = -(-slabs * steps // 8) * 8
    smem = pl.BlockSpec(memory_space=pltpu.SMEM)
    vmem = pl.BlockSpec(memory_space=pltpu.VMEM)
    return pl.pallas_call(
        functools.partial(march_kernel, steps, slabs),
        out_shape=jax.ShapeDtypeStruct((rows, steps * VB), jnp.bfloat16),
        in_specs=[smem] * 3 + [vmem] * 5,
        out_specs=vmem,
        scratch_shapes=[
            pltpu.VMEM((padded, height), jnp.float32),
            pltpu.VMEM((slabs * steps, 16, height), jnp.float32),
            pltpu.VMEM((slabs * steps, 16, height), jnp.float32),
            pltpu.VMEM((rows, height), jnp.float32),
            pltpu.VMEM((rows, height), jnp.float32),
            pltpu.VMEM((rows * RADIX, 2 * height // RADIX), jnp.bfloat16),
            pltpu.VMEM((rows * RADIX, 2 * height // RADIX), jnp.bfloat16),
        ],
        compiler_params=pltpu.CompilerParams(vmem_limit_bytes=24 * 1024 * 1024),
        name="march",
    )(profile_index, group_power, group_slot, field, phase_table, weights, waves, absorber)


def tile_kernel(places, shift_ref, sub_ref, count_ref, place_ref, *refs):
    part_refs = refs[: len(places)]
    row_ref, col_ref, out_ref, polar_ref, mixed_ref = refs[len(places) :]
    tile = lax.axis_index("radial")
    devices = lax.axis_size("radial")
    local_rows = polar_ref.shape[0] // devices
    for number, part_ref in enumerate(part_refs):
        size = places[number]
        for piece in range(part_ref.shape[0] // size):
            start = pl.multiple_of(place_ref[number, piece] * local_rows, local_rows)
            polar_ref[pl.ds(start, size), :] = part_ref[piece * size : (piece + 1) * size, :]
    own_shift = shift_ref[0, tile]
    own_count = count_ref[0, tile]
    for slot in range(K_MAX):
        source = lax.rem(tile + own_shift + slot // CAP, devices)
        start = pl.multiple_of(source * local_rows + sub_ref[0, tile, slot] * SUB, SUB)
        block = polar_ref[pl.ds(start, SUB), :]
        block = jnp.where(slot < own_count, block, jnp.zeros_like(block))
        mixed = jnp.dot(block, col_ref[slot], preferred_element_type=jnp.float32)
        mixed_ref[slot * SUB : (slot + 1) * SUB, :] = mixed.astype(jnp.bfloat16)
    out_ref[...] = lax.dot_general(
        row_ref[...], mixed_ref[...], (((0,), (0,)), ((), ())), preferred_element_type=jnp.float32
    )


def tile_sum(parts, source_shift, slot_sub, tile_count, row_weights, col_weights, devices):
    pixels = row_weights.shape[-1]
    channels = col_weights.shape[-2]
    local_rows = sum(part.shape[0] for part, _, _ in parts) // devices
    most = max(len(places) for _, _, places in parts)
    table = jnp.stack(
        [jnp.stack([jnp.asarray(p, jnp.int32) for p in places + [0] * (most - len(places))]) for _, _, places in parts]
    )
    smem = pl.BlockSpec(memory_space=pltpu.SMEM)
    vmem = pl.BlockSpec(memory_space=pltpu.VMEM)
    return pl.pallas_call(
        functools.partial(tile_kernel, [size for _, size, _ in parts]),
        out_shape=jax.ShapeDtypeStruct((pixels, pixels), jnp.float32),
        in_specs=[smem] * 4 + [vmem] * (len(parts) + 2),
        out_specs=vmem,
        scratch_shapes=[
            pltpu.VMEM((devices * local_rows, channels), jnp.bfloat16),
            pltpu.VMEM((K_MAX * SUB, pixels), jnp.bfloat16),
        ],
        compiler_params=pltpu.CompilerParams(vmem_limit_bytes=24 * 1024 * 1024),
        name="tile_sum",
    )(
        source_shift,
        slot_sub,
        tile_count,
        table,
        *[part for part, _, _ in parts],
        row_weights.reshape(K_MAX * SUB, pixels),
        col_weights.reshape(K_MAX, channels, pixels),
    )


def swap(value, distance, devices):
    return lax.ppermute(value, "radial", [(i, i ^ distance) for i in range(devices)])


def gather_parts(polar, devices):
    local_rows = polar.shape[0]
    if devices != 16:
        whole = lax.all_gather(polar, "radial", axis=0, tiled=True)
        return [(whole, whole.shape[0], [0])]
    index = lax.axis_index("radial")
    core, chip = index % 2, index // 2
    sibling = swap(polar, 1, devices)
    pair = jnp.where(
        core == 0, jnp.concatenate([polar, sibling], 0), jnp.concatenate([sibling, polar], 0)
    )
    mine, theirs, size = [], [], 2 * local_rows
    held = []
    for pair_step in range(3):
        near, far = 2 * pair_step + 1, 2 * pair_step + 2
        routes = [(i, i ^ (2 * (near if i % 2 == 0 else far))) for i in range(devices)]
        held.append(lax.ppermute(pair, "radial", routes))
        mine.append(2 * (chip ^ jnp.where(core == 0, near, far)))
        theirs.append(2 * (chip ^ jnp.where(core == 0, far, near)))
    last = swap(polar, 14, devices)
    bundle = jnp.concatenate(held + [last], 0)
    other = swap(bundle, 1, devices)
    last_chip = 2 * (chip ^ 7)
    parts = [(polar, local_rows, [index]), (sibling, local_rows, [index ^ 1])]
    parts += [(h, size, [place]) for h, place in zip(held, mine)]
    parts.append((last, local_rows, [last_chip + core]))
    parts.append((other[: 3 * size], size, theirs))
    parts.append((other[3 * size :], local_rows, [last_chip + (1 - core)]))
    return parts


def per_device(
    field_start,
    phase_table,
    profile_index,
    group_power,
    group_slot,
    source_shift,
    slot_sub,
    tile_count,
    row_weights,
    col_weights,
):
    devices = lax.axis_size("radial")
    polar = march(field_start, phase_table, profile_index, group_power, group_slot)
    parts = gather_parts(polar, devices)
    tile_value = tile_sum(
        parts, source_shift, slot_sub, tile_count, row_weights, col_weights, devices
    )
    return tile_value.reshape((1, 1) + tile_value.shape)


def solution(mesh):
    return jax.shard_map(
        per_device,
        mesh=mesh,
        in_specs=(
            P(None, "radial", None),
            P(),
            P(),
            P(),
            P(),
            P("range", None),
            P("range", None, None),
            P("range", None),
            P("range", "radial", None, None, None),
            P("range", "radial", None, None, None),
        ),
        out_specs=P("range", "radial", None, None),
        check_vma=False,
    )
```

time: 87.3 us -> 28.5 us (0.33)
  the two profiles are of different devices: /device:TPU:0 before, /device:TPU:5 now
where the time goes in v1:
time: 28.5 us; the launch traced here: 28.1 us
  starting transfers between devices  9.66 us (34%)
  local copies, waits for them, and re-layouts  8.03 us (28%)
  Pallas kernels  5.41 us (19%)
  waiting for transfers between devices  4.8 us (17%)
    unnamed x26, local copies, waits for them, and re-layouts  7.98 us
    ppermute x3, starting transfers between devices, swap(): lax.ppermute(value, 'radial', [(i, i ^ distance) for i in range(devices)])  6.05 us
    ppermute x3, waiting for transfers between devices, gather_parts(): held.append(lax.ppermute(pair, 'radial', routes))  3.79 us
    ppermute x3, starting transfers between devices, gather_parts(): held.append(lax.ppermute(pair, 'radial', routes))  3.61 us
    pallas_call x1, Pallas kernels, march(): pl.pallas_call(functools.partial(march_kernel, steps, slabs), out_shape=j...  3.34 us
    pallas_call x1, Pallas kernels, tile_sum(): pl.pallas_call(functools.partial(tile_kernel, [size for _, size, _ in par...  2.07 us
    ppermute x3, waiting for transfers between devices, swap(): lax.ppermute(value, 'radial', [(i, i ^ distance) for i in range(devices)])  1.01 us
  transfers between devices with their start and end apart: 6, of which 4 were waited for; matrix products, arithmetic and copies ran while one was open for 0% of the time, Pallas kernels for 0%

profile of v1, /device:TPU:5, one launch (start us, length us, event | category | flops | bytes accessed | tf_op | source)
XLA Modules:
  0.0 28.1 jit_solution(15010880058956780385)
XLA Ops:
  0.0 0.0 copy-start
  0.0 0.0 copy-start.1
  0.0 1.2 %copy-done.1 = bf16[512,512]{1,0:T(8,128)(2,1)S(1)} copy-done((bf16[512,512]{1,0:T(8,128)(2,1)S(1)}, bf16[512,512]{1,0:T(8,128)(2,1)}, u32[]{:S(2)}) %copy-start.1) | copy-done | bytes 524312
  1.2 0.0 copy-start.2
  1.2 0.9 %copy-done.2 = bf16[2,64,1024]{2,1,0:T(8,128)(2,1)S(1)} copy-done((bf16[2,64,1024]{2,1,0:T(8,128)(2,1)S(1)}, bf16[2,64,1024]{2,1,0:T(8,128)(2,1)}, u32[]{:S(2)}) %copy-start.2) | copy-done | bytes 262168
  2.1 0.8 %copy-done.4 = f32[16,1024]{1,0:T(8,128)S(1)} copy-done((f32[16,1024]{1,0:T(8,128)S(1)}, f32[16,1024]{1,0:T(8,128)}, u32[]{:S(2)}) %copy-start.4) | copy-done | bytes 65560
  3.0 0.7 %copy-done.5 = f32[16,256]{1,0:T(8,128)S(1)} copy-done((f32[16,256]{1,0:T(8,128)S(1)}, f32[16,256]{1,0:T(8,128)}, u32[]{:S(2)}) %copy-start.5) | copy-done | bytes 16408
  3.7 0.7 %copy-done.7 = f32[1,1024]{1,0:T(1,128)S(1)} copy-done((f32[1,1024]{1,0:T(1,128)S(1)}, f32[1,1024]{1,0:T(1,128)}, u32[]{:S(2)}) %copy-start.7) | copy-done | bytes 4120
  4.4 0.7 %copy-done.8 = s32[2,2]{1,0:T(2,128)S(1)} copy-done((s32[2,2]{1,0:T(2,128)S(1)}, s32[2,2]{1,0:T(2,128)}, u32[]{:S(2)}) %copy-start.8) | copy-done | bytes 40
  5.1 0.7 %copy-done.9 = f32[2]{0:T(128)S(1)} copy-done((f32[2]{0:T(128)S(1)}, f32[2]{0:T(128)}, u32[]{:S(2)}) %copy-start.9) | copy-done | bytes 32
  5.7 0.7 %copy-done.10 = s32[2]{0:T(128)S(1)} copy-done((s32[2]{0:T(128)S(1)}, s32[2]{0:T(128)}, u32[]{:S(2)}) %copy-start.10) | copy-done | bytes 32
  6.4 3.3 %march.1.refs_0_ = bf16[64,256]{1,0:T(8,128)(2,1)S(1)} custom-call(s32[2,2]{1,0:T(2,128)S(1)} %copy-done.8, f32[2]{0:T(128)S(1)} %copy-done.9, s32[2]{0:T(128)S(1)} %copy-done.10, bf16[2,64,1024]{2,1,0:T(8,128)(2,1)S(1)} %copy-done.2, f32[16,1024]{1,0:T(8,128)S(1)} %copy-done.4, bf16[512,512]{1,0:T(8,128)(2,1)S(1)} %copy-done.1, f32[16,256]{1,0:T(8,128)S(1)} %copy-done.5, ...), custom_call_target="tpu_custom_call" | custom-call | tf_op jit(solution)/shard_map/march/pallas_call | solution.py:182
  9.7 0.7 %collective-permute-start = (bf16[64,256]{1,0:T(8,128)(2,1)S(1)}, bf16[64,256]{1,0:T(8,128)(2,1)S(1)}, u32[]{:S(2)}, u32[]{:S(2)}) collective-permute-start(bf16[64,256]{1,0:T(8,128)(2,1)S(1)} %march.1.refs_0_), channel_id=1, source_target_pairs={{0,1},{1,0},{2,3},{3,2},{4,5},{5,4},{6,7},{7,6},{8,9},{9,8},{10,11... | collective-permute-start | bytes 98312 | tf_op jit(solution)/shard_map/ppermute | solution.py:259
  10.5 4.3 %collective-permute-start.4 = (bf16[64,256]{1,0:T(8,128)(2,1)S(1)}, bf16[64,256]{1,0:T(8,128)(2,1)S(1)}, u32[]{:S(2)}, u32[]{:S(2)}) collective-permute-start(bf16[64,256]{1,0:T(8,128)(2,1)S(1)} %march.1.refs_0_), channel_id=1, source_target_pairs={{0,14},{1,15},{2,12},{3,13},{4,10},{5,11},{6,8},{7,9},{8,6},{9,7},... | collective-permute-start | bytes 98312 | tf_op jit(solution)/shard_map/ppermute | solution.py:259
  14.7 0.0 collective-permute-done.refs_1_
  14.8 0.1 collective-permute-start.3
  14.8 0.4 %collective-permute-start.2 = (bf16[128,256]{1,0:T(8,128)(2,1)S(1)}, bf16[128,256]{1,0:T(8,128)(2,1)S(1)}, u32[]{:S(2)}, u32[]{:S(2)}) collective-permute-start(bf16[128,256]{1,0:T(8,128)(2,1)S(1)} %maximum_select_fusion), channel_id=1, source_target_pairs={{0,6},{1,9},{2,4},{3,11},{4,2},{5,13},{6,0},{7,15},{8,14},{9,1},{1... | collective-permute-start | bytes 196616 | tf_op jit(solution)/shard_map/ppermute | solution.py:278
  15.3 3.1 %collective-permute-start.1 = (bf16[128,256]{1,0:T(8,128)(2,1)S(1)}, bf16[128,256]{1,0:T(8,128)(2,1)S(1)}, u32[]{:S(2)}, u32[]{:S(2)}) collective-permute-start(bf16[128,256]{1,0:T(8,128)(2,1)S(1)} %maximum_select_fusion), channel_id=1, source_target_pairs={{0,2},{1,5},{2,0},{3,7},{4,6},{5,1},{6,4},{7,3},{8,10},{9,13},{10,... | collective-permute-start | bytes 196616 | tf_op jit(solution)/shard_map/ppermute | solution.py:278
  18.4 0.0 collective-permute-done.4.refs_5_
  18.4 1.5 %collective-permute-done.3.refs_4_ = bf16[128,256]{1,0:T(8,128)(2,1)S(1)} collective-permute-done((bf16[128,256]{1,0:T(8,128)(2,1)S(1)}, bf16[128,256]{1,0:T(8,128)(2,1)S(1)}, u32[]{:S(2)}, u32[]{:S(2)}) %collective-permute-start.3) | collective-permute-done | bytes 65568 | tf_op jit(solution)/shard_map/ppermute | solution.py:278
  19.9 1.6 %collective-permute-done.2.refs_3_ = bf16[128,256]{1,0:T(8,128)(2,1)S(1)} collective-permute-done((bf16[128,256]{1,0:T(8,128)(2,1)S(1)}, bf16[128,256]{1,0:T(8,128)(2,1)S(1)}, u32[]{:S(2)}, u32[]{:S(2)}) %collective-permute-start.2) | collective-permute-done | bytes 65568 | tf_op jit(solution)/shard_map/ppermute | solution.py:278
  21.5 0.7 %collective-permute-done.1.refs_2_ = bf16[128,256]{1,0:T(8,128)(2,1)S(1)} collective-permute-done((bf16[128,256]{1,0:T(8,128)(2,1)S(1)}, bf16[128,256]{1,0:T(8,128)(2,1)S(1)}, u32[]{:S(2)}, u32[]{:S(2)}) %collective-permute-start.1) | collective-permute-done | bytes 65568 | tf_op jit(solution)/shard_map/ppermute | solution.py:278
  22.2 1.0 %collective-permute-start.5 = (bf16[448,256]{1,0:T(8,128)(2,1)S(1)}, bf16[448,256]{1,0:T(8,128)(2,1)S(1)}, u32[]{:S(2)}, u32[]{:S(2)}) collective-permute-start(bf16[448,256]{1,0:T(8,128)(2,1)S(1)} %pad_maximum_fusion), channel_id=1, source_target_pairs={{0,1},{1,0},{2,3},{3,2},{4,5},{5,4},{6,7},{7,6},{8,9},{9,8},{10,11... | collective-permute-start | bytes 688136 | tf_op jit(solution)/shard_map/ppermute | solution.py:259
  23.2 0.1 add_bitcast_fusion
  23.3 1.0 %collective-permute-done.5 = bf16[448,256]{1,0:T(8,128)(2,1)S(1)} collective-permute-done((bf16[448,256]{1,0:T(8,128)(2,1)S(1)}, bf16[448,256]{1,0:T(8,128)(2,1)S(1)}, u32[]{:S(2)}, u32[]{:S(2)}) %collective-permute-start.5) | collective-permute-done | bytes 229408 | tf_op jit(solution)/shard_map/ppermute | solution.py:259
  24.4 0.0 copy-done
  24.4 0.0 copy-done.11
  24.4 0.0 copy-done.12
  24.4 0.0 copy-start.3
  24.4 0.9 %copy-done.3 = bf16[1,1,16,16,256]{4,3,2,1,0:T(8,128)(2,1)S(1)} copy-done((bf16[1,1,16,16,256]{4,3,2,1,0:T(8,128)(2,1)S(1)}, bf16[1,1,16,16,256]{4,3,2,1,0:T(8,128)(2,1)}, u32[]{:S(2)}) %copy-start.3) | copy-done | bytes 131096
  25.3 0.7 %copy-done.6 = s32[1,16,16]{2,1,0:T(8,128)S(1)} copy-done((s32[1,16,16]{2,1,0:T(8,128)S(1)}, s32[1,16,16]{2,1,0:T(8,128)}, u32[]{:S(2)}) %copy-start.6) | copy-done | bytes 1048
  26.0 2.1 %tile_sum.1 = f32[256,256]{1,0:T(8,128)} custom-call(s32[1,16]{1,0:T(1,128)S(1)} %copy-done.11, s32[1,16,16]{2,1,0:T(8,128)S(1)} %copy-done.6, s32[1,16]{1,0:T(1,128)S(1)} %copy-done.12, s32[8,3]{1,0:T(8,128)S(1)} %stack.107.place_ref, bf16[64,256]{1,0:T(8,128)(2,1)S(1)} %march.1.refs_0_, bf16[64,256]{1,0:T(8,128)(2,1)S(1)} %collective-permute-done.refs_1_, ...), custom_call_target="tpu_custom_call" | custom-call | tf_op jit(solution)/shard_map/tile_sum/pallas_call | solution.py:236
  (17 shorter events, 0.1 us)
Async XLA Ops:
  0.0 24.4 %copy-start = (bf16[1,1,16,256,256]{4,3,2,1,0:T(8,128)(2,1)S(1)}, bf16[1,1,16,256,256]{4,3,2,1,0:T(8,128)(2,1)}, u32[]{:S(2)}) copy-start(bf16[1,1,16,256,256]{4,3,2,1,0:T(8,128)(2,1)} %param.22) | copy-start | bytes 6291460
  0.0 1.2 %copy-start.1 = (bf16[512,512]{1,0:T(8,128)(2,1)S(1)}, bf16[512,512]{1,0:T(8,128)(2,1)}, u32[]{:S(2)}) copy-start(bf16[512,512]{1,0:T(8,128)(2,1)} %constant.47.clone.weight_ref) | copy-start | bytes 1572868
  1.2 0.9 %copy-start.2 = (bf16[2,64,1024]{2,1,0:T(8,128)(2,1)S(1)}, bf16[2,64,1024]{2,1,0:T(8,128)(2,1)}, u32[]{:S(2)}) copy-start(bf16[2,64,1024]{2,1,0:T(8,128)(2,1)} %field_ref.1) | copy-start | bytes 786436
  2.1 0.8 %copy-start.4 = (f32[16,1024]{1,0:T(8,128)S(1)}, f32[16,1024]{1,0:T(8,128)}, u32[]{:S(2)}) copy-start(f32[16,1024]{1,0:T(8,128)} %phase_ref.1) | copy-start | bytes 196612
  3.0 0.7 %copy-start.5 = (f32[16,256]{1,0:T(8,128)S(1)}, f32[16,256]{1,0:T(8,128)}, u32[]{:S(2)}) copy-start(f32[16,256]{1,0:T(8,128)} %constant.48.clone.wave_ref) | copy-start | bytes 49156
  3.7 0.7 %copy-start.7 = (f32[1,1024]{1,0:T(1,128)S(1)}, f32[1,1024]{1,0:T(1,128)}, u32[]{:S(2)}) copy-start(f32[1,1024]{1,0:T(1,128)} %constant.49.clone.absorb_ref) | copy-start | bytes 12292
  4.4 0.7 %copy-start.8 = (s32[2,2]{1,0:T(2,128)S(1)}, s32[2,2]{1,0:T(2,128)}, u32[]{:S(2)}) copy-start(s32[2,2]{1,0:T(2,128)} %profile_ref.1) | copy-start | bytes 52
  5.1 0.7 %copy-start.9 = (f32[2]{0:T(128)S(1)}, f32[2]{0:T(128)}, u32[]{:S(2)}) copy-start(f32[2]{0:T(128)} %power_ref.1) | copy-start | bytes 28
  5.7 0.7 %copy-start.10 = (s32[2]{0:T(128)S(1)}, s32[2]{0:T(128)}, u32[]{:S(2)}) copy-start(s32[2]{0:T(128)} %slot_ref.1) | copy-start | bytes 28
  6.4 18.0 %copy-start.11 = (s32[1,16]{1,0:T(1,128)S(1)}, s32[1,16]{1,0:T(1,128)}, u32[]{:S(2)}) copy-start(s32[1,16]{1,0:T(1,128)} %shift_ref.1) | copy-start | bytes 196
  6.4 18.0 %copy-start.12 = (s32[1,16]{1,0:T(1,128)S(1)}, s32[1,16]{1,0:T(1,128)}, u32[]{:S(2)}) copy-start(s32[1,16]{1,0:T(1,128)} %count_ref.1) | copy-start | bytes 196
  9.7 5.0 %collective-permute-start = (bf16[64,256]{1,0:T(8,128)(2,1)S(1)}, bf16[64,256]{1,0:T(8,128)(2,1)S(1)}, u32[]{:S(2)}, u32[]{:S(2)}) collective-permute-start(bf16[64,256]{1,0:T(8,128)(2,1)S(1)} %march.1.refs_0_), channel_id=1, source_target_pairs={{0,1},{1,0},{2,3},{3,2},{4,5},{5,4},{6,7},{7,6},{8,9},{9,8},{10,11... | collective-permute-start | bytes 98312 | tf_op jit(solution)/shard_map/ppermute | solution.py:259
  10.5 7.9 %collective-permute-start.4 = (bf16[64,256]{1,0:T(8,128)(2,1)S(1)}, bf16[64,256]{1,0:T(8,128)(2,1)S(1)}, u32[]{:S(2)}, u32[]{:S(2)}) collective-permute-start(bf16[64,256]{1,0:T(8,128)(2,1)S(1)} %march.1.refs_0_), channel_id=1, source_target_pairs={{0,14},{1,15},{2,12},{3,13},{4,10},{5,11},{6,8},{7,9},{8,6},{9,7},... | collective-permute-start | bytes 98312 | tf_op jit(solution)/shard_map/ppermute | solution.py:259
  14.8 5.1 %collective-permute-start.3 = (bf16[128,256]{1,0:T(8,128)(2,1)S(1)}, bf16[128,256]{1,0:T(8,128)(2,1)S(1)}, u32[]{:S(2)}, u32[]{:S(2)}) collective-permute-start(bf16[128,256]{1,0:T(8,128)(2,1)S(1)} %maximum_select_fusion), channel_id=1, source_target_pairs={{0,10},{1,13},{2,8},{3,15},{4,14},{5,9},{6,12},{7,11},{8,2},{9,5},... | collective-permute-start | bytes 196616 | tf_op jit(solution)/shard_map/ppermute | solution.py:278
  14.8 6.6 %collective-permute-start.2 = (bf16[128,256]{1,0:T(8,128)(2,1)S(1)}, bf16[128,256]{1,0:T(8,128)(2,1)S(1)}, u32[]{:S(2)}, u32[]{:S(2)}) collective-permute-start(bf16[128,256]{1,0:T(8,128)(2,1)S(1)} %maximum_select_fusion), channel_id=1, source_target_pairs={{0,6},{1,9},{2,4},{3,11},{4,2},{5,13},{6,0},{7,15},{8,14},{9,1},{1... | collective-permute-start | bytes 196616 | tf_op jit(solution)/shard_map/ppermute | solution.py:278
  15.3 6.9 %collective-permute-start.1 = (bf16[128,256]{1,0:T(8,128)(2,1)S(1)}, bf16[128,256]{1,0:T(8,128)(2,1)S(1)}, u32[]{:S(2)}, u32[]{:S(2)}) collective-permute-start(bf16[128,256]{1,0:T(8,128)(2,1)S(1)} %maximum_select_fusion), channel_id=1, source_target_pairs={{0,2},{1,5},{2,0},{3,7},{4,6},{5,1},{6,4},{7,3},{8,10},{9,13},{10,... | collective-permute-start | bytes 196616 | tf_op jit(solution)/shard_map/ppermute | solution.py:278
  22.2 2.1 %collective-permute-start.5 = (bf16[448,256]{1,0:T(8,128)(2,1)S(1)}, bf16[448,256]{1,0:T(8,128)(2,1)S(1)}, u32[]{:S(2)}, u32[]{:S(2)}) collective-permute-start(bf16[448,256]{1,0:T(8,128)(2,1)S(1)} %pad_maximum_fusion), channel_id=1, source_target_pairs={{0,1},{1,0},{2,3},{3,2},{4,5},{5,4},{6,7},{7,6},{8,9},{9,8},{10,11... | collective-permute-start | bytes 688136 | tf_op jit(solution)/shard_map/ppermute | solution.py:259
  24.4 0.9 %copy-start.3 = (bf16[1,1,16,16,256]{4,3,2,1,0:T(8,128)(2,1)S(1)}, bf16[1,1,16,16,256]{4,3,2,1,0:T(8,128)(2,1)}, u32[]{:S(2)}) copy-start(bf16[1,1,16,16,256]{4,3,2,1,0:T(8,128)(2,1)} %param.21) | copy-start | bytes 393220
  25.3 0.7 %copy-start.6 = (s32[1,16,16]{2,1,0:T(8,128)S(1)}, s32[1,16,16]{2,1,0:T(8,128)}, u32[]{:S(2)}) copy-start(s32[1,16,16]{2,1,0:T(8,128)} %sub_ref.1) | copy-start | bytes 3076

commit v2 on v1

--- a/solution.py
+++ b/solution.py
@@ -33,9 +33,10 @@
     theta = -spread_angle * (2.0 * folded / height) ** 2
     theta = theta.reshape(quarter, RADIX).T
     depth = np.maximum(0.0, (level - 0.9375 * height) / (0.0625 * height))
-    absorber = np.exp(-absorb_rate * depth * depth).reshape(1, height)
-    waves = np.concatenate([np.cos(turn), np.sin(turn), np.cos(theta), np.sin(theta)], 0)
-    return weights, waves.astype(np.float32), absorber.astype(np.float32)
+    absorber = np.exp(-absorb_rate * depth * depth).reshape(RADIX, quarter)
+    waves = np.concatenate([np.cos(turn), np.sin(turn), np.cos(theta), np.sin(theta), absorber], 0)
+    waves = np.pad(waves, ((0, -len(waves) % 8), (0, 0)))
+    return weights, waves.astype(np.float32)
 
 
 def cos_sin(angle):
@@ -52,15 +53,28 @@
 def march_kernel(
     steps,
     slabs,
+    profile_hbm,
+    power_hbm,
+    slot_hbm,
+    shift_hbm,
+    sub_hbm,
+    count_hbm,
+    field_hbm,
+    phase_hbm,
+    weight_hbm,
+    wave_hbm,
+    polar_ref,
+    pick_ref,
     profile_ref,
     power_ref,
     slot_ref,
+    shift_ref,
+    sub_ref,
+    count_ref,
     field_ref,
     phase_ref,
     weight_ref,
     wave_ref,
-    absorb_ref,
-    polar_ref,
     phase_rows,
     screen_cos,
     screen_sin,
@@ -68,25 +82,62 @@
     imag_ref,
     mixed_ref,
     moved_ref,
+    sems,
 ):
+    pairs = (
+        (profile_hbm, profile_ref),
+        (phase_hbm, phase_ref),
+        (wave_hbm, wave_ref),
+        (field_hbm, field_ref),
+        (weight_hbm, weight_ref),
+        (power_hbm, power_ref),
+        (slot_hbm, slot_ref),
+        (shift_hbm, shift_ref),
+        (sub_hbm, sub_ref),
+        (count_hbm, count_ref),
+    )
+    copies = [
+        pltpu.make_async_copy(source, target, sems.at[number])
+        for number, (source, target) in enumerate(pairs)
+    ]
+    for copy in copies:
+        copy.start()
     rows, height = field_ref.shape[1:]
     quarter = height // RADIX
     slab = lax.axis_index("range")
-    first_radial = lax.axis_index("radial") * rows
-    gain = power_ref[slot_ref[first_radial // GROUP_RADIALS]]
+    tile = lax.axis_index("radial")
+    devices = lax.axis_size("radial")
     total = slabs * steps
+    for copy in copies[:3]:
+        copy.wait()
     for place in range(total):
         phase_rows[place : place + 1, :] = phase_ref[
             pl.ds(profile_ref[place // steps, place % steps], 1), :
         ]
-    cosine, sine = cos_sin(phase_rows[...])
-    damp = jnp.where(lax.broadcasted_iota(jnp.int32, cosine.shape, 0) == 0, 1.0, absorb_ref[...])
-    cosine, sine = cosine * damp, sine * damp
-    for place in range(total):
-        screen_cos[place] = jnp.broadcast_to(cosine[place : place + 1, :], (16, height))
-        screen_sin[place] = jnp.broadcast_to(sine[place : place + 1, :], (16, height))
+    for q in range(RADIX):
+        lanes = slice(q * quarter, (q + 1) * quarter)
+        cosine, sine = cos_sin(phase_rows[:, lanes])
+        absorber = wave_ref[4 * RADIX + q : 4 * RADIX + q + 1, :]
+        damp = jnp.where(lax.broadcasted_iota(jnp.int32, cosine.shape, 0) == 0, 1.0, absorber)
+        cosine, sine = cosine * damp, sine * damp
+        for place in range(total):
+            screen_cos[place, :, lanes] = jnp.broadcast_to(cosine[place : place + 1], (16, quarter))
+            screen_sin[place, :, lanes] = jnp.broadcast_to(sine[place : place + 1], (16, quarter))
+    for copy in copies[3:]:
+        copy.wait()
+    gain = power_ref[slot_ref[tile * rows // GROUP_RADIALS]]
     real_ref[...] = field_ref[0].astype(jnp.float32)
     imag_ref[...] = field_ref[1].astype(jnp.float32)
+
+    shape = (SUB, pick_ref.shape[1])
+    offset = lax.broadcasted_iota(jnp.int32, shape, 1) - lax.broadcasted_iota(jnp.int32, shape, 0)
+    for slot in range(K_MAX):
+        source = lax.rem(tile + shift_ref[0, tile] + slot // CAP, devices)
+        start = source * rows + sub_ref[0, tile, slot] * SUB
+        start = jnp.where(slot < count_ref[0, tile], start, -height * devices)
+        pick_ref[slot * SUB : (slot + 1) * SUB, :] = jnp.where(offset == start, 1.0, 0.0).astype(
+            jnp.bfloat16
+        )
 
     def one_step(place, step):
         for row in range(0, rows, 16):
@@ -172,50 +223,56 @@
     lax.fori_loop(0, slab + 1, one_slab, 0)
 
 
-def march(field, phase_table, profile_index, group_power, group_slot):
+def march(
+    field, phase_table, profile_index, group_power, group_slot, source_shift, slot_sub, tile_count
+):
     rows, height = field.shape[1:]
     slabs, steps = profile_index.shape
-    weights, waves, absorber = march_constants(height)
-    padded = -(-slabs * steps // 8) * 8
-    smem = pl.BlockSpec(memory_space=pltpu.SMEM)
-    vmem = pl.BlockSpec(memory_space=pltpu.VMEM)
+    weights, waves = march_constants(height)
+    operands = [profile_index, group_power, group_slot, source_shift, slot_sub, tile_count]
+    places = [pltpu.SMEM] * len(operands)
+    operands += [field, phase_table, weights, waves]
+    places += [pltpu.VMEM] * 4
+    radials = rows * lax.axis_size("radial")
     return pl.pallas_call(
         functools.partial(march_kernel, steps, slabs),
-        out_shape=jax.ShapeDtypeStruct((rows, steps * VB), jnp.bfloat16),
-        in_specs=[smem] * 3 + [vmem] * 5,
-        out_specs=vmem,
-        scratch_shapes=[
-            pltpu.VMEM((padded, height), jnp.float32),
+        out_shape=[
+            jax.ShapeDtypeStruct((rows, steps * VB), jnp.bfloat16),
+            jax.ShapeDtypeStruct((K_MAX * SUB, radials), jnp.bfloat16),
+        ],
+        in_specs=[pl.BlockSpec(memory_space=pltpu.HBM)] * len(operands),
+        out_specs=[pl.BlockSpec(memory_space=pltpu.VMEM)] * 2,
+        scratch_shapes=[place(o.shape, o.dtype) for place, o in zip(places, operands)]
+        + [
+            pltpu.VMEM((-(-slabs * steps // 8) * 8, height), jnp.float32),
             pltpu.VMEM((slabs * steps, 16, height), jnp.float32),
             pltpu.VMEM((slabs * steps, 16, height), jnp.float32),
             pltpu.VMEM((rows, height), jnp.float32),
             pltpu.VMEM((rows, height), jnp.float32),
             pltpu.VMEM((rows * RADIX, 2 * height // RADIX), jnp.bfloat16),
             pltpu.VMEM((rows * RADIX, 2 * height // RADIX), jnp.bfloat16),
+            pltpu.SemaphoreType.DMA((len(operands),)),
         ],
         compiler_params=pltpu.CompilerParams(vmem_limit_bytes=24 * 1024 * 1024),
         name="march",
-    )(profile_index, group_power, group_slot, field, phase_table, weights, waves, absorber)
-
-
-def tile_kernel(places, shift_ref, sub_ref, count_ref, place_ref, *refs):
+    )(*[pltpu.with_memory_space_constraint(o, pltpu.HBM) for o in operands])
+
+
+def tile_kernel(places, pick_ref, *refs):
     part_refs = refs[: len(places)]
     row_ref, col_ref, out_ref, polar_ref, mixed_ref = refs[len(places) :]
-    tile = lax.axis_index("radial")
-    devices = lax.axis_size("radial")
-    local_rows = polar_ref.shape[0] // devices
-    for number, part_ref in enumerate(part_refs):
-        size = places[number]
-        for piece in range(part_ref.shape[0] // size):
-            start = pl.multiple_of(place_ref[number, piece] * local_rows, local_rows)
-            polar_ref[pl.ds(start, size), :] = part_ref[piece * size : (piece + 1) * size, :]
-    own_shift = shift_ref[0, tile]
-    own_count = count_ref[0, tile]
+    chip = lax.axis_index("radial") // 2
+    core = lax.axis_index("radial") % 2
+    for (even, odd), part_ref in zip(places, part_refs):
+        size = part_ref.shape[0]
+        start = jnp.where(core == 0, chip ^ even, chip ^ odd) * size
+        if size == polar_ref.shape[0]:
+            start = 0
+        polar_ref[pl.ds(start, size), :] = part_ref[...]
+    blocks = jnp.dot(pick_ref[...], polar_ref[...], preferred_element_type=jnp.float32)
+    blocks = blocks.astype(jnp.bfloat16)
     for slot in range(K_MAX):
-        source = lax.rem(tile + own_shift + slot // CAP, devices)
-        start = pl.multiple_of(source * local_rows + sub_ref[0, tile, slot] * SUB, SUB)
-        block = polar_ref[pl.ds(start, SUB), :]
-        block = jnp.where(slot < own_count, block, jnp.zeros_like(block))
+        block = blocks[slot * SUB : (slot + 1) * SUB]
         mixed = jnp.dot(block, col_ref[slot], preferred_element_type=jnp.float32)
         mixed_ref[slot * SUB : (slot + 1) * SUB, :] = mixed.astype(jnp.bfloat16)
     out_ref[...] = lax.dot_general(
@@ -223,33 +280,24 @@
     )
 
 
-def tile_sum(parts, source_shift, slot_sub, tile_count, row_weights, col_weights, devices):
+def tile_sum(pick, parts, places, row_weights, col_weights):
     pixels = row_weights.shape[-1]
     channels = col_weights.shape[-2]
-    local_rows = sum(part.shape[0] for part, _, _ in parts) // devices
-    most = max(len(places) for _, _, places in parts)
-    table = jnp.stack(
-        [jnp.stack([jnp.asarray(p, jnp.int32) for p in places + [0] * (most - len(places))]) for _, _, places in parts]
-    )
-    smem = pl.BlockSpec(memory_space=pltpu.SMEM)
     vmem = pl.BlockSpec(memory_space=pltpu.VMEM)
     return pl.pallas_call(
-        functools.partial(tile_kernel, [size for _, size, _ in parts]),
+        functools.partial(tile_kernel, places),
         out_shape=jax.ShapeDtypeStruct((pixels, pixels), jnp.float32),
-        in_specs=[smem] * 4 + [vmem] * (len(parts) + 2),
+        in_specs=[vmem] * (len(parts) + 3),
         out_specs=vmem,
         scratch_shapes=[
-            pltpu.VMEM((devices * local_rows, channels), jnp.bfloat16),
+            pltpu.VMEM((pick.shape[1], channels), jnp.bfloat16),
             pltpu.VMEM((K_MAX * SUB, pixels), jnp.bfloat16),
         ],
         compiler_params=pltpu.CompilerParams(vmem_limit_bytes=24 * 1024 * 1024),
         name="tile_sum",
     )(
-        source_shift,
-        slot_sub,
-        tile_count,
-        table,
-        *[part for part, _, _ in parts],
+        pick,
+        *parts,
         row_weights.reshape(K_MAX * SUB, pixels),
         col_weights.reshape(K_MAX, channels, pixels),
     )
@@ -260,34 +308,27 @@
 
 
 def gather_parts(polar, devices):
-    local_rows = polar.shape[0]
     if devices != 16:
-        whole = lax.all_gather(polar, "radial", axis=0, tiled=True)
-        return [(whole, whole.shape[0], [0])]
-    index = lax.axis_index("radial")
-    core, chip = index % 2, index // 2
-    sibling = swap(polar, 1, devices)
-    pair = jnp.where(
-        core == 0, jnp.concatenate([polar, sibling], 0), jnp.concatenate([sibling, polar], 0)
-    )
-    mine, theirs, size = [], [], 2 * local_rows
+        return [lax.all_gather(polar, "radial", axis=0, tiled=True)], [(0, 0)]
+    core = lax.axis_index("radial") % 2
+    size = 2 * polar.shape[0]
+
+    def in_order(own, other):
+        return jnp.where(
+            core == 0, jnp.concatenate([own, other], 0), jnp.concatenate([other, own], 0)
+        )
+
+    pair = in_order(polar, swap(polar, 1, devices))
     held = []
-    for pair_step in range(3):
-        near, far = 2 * pair_step + 1, 2 * pair_step + 2
-        routes = [(i, i ^ (2 * (near if i % 2 == 0 else far))) for i in range(devices)]
+    for even, odd in ((1, 2), (3, 4), (5, 6)):
+        routes = [(i, i ^ (2 * (odd if i % 2 else even))) for i in range(devices)]
         held.append(lax.ppermute(pair, "radial", routes))
-        mine.append(2 * (chip ^ jnp.where(core == 0, near, far)))
-        theirs.append(2 * (chip ^ jnp.where(core == 0, far, near)))
     last = swap(polar, 14, devices)
-    bundle = jnp.concatenate(held + [last], 0)
-    other = swap(bundle, 1, devices)
-    last_chip = 2 * (chip ^ 7)
-    parts = [(polar, local_rows, [index]), (sibling, local_rows, [index ^ 1])]
-    parts += [(h, size, [place]) for h, place in zip(held, mine)]
-    parts.append((last, local_rows, [last_chip + core]))
-    parts.append((other[: 3 * size], size, theirs))
-    parts.append((other[3 * size :], local_rows, [last_chip + (1 - core)]))
-    return parts
+    other = swap(jnp.concatenate(held + [last], 0), 1, devices)
+    parts = [pair] + held + [other[i * size : (i + 1) * size] for i in range(3)]
+    parts.append(in_order(last, other[3 * size :]))
+    places = [(0, 0), (1, 2), (3, 4), (5, 6), (2, 1), (4, 3), (6, 5), (7, 7)]
+    return parts, places
 
 
 def per_device(
@@ -303,11 +344,18 @@
     col_weights,
 ):
     devices = lax.axis_size("radial")
-    polar = march(field_start, phase_table, profile_index, group_power, group_slot)
-    parts = gather_parts(polar, devices)
-    tile_value = tile_sum(
-        parts, source_shift, slot_sub, tile_count, row_weights, col_weights, devices
-    )
+    polar, pick = march(
+        field_start,
+        phase_table,
+        profile_index,
+        group_power,
+        group_slot,
+        source_shift,
+        slot_sub,
+        tile_count,
+    )
+    parts, places = gather_parts(polar, devices)
+    tile_value = tile_sum(pick, parts, places, row_weights, col_weights)
     return tile_value.reshape((1, 1) + tile_value.shape)
 
 

time: 28.5 us -> 23.5 us (0.82)
  the two profiles are of different devices: /device:TPU:5 before, /device:TPU:0 now
where the time goes in v2:
time: 23.5 us; the launch traced here: 23.2 us
  waiting for transfers between devices  8.95 us (38%)
  starting transfers between devices  8.56 us (36%)
  Pallas kernels  4.63 us (20%)
  local copies, waits for them, and re-layouts  0.91 us (4%)
    ppermute x3, waiting for transfers between devices, swap(): lax.ppermute(value, 'radial', [(i, i ^ distance) for i in range(devices)])  8.94 us
    ppermute x3, starting transfers between devices, gather_parts(): held.append(lax.ppermute(pair, 'radial', routes))  7.96 us
    pallas_call x1, Pallas kernels, march(): pl.pallas_call(functools.partial(march_kernel, steps, slabs), out_shape=[...  2.88 us
    pallas_call x1, Pallas kernels, tile_sum(): pl.pallas_call(functools.partial(tile_kernel, places), out_shape=jax.Shap...  1.75 us
    unnamed x4, local copies, waits for them, and re-layouts  0.9 us
    ppermute x3, starting transfers between devices, swap(): lax.ppermute(value, 'radial', [(i, i ^ distance) for i in range(devices)])  0.59 us
  transfers between devices with their start and end apart: 6, of which 3 were waited for; matrix products, arithmetic and copies ran while one was open for 0% of the time, Pallas kernels for 0%

profile of v2, /device:TPU:0, one launch (start us, length us, event | category | flops | bytes accessed | tf_op | source)
XLA Modules:
  0.0 23.2 jit_solution(10143352420859673095)
XLA Ops:
  0.0 0.0 copy-start
  0.0 2.9 %march.1 = (bf16[64,256]{1,0:T(8,128)(2,1)S(1)}, bf16[256,1024]{1,0:T(8,128)(2,1)S(1)}) custom-call(s32[2,2]{1,0:T(2,128)} %profile_hbm.1, f32[2]{0:T(128)} %power_hbm.1, s32[2]{0:T(128)} %slot_hbm.1, s32[1,16]{1,0:T(1,128)} %shift_hbm.1, s32[1,16,16]{2,1,0:T(8,128)} %sub_hbm.1, s32[1,16]{1,0:T(1,128)} %count_hbm.1, bf16[2,64,1024]{2,1,0:T(8,128)(2,1)} %field_hbm.1, ...), custom_call_target="tpu_custom_call" | custom-call | tf_op jit(solution)/shard_map/march/pallas_call | solution.py:237
  2.9 0.5 %collective-permute-start = (bf16[64,256]{1,0:T(8,128)(2,1)S(1)}, bf16[64,256]{1,0:T(8,128)(2,1)S(1)}, u32[]{:S(2)}, u32[]{:S(2)}) collective-permute-start(bf16[64,256]{1,0:T(8,128)(2,1)S(1)} %get-tuple-element.8), channel_id=1, source_target_pairs={{0,1},{1,0},{2,3},{3,2},{4,5},{5,4},{6,7},{7,6},{8,9},{9,8},{10,11... | collective-permute-start | bytes 98312 | tf_op jit(solution)/shard_map/ppermute | solution.py:307
  3.4 0.9 %collective-permute-done = bf16[64,256]{1,0:T(8,128)(2,1)S(1)} collective-permute-done((bf16[64,256]{1,0:T(8,128)(2,1)S(1)}, bf16[64,256]{1,0:T(8,128)(2,1)S(1)}, u32[]{:S(2)}, u32[]{:S(2)}) %collective-permute-start) | collective-permute-done | bytes 32800 | tf_op jit(solution)/shard_map/ppermute | solution.py:307
  4.3 4.9 %collective-permute-start.3 = (bf16[128,256]{1,0:T(8,128)(2,1)S(1)}, bf16[128,256]{1,0:T(8,128)(2,1)S(1)}, u32[]{:S(2)}, u32[]{:S(2)}) collective-permute-start(bf16[128,256]{1,0:T(8,128)(2,1)S(1)} %maximum_select_fusion.refs_0_), channel_id=1, source_target_pairs={{0,10},{1,13},{2,8},{3,15},{4,14},{5,9},{6,12},{7,11},{8,2},{9,5},... | collective-permute-start | bytes 196616 | tf_op jit(solution)/shard_map/ppermute | solution.py:325
  9.2 1.5 %collective-permute-start.2 = (bf16[128,256]{1,0:T(8,128)(2,1)S(1)}, bf16[128,256]{1,0:T(8,128)(2,1)S(1)}, u32[]{:S(2)}, u32[]{:S(2)}) collective-permute-start(bf16[128,256]{1,0:T(8,128)(2,1)S(1)} %maximum_select_fusion.refs_0_), channel_id=1, source_target_pairs={{0,6},{1,9},{2,4},{3,11},{4,2},{5,13},{6,0},{7,15},{8,14},{9,1},{1... | collective-permute-start | bytes 196616 | tf_op jit(solution)/shard_map/ppermute | solution.py:325
  10.8 1.5 %collective-permute-start.1 = (bf16[128,256]{1,0:T(8,128)(2,1)S(1)}, bf16[128,256]{1,0:T(8,128)(2,1)S(1)}, u32[]{:S(2)}, u32[]{:S(2)}) collective-permute-start(bf16[128,256]{1,0:T(8,128)(2,1)S(1)} %maximum_select_fusion.refs_0_), channel_id=1, source_target_pairs={{0,2},{1,5},{2,0},{3,7},{4,6},{5,1},{6,4},{7,3},{8,10},{9,13},{10,... | collective-permute-start | bytes 196616 | tf_op jit(solution)/shard_map/ppermute | solution.py:325
  12.3 0.0 collective-permute-start.4
  12.3 6.6 %collective-permute-done.4 = bf16[64,256]{1,0:T(8,128)(2,1)S(1)} collective-permute-done((bf16[64,256]{1,0:T(8,128)(2,1)S(1)}, bf16[64,256]{1,0:T(8,128)(2,1)S(1)}, u32[]{:S(2)}, u32[]{:S(2)}) %collective-permute-start.4) | collective-permute-done | bytes 32800 | tf_op jit(solution)/shard_map/ppermute | solution.py:307
  18.9 0.0 collective-permute-done.3.refs_3_
  18.9 0.0 collective-permute-done.2.refs_2_
  18.9 0.0 collective-permute-done.1.refs_1_
  18.9 0.1 collective-permute-start.5
  19.0 1.5 %collective-permute-done.5 = bf16[448,256]{1,0:T(8,128)(2,1)S(1)} collective-permute-done((bf16[448,256]{1,0:T(8,128)(2,1)S(1)}, bf16[448,256]{1,0:T(8,128)(2,1)S(1)}, u32[]{:S(2)}, u32[]{:S(2)}) %collective-permute-start.5) | collective-permute-done | bytes 229408 | tf_op jit(solution)/shard_map/ppermute | solution.py:307
  20.5 0.0 copy-done
  20.5 0.0 copy-start.1
  20.5 0.9 %copy-done.1 = bf16[1,1,16,16,256]{4,3,2,1,0:T(8,128)(2,1)S(1)} copy-done((bf16[1,1,16,16,256]{4,3,2,1,0:T(8,128)(2,1)S(1)}, bf16[1,1,16,16,256]{4,3,2,1,0:T(8,128)(2,1)}, u32[]{:S(2)}) %copy-start.1) | copy-done | bytes 131096
  21.4 1.7 %tile_sum.1 = f32[256,256]{1,0:T(8,128)} custom-call(bf16[256,1024]{1,0:T(8,128)(2,1)S(1)} %get-tuple-element.7.pick_ref, bf16[128,256]{1,0:T(8,128)(2,1)S(1)} %maximum_select_fusion.refs_0_, bf16[128,256]{1,0:T(8,128)(2,1)S(1)} %collective-permute-done.1.refs_1_, bf16[128,256]{1,0:T(8,128)(2,1)S(1)} %collective-permute-done.2.refs_2_, ...), custom_call_target="tpu_custom_call" | custom-call | tf_op jit(solution)/shard_map/tile_sum/pallas_call | solution.py:287
  (4 shorter events, 0.1 us)
Async XLA Ops:
  0.0 20.5 %copy-start = (bf16[1,1,16,256,256]{4,3,2,1,0:T(8,128)(2,1)S(1)}, bf16[1,1,16,256,256]{4,3,2,1,0:T(8,128)(2,1)}, u32[]{:S(2)}) copy-start(bf16[1,1,16,256,256]{4,3,2,1,0:T(8,128)(2,1)} %param.21) | copy-start | bytes 6291460
  2.9 1.4 %collective-permute-start = (bf16[64,256]{1,0:T(8,128)(2,1)S(1)}, bf16[64,256]{1,0:T(8,128)(2,1)S(1)}, u32[]{:S(2)}, u32[]{:S(2)}) collective-permute-start(bf16[64,256]{1,0:T(8,128)(2,1)S(1)} %get-tuple-element.8), channel_id=1, source_target_pairs={{0,1},{1,0},{2,3},{3,2},{4,5},{5,4},{6,7},{7,6},{8,9},{9,8},{10,11... | collective-permute-start | bytes 98312 | tf_op jit(solution)/shard_map/ppermute | solution.py:307
  4.3 14.6 %collective-permute-start.3 = (bf16[128,256]{1,0:T(8,128)(2,1)S(1)}, bf16[128,256]{1,0:T(8,128)(2,1)S(1)}, u32[]{:S(2)}, u32[]{:S(2)}) collective-permute-start(bf16[128,256]{1,0:T(8,128)(2,1)S(1)} %maximum_select_fusion.refs_0_), channel_id=1, source_target_pairs={{0,10},{1,13},{2,8},{3,15},{4,14},{5,9},{6,12},{7,11},{8,2},{9,5},... | collective-permute-start | bytes 196616 | tf_op jit(solution)/shard_map/ppermute | solution.py:325
  9.2 9.7 %collective-permute-start.2 = (bf16[128,256]{1,0:T(8,128)(2,1)S(1)}, bf16[128,256]{1,0:T(8,128)(2,1)S(1)}, u32[]{:S(2)}, u32[]{:S(2)}) collective-permute-start(bf16[128,256]{1,0:T(8,128)(2,1)S(1)} %maximum_select_fusion.refs_0_), channel_id=1, source_target_pairs={{0,6},{1,9},{2,4},{3,11},{4,2},{5,13},{6,0},{7,15},{8,14},{9,1},{1... | collective-permute-start | bytes 196616 | tf_op jit(solution)/shard_map/ppermute | solution.py:325
  10.8 8.1 %collective-permute-start.1 = (bf16[128,256]{1,0:T(8,128)(2,1)S(1)}, bf16[128,256]{1,0:T(8,128)(2,1)S(1)}, u32[]{:S(2)}, u32[]{:S(2)}) collective-permute-start(bf16[128,256]{1,0:T(8,128)(2,1)S(1)} %maximum_select_fusion.refs_0_), channel_id=1, source_target_pairs={{0,2},{1,5},{2,0},{3,7},{4,6},{5,1},{6,4},{7,3},{8,10},{9,13},{10,... | collective-permute-start | bytes 196616 | tf_op jit(solution)/shard_map/ppermute | solution.py:325
  12.3 6.6 %collective-permute-start.4 = (bf16[64,256]{1,0:T(8,128)(2,1)S(1)}, bf16[64,256]{1,0:T(8,128)(2,1)S(1)}, u32[]{:S(2)}, u32[]{:S(2)}) collective-permute-start(bf16[64,256]{1,0:T(8,128)(2,1)S(1)} %get-tuple-element.8), channel_id=1, source_target_pairs={{0,14},{1,15},{2,12},{3,13},{4,10},{5,11},{6,8},{7,9},{8,6},{9,7},... | collective-permute-start | bytes 98312 | tf_op jit(solution)/shard_map/ppermute | solution.py:307
  18.9 1.6 %collective-permute-start.5 = (bf16[448,256]{1,0:T(8,128)(2,1)S(1)}, bf16[448,256]{1,0:T(8,128)(2,1)S(1)}, u32[]{:S(2)}, u32[]{:S(2)}) collective-permute-start(bf16[448,256]{1,0:T(8,128)(2,1)S(1)} %pad_maximum_fusion), channel_id=1, source_target_pairs={{0,1},{1,0},{2,3},{3,2},{4,5},{5,4},{6,7},{7,6},{8,9},{9,8},{10,11... | collective-permute-start | bytes 688136 | tf_op jit(solution)/shard_map/ppermute | solution.py:307
  20.5 0.9 %copy-start.1 = (bf16[1,1,16,16,256]{4,3,2,1,0:T(8,128)(2,1)S(1)}, bf16[1,1,16,16,256]{4,3,2,1,0:T(8,128)(2,1)}, u32[]{:S(2)}) copy-start(bf16[1,1,16,16,256]{4,3,2,1,0:T(8,128)(2,1)} %param.20) | copy-start | bytes 393220

commit v3 on v2

--- a/solution.py
+++ b/solution.py
@@ -63,8 +63,12 @@
     phase_hbm,
     weight_hbm,
     wave_hbm,
+    row_hbm,
+    col_hbm,
     polar_ref,
     pick_ref,
+    turned_ref,
+    col_ref,
     profile_ref,
     power_ref,
     slot_ref,
@@ -75,6 +79,7 @@
     phase_ref,
     weight_ref,
     wave_ref,
+    row_ref,
     phase_rows,
     screen_cos,
     screen_sin,
@@ -95,12 +100,14 @@
         (shift_hbm, shift_ref),
         (sub_hbm, sub_ref),
         (count_hbm, count_ref),
+        (row_hbm, row_ref),
+        (col_hbm, col_ref),
     )
     copies = [
         pltpu.make_async_copy(source, target, sems.at[number])
         for number, (source, target) in enumerate(pairs)
     ]
-    for copy in copies:
+    for copy in copies[:-1]:
         copy.start()
     rows, height = field_ref.shape[1:]
     quarter = height // RADIX
@@ -123,12 +130,9 @@
         for place in range(total):
             screen_cos[place, :, lanes] = jnp.broadcast_to(cosine[place : place + 1], (16, quarter))
             screen_sin[place, :, lanes] = jnp.broadcast_to(sine[place : place + 1], (16, quarter))
-    for copy in copies[3:]:
+    for copy in copies[5:-1]:
         copy.wait()
     gain = power_ref[slot_ref[tile * rows // GROUP_RADIALS]]
-    real_ref[...] = field_ref[0].astype(jnp.float32)
-    imag_ref[...] = field_ref[1].astype(jnp.float32)
-
     shape = (SUB, pick_ref.shape[1])
     offset = lax.broadcasted_iota(jnp.int32, shape, 1) - lax.broadcasted_iota(jnp.int32, shape, 0)
     for slot in range(K_MAX):
@@ -138,6 +142,13 @@
         pick_ref[slot * SUB : (slot + 1) * SUB, :] = jnp.where(offset == start, 1.0, 0.0).astype(
             jnp.bfloat16
         )
+
+    turned_ref[...] = row_ref[...].T
+    for copy in copies[3:5]:
+        copy.wait()
+    copies[-1].start()
+    real_ref[...] = field_ref[0].astype(jnp.float32)
+    imag_ref[...] = field_ref[1].astype(jnp.float32)
 
     def one_step(place, step):
         for row in range(0, rows, 16):
@@ -221,27 +232,42 @@
         return carry
 
     lax.fori_loop(0, slab + 1, one_slab, 0)
+    copies[-1].wait()
 
 
 def march(
-    field, phase_table, profile_index, group_power, group_slot, source_shift, slot_sub, tile_count
+    field,
+    phase_table,
+    profile_index,
+    group_power,
+    group_slot,
+    source_shift,
+    slot_sub,
+    tile_count,
+    row_weights,
+    col_weights,
 ):
     rows, height = field.shape[1:]
     slabs, steps = profile_index.shape
     weights, waves = march_constants(height)
     operands = [profile_index, group_power, group_slot, source_shift, slot_sub, tile_count]
     places = [pltpu.SMEM] * len(operands)
-    operands += [field, phase_table, weights, waves]
-    places += [pltpu.VMEM] * 4
+    pixels = row_weights.shape[-1]
+    rows_flat = row_weights.reshape(K_MAX * SUB, pixels)
+    cols_flat = col_weights.reshape(K_MAX, col_weights.shape[-2], pixels)
+    operands += [field, phase_table, weights, waves, rows_flat]
+    places += [pltpu.VMEM] * 5
     radials = rows * lax.axis_size("radial")
     return pl.pallas_call(
         functools.partial(march_kernel, steps, slabs),
         out_shape=[
             jax.ShapeDtypeStruct((rows, steps * VB), jnp.bfloat16),
             jax.ShapeDtypeStruct((K_MAX * SUB, radials), jnp.bfloat16),
+            jax.ShapeDtypeStruct((pixels, K_MAX * SUB), jnp.bfloat16),
+            jax.ShapeDtypeStruct(cols_flat.shape, jnp.bfloat16),
         ],
-        in_specs=[pl.BlockSpec(memory_space=pltpu.HBM)] * len(operands),
-        out_specs=[pl.BlockSpec(memory_space=pltpu.VMEM)] * 2,
+        in_specs=[pl.BlockSpec(memory_space=pltpu.HBM)] * (len(operands) + 1),
+        out_specs=[pl.BlockSpec(memory_space=pltpu.VMEM)] * 4,
         scratch_shapes=[place(o.shape, o.dtype) for place, o in zip(places, operands)]
         + [
             pltpu.VMEM((-(-slabs * steps // 8) * 8, height), jnp.float32),
@@ -251,11 +277,11 @@
             pltpu.VMEM((rows, height), jnp.float32),
             pltpu.VMEM((rows * RADIX, 2 * height // RADIX), jnp.bfloat16),
             pltpu.VMEM((rows * RADIX, 2 * height // RADIX), jnp.bfloat16),
-            pltpu.SemaphoreType.DMA((len(operands),)),
+            pltpu.SemaphoreType.DMA((len(operands) + 1,)),
         ],
         compiler_params=pltpu.CompilerParams(vmem_limit_bytes=24 * 1024 * 1024),
         name="march",
-    )(*[pltpu.with_memory_space_constraint(o, pltpu.HBM) for o in operands])
+    )(*[pltpu.with_memory_space_constraint(o, pltpu.HBM) for o in operands + [cols_flat]])
 
 
 def tile_kernel(places, pick_ref, *refs):
@@ -275,13 +301,11 @@
         block = blocks[slot * SUB : (slot + 1) * SUB]
         mixed = jnp.dot(block, col_ref[slot], preferred_element_type=jnp.float32)
         mixed_ref[slot * SUB : (slot + 1) * SUB, :] = mixed.astype(jnp.bfloat16)
-    out_ref[...] = lax.dot_general(
-        row_ref[...], mixed_ref[...], (((0,), (0,)), ((), ())), preferred_element_type=jnp.float32
-    )
+    out_ref[...] = jnp.dot(row_ref[...], mixed_ref[...], preferred_element_type=jnp.float32)
 
 
 def tile_sum(pick, parts, places, row_weights, col_weights):
-    pixels = row_weights.shape[-1]
+    pixels = row_weights.shape[0]
     channels = col_weights.shape[-2]
     vmem = pl.BlockSpec(memory_space=pltpu.VMEM)
     return pl.pallas_call(
@@ -298,8 +322,8 @@
     )(
         pick,
         *parts,
-        row_weights.reshape(K_MAX * SUB, pixels),
-        col_weights.reshape(K_MAX, channels, pixels),
+        row_weights,
+        col_weights,
     )
 
 
@@ -320,14 +344,14 @@
 
     pair = in_order(polar, swap(polar, 1, devices))
     held = []
-    for even, odd in ((1, 2), (3, 4), (5, 6)):
+    for even, odd in ((1, 2), (4, 5), (6, 7)):
         routes = [(i, i ^ (2 * (odd if i % 2 else even))) for i in range(devices)]
         held.append(lax.ppermute(pair, "radial", routes))
-    last = swap(polar, 14, devices)
+    last = swap(polar, 6, devices)
     other = swap(jnp.concatenate(held + [last], 0), 1, devices)
     parts = [pair] + held + [other[i * size : (i + 1) * size] for i in range(3)]
     parts.append(in_order(last, other[3 * size :]))
-    places = [(0, 0), (1, 2), (3, 4), (5, 6), (2, 1), (4, 3), (6, 5), (7, 7)]
+    places = [(0, 0), (1, 2), (4, 5), (6, 7), (2, 1), (5, 4), (7, 6), (3, 3)]
     return parts, places
 
 
@@ -344,7 +368,7 @@
     col_weights,
 ):
     devices = lax.axis_size("radial")
-    polar, pick = march(
+    polar, pick, turned, cols = march(
         field_start,
         phase_table,
         profile_index,
@@ -353,9 +377,11 @@
         source_shift,
         slot_sub,
         tile_count,
+        row_weights,
+        col_weights,
     )
     parts, places = gather_parts(polar, devices)
-    tile_value = tile_sum(pick, parts, places, row_weights, col_weights)
+    tile_value = tile_sum(pick, parts, places, turned, cols)
     return tile_value.reshape((1, 1) + tile_value.shape)
 
 

time: 23.5 us -> 20.3 us (0.86)
  waiting for transfers between devices: 8.95 us -> 7.59 us
  local copies, waits for them, and re-layouts: 0.91 us -> 0.01 us
  starting transfers between devices: 8.56 us -> 7.7 us
    ppermute x3, starting transfers between devices: 7.96 us -> 6.5 us  [gather_parts(): held.append(lax.ppermute(pair, 'radial', routes))]
    ppermute x3, waiting for transfers between devices: 8.94 us -> 7.58 us  [swap(): lax.ppermute(value, 'radial', [(i, i ^ distance) for i in range(devices)])]
    unnamed x4 -> x0, local copies, waits for them, and re-layouts: 0.9 us -> none
    ppermute x3, starting transfers between devices: 0.59 us -> 1.2 us  [swap(): lax.ppermute(value, 'radial', [(i, i ^ distance) for i in range(devices)])]
where the time goes in v3:
time: 20.3 us; the launch traced here: 20.1 us
  starting transfers between devices  7.7 us (38%)
  waiting for transfers between devices  7.59 us (37%)
  Pallas kernels  4.76 us (23%)
    ppermute x3, waiting for transfers between devices, swap(): lax.ppermute(value, 'radial', [(i, i ^ distance) for i in range(devices)])  7.58 us
    ppermute x3, starting transfers between devices, gather_parts(): held.append(lax.ppermute(pair, 'radial', routes))  6.5 us
    pallas_call x1, Pallas kernels, march(): pl.pallas_call(functools.partial(march_kernel, steps, slabs), out_shape=[...  3.01 us
    pallas_call x1, Pallas kernels, tile_sum(): pl.pallas_call(functools.partial(tile_kernel, places), out_shape=jax.Shap...  1.75 us
    ppermute x3, starting transfers between devices, swap(): lax.ppermute(value, 'radial', [(i, i ^ distance) for i in range(devices)])  1.2 us
  transfers between devices with their start and end apart: 6, of which 3 were waited for; matrix products, arithmetic and copies ran while one was open for 0% of the time, Pallas kernels for 0%

profile of v3, /device:TPU:0, one launch (start us, length us, event | category | flops | bytes accessed | tf_op | source)
XLA Modules:
  0.0 20.1 jit_solution(15730685751252069499)
XLA Ops:
  0.0 3.0 %march.1 = (bf16[64,256]{1,0:T(8,128)(2,1)S(1)}, bf16[256,1024]{1,0:T(8,128)(2,1)S(1)}, bf16[256,256]{1,0:T(8,128)(2,1)S(1)}, bf16[16,256,256]{2,1,0:T(8,128)(2,1)S(1)}) custom-call(s32[2,2]{1,0:T(2,128)} %profile_hbm.1, f32[2]{0:T(128)} %power_hbm.1, s32[2]{0:T(128)} %slot_hbm.1, s32[1,16]{1,0:T(1,128)} %shift_hbm.1, s32[1,16,16]{2,1,0:T(8,128)} %sub_hbm.1, ...), custom_call_target="tpu_custom_call" | custom-call | tf_op jit(solution)/shard_map/march/pallas_call | solution.py:261
  3.0 0.5 %collective-permute-start = (bf16[64,256]{1,0:T(8,128)(2,1)S(1)}, bf16[64,256]{1,0:T(8,128)(2,1)S(1)}, u32[]{:S(2)}, u32[]{:S(2)}) collective-permute-start(bf16[64,256]{1,0:T(8,128)(2,1)S(1)} %get-tuple-element.10), channel_id=1, source_target_pairs={{0,1},{1,0},{2,3},{3,2},{4,5},{5,4},{6,7},{7,6},{8,9},{9,8},{10,11... | collective-permute-start | bytes 98312 | tf_op jit(solution)/shard_map/ppermute | solution.py:331
  3.5 0.9 %collective-permute-done = bf16[64,256]{1,0:T(8,128)(2,1)S(1)} collective-permute-done((bf16[64,256]{1,0:T(8,128)(2,1)S(1)}, bf16[64,256]{1,0:T(8,128)(2,1)S(1)}, u32[]{:S(2)}, u32[]{:S(2)}) %collective-permute-start) | collective-permute-done | bytes 32800 | tf_op jit(solution)/shard_map/ppermute | solution.py:331
  4.4 5.0 %collective-permute-start.3 = (bf16[128,256]{1,0:T(8,128)(2,1)S(1)}, bf16[128,256]{1,0:T(8,128)(2,1)S(1)}, u32[]{:S(2)}, u32[]{:S(2)}) collective-permute-start(bf16[128,256]{1,0:T(8,128)(2,1)S(1)} %maximum_select_fusion.refs_0_), channel_id=1, source_target_pairs={{0,12},{1,15},{2,14},{3,13},{4,8},{5,11},{6,10},{7,9},{8,4},{9,7},... | collective-permute-start | bytes 196616 | tf_op jit(solution)/shard_map/ppermute | solution.py:349
  9.4 0.0 collective-permute-start.2
  9.4 1.5 %collective-permute-start.1 = (bf16[128,256]{1,0:T(8,128)(2,1)S(1)}, bf16[128,256]{1,0:T(8,128)(2,1)S(1)}, u32[]{:S(2)}, u32[]{:S(2)}) collective-permute-start(bf16[128,256]{1,0:T(8,128)(2,1)S(1)} %maximum_select_fusion.refs_0_), channel_id=1, source_target_pairs={{0,2},{1,5},{2,0},{3,7},{4,6},{5,1},{6,4},{7,3},{8,10},{9,13},{10,... | collective-permute-start | bytes 196616 | tf_op jit(solution)/shard_map/ppermute | solution.py:349
  10.9 0.6 %collective-permute-start.4 = (bf16[64,256]{1,0:T(8,128)(2,1)S(1)}, bf16[64,256]{1,0:T(8,128)(2,1)S(1)}, u32[]{:S(2)}, u32[]{:S(2)}) collective-permute-start(bf16[64,256]{1,0:T(8,128)(2,1)S(1)} %get-tuple-element.10), channel_id=1, source_target_pairs={{0,6},{1,7},{2,4},{3,5},{4,2},{5,3},{6,0},{7,1},{8,14},{9,15},{10,... | collective-permute-start | bytes 98312 | tf_op jit(solution)/shard_map/ppermute | solution.py:331
  11.5 5.2 %collective-permute-done.4 = bf16[64,256]{1,0:T(8,128)(2,1)S(1)} collective-permute-done((bf16[64,256]{1,0:T(8,128)(2,1)S(1)}, bf16[64,256]{1,0:T(8,128)(2,1)S(1)}, u32[]{:S(2)}, u32[]{:S(2)}) %collective-permute-start.4) | collective-permute-done | bytes 32800 | tf_op jit(solution)/shard_map/ppermute | solution.py:331
  16.8 0.0 collective-permute-done.3.refs_3_
  16.8 0.0 collective-permute-done.2.refs_2_
  16.8 0.0 collective-permute-done.1.refs_1_
  16.8 0.1 collective-permute-start.5
  16.9 1.5 %collective-permute-done.5 = bf16[448,256]{1,0:T(8,128)(2,1)S(1)} collective-permute-done((bf16[448,256]{1,0:T(8,128)(2,1)S(1)}, bf16[448,256]{1,0:T(8,128)(2,1)S(1)}, u32[]{:S(2)}, u32[]{:S(2)}) %collective-permute-start.5) | collective-permute-done | bytes 229408 | tf_op jit(solution)/shard_map/ppermute | solution.py:331
  18.4 1.8 %tile_sum.1 = f32[256,256]{1,0:T(8,128)} custom-call(bf16[256,1024]{1,0:T(8,128)(2,1)S(1)} %get-tuple-element.9.pick_ref, bf16[128,256]{1,0:T(8,128)(2,1)S(1)} %maximum_select_fusion.refs_0_, bf16[128,256]{1,0:T(8,128)(2,1)S(1)} %collective-permute-done.1.refs_1_, bf16[128,256]{1,0:T(8,128)(2,1)S(1)} %collective-permute-done.2.refs_2_, ...), custom_call_target="tpu_custom_call" | custom-call | tf_op jit(solution)/shard_map/tile_sum/pallas_call | solution.py:311
  (4 shorter events, 0.1 us)
Async XLA Ops:
  3.0 1.4 %collective-permute-start = (bf16[64,256]{1,0:T(8,128)(2,1)S(1)}, bf16[64,256]{1,0:T(8,128)(2,1)S(1)}, u32[]{:S(2)}, u32[]{:S(2)}) collective-permute-start(bf16[64,256]{1,0:T(8,128)(2,1)S(1)} %get-tuple-element.10), channel_id=1, source_target_pairs={{0,1},{1,0},{2,3},{3,2},{4,5},{5,4},{6,7},{7,6},{8,9},{9,8},{10,11... | collective-permute-start | bytes 98312 | tf_op jit(solution)/shard_map/ppermute | solution.py:331
  4.4 12.4 %collective-permute-start.3 = (bf16[128,256]{1,0:T(8,128)(2,1)S(1)}, bf16[128,256]{1,0:T(8,128)(2,1)S(1)}, u32[]{:S(2)}, u32[]{:S(2)}) collective-permute-start(bf16[128,256]{1,0:T(8,128)(2,1)S(1)} %maximum_select_fusion.refs_0_), channel_id=1, source_target_pairs={{0,12},{1,15},{2,14},{3,13},{4,8},{5,11},{6,10},{7,9},{8,4},{9,7},... | collective-permute-start | bytes 196616 | tf_op jit(solution)/shard_map/ppermute | solution.py:349
  9.4 7.4 %collective-permute-start.2 = (bf16[128,256]{1,0:T(8,128)(2,1)S(1)}, bf16[128,256]{1,0:T(8,128)(2,1)S(1)}, u32[]{:S(2)}, u32[]{:S(2)}) collective-permute-start(bf16[128,256]{1,0:T(8,128)(2,1)S(1)} %maximum_select_fusion.refs_0_), channel_id=1, source_target_pairs={{0,8},{1,11},{2,10},{3,9},{4,12},{5,15},{6,14},{7,13},{8,0},{9,3},... | collective-permute-start | bytes 196616 | tf_op jit(solution)/shard_map/ppermute | solution.py:349
  9.4 7.4 %collective-permute-start.1 = (bf16[128,256]{1,0:T(8,128)(2,1)S(1)}, bf16[128,256]{1,0:T(8,128)(2,1)S(1)}, u32[]{:S(2)}, u32[]{:S(2)}) collective-permute-start(bf16[128,256]{1,0:T(8,128)(2,1)S(1)} %maximum_select_fusion.refs_0_), channel_id=1, source_target_pairs={{0,2},{1,5},{2,0},{3,7},{4,6},{5,1},{6,4},{7,3},{8,10},{9,13},{10,... | collective-permute-start | bytes 196616 | tf_op jit(solution)/shard_map/ppermute | solution.py:349
  10.9 5.9 %collective-permute-start.4 = (bf16[64,256]{1,0:T(8,128)(2,1)S(1)}, bf16[64,256]{1,0:T(8,128)(2,1)S(1)}, u32[]{:S(2)}, u32[]{:S(2)}) collective-permute-start(bf16[64,256]{1,0:T(8,128)(2,1)S(1)} %get-tuple-element.10), channel_id=1, source_target_pairs={{0,6},{1,7},{2,4},{3,5},{4,2},{5,3},{6,0},{7,1},{8,14},{9,15},{10,... | collective-permute-start | bytes 98312 | tf_op jit(solution)/shard_map/ppermute | solution.py:331
  16.8 1.6 %collective-permute-start.5 = (bf16[448,256]{1,0:T(8,128)(2,1)S(1)}, bf16[448,256]{1,0:T(8,128)(2,1)S(1)}, u32[]{:S(2)}, u32[]{:S(2)}) collective-permute-start(bf16[448,256]{1,0:T(8,128)(2,1)S(1)} %pad_maximum_fusion), channel_id=1, source_target_pairs={{0,1},{1,0},{2,3},{3,2},{4,5},{5,4},{6,7},{7,6},{8,9},{9,8},{10,11... | collective-permute-start | bytes 688136 | tf_op jit(solution)/shard_map/ppermute | solution.py:331

commit v4 on v2

--- a/solution.py
+++ b/solution.py
@@ -56,21 +56,14 @@
     profile_hbm,
     power_hbm,
     slot_hbm,
-    shift_hbm,
-    sub_hbm,
-    count_hbm,
     field_hbm,
     phase_hbm,
     weight_hbm,
     wave_hbm,
     polar_ref,
-    pick_ref,
     profile_ref,
     power_ref,
     slot_ref,
-    shift_ref,
-    sub_ref,
-    count_ref,
     field_ref,
     phase_ref,
     weight_ref,
@@ -92,9 +85,6 @@
         (weight_hbm, weight_ref),
         (power_hbm, power_ref),
         (slot_hbm, slot_ref),
-        (shift_hbm, shift_ref),
-        (sub_hbm, sub_ref),
-        (count_hbm, count_ref),
     )
     copies = [
         pltpu.make_async_copy(source, target, sems.at[number])
@@ -106,7 +96,6 @@
     quarter = height // RADIX
     slab = lax.axis_index("range")
     tile = lax.axis_index("radial")
-    devices = lax.axis_size("radial")
     total = slabs * steps
     for copy in copies[:3]:
         copy.wait()
@@ -128,16 +117,6 @@
     gain = power_ref[slot_ref[tile * rows // GROUP_RADIALS]]
     real_ref[...] = field_ref[0].astype(jnp.float32)
     imag_ref[...] = field_ref[1].astype(jnp.float32)
-
-    shape = (SUB, pick_ref.shape[1])
-    offset = lax.broadcasted_iota(jnp.int32, shape, 1) - lax.broadcasted_iota(jnp.int32, shape, 0)
-    for slot in range(K_MAX):
-        source = lax.rem(tile + shift_ref[0, tile] + slot // CAP, devices)
-        start = source * rows + sub_ref[0, tile, slot] * SUB
-        start = jnp.where(slot < count_ref[0, tile], start, -height * devices)
-        pick_ref[slot * SUB : (slot + 1) * SUB, :] = jnp.where(offset == start, 1.0, 0.0).astype(
-            jnp.bfloat16
-        )
 
     def one_step(place, step):
         for row in range(0, rows, 16):
@@ -223,25 +202,21 @@
     lax.fori_loop(0, slab + 1, one_slab, 0)
 
 
-def march(
-    field, phase_table, profile_index, group_power, group_slot, source_shift, slot_sub, tile_count
-):
+def in_hbm(operands):
+    return [pltpu.with_memory_space_constraint(value, pltpu.HBM) for value in operands]
+
+
+def march(field, phase_table, profile_index, group_power, group_slot):
     rows, height = field.shape[1:]
     slabs, steps = profile_index.shape
     weights, waves = march_constants(height)
-    operands = [profile_index, group_power, group_slot, source_shift, slot_sub, tile_count]
-    places = [pltpu.SMEM] * len(operands)
-    operands += [field, phase_table, weights, waves]
-    places += [pltpu.VMEM] * 4
-    radials = rows * lax.axis_size("radial")
+    operands = [profile_index, group_power, group_slot, field, phase_table, weights, waves]
+    places = [pltpu.SMEM] * 3 + [pltpu.VMEM] * 4
     return pl.pallas_call(
         functools.partial(march_kernel, steps, slabs),
-        out_shape=[
-            jax.ShapeDtypeStruct((rows, steps * VB), jnp.bfloat16),
-            jax.ShapeDtypeStruct((K_MAX * SUB, radials), jnp.bfloat16),
-        ],
+        out_shape=jax.ShapeDtypeStruct((rows, steps * VB), jnp.bfloat16),
         in_specs=[pl.BlockSpec(memory_space=pltpu.HBM)] * len(operands),
-        out_specs=[pl.BlockSpec(memory_space=pltpu.VMEM)] * 2,
+        out_specs=pl.BlockSpec(memory_space=pltpu.VMEM),
         scratch_shapes=[place(o.shape, o.dtype) for place, o in zip(places, operands)]
         + [
             pltpu.VMEM((-(-slabs * steps // 8) * 8, height), jnp.float32),
@@ -255,7 +230,84 @@
         ],
         compiler_params=pltpu.CompilerParams(vmem_limit_bytes=24 * 1024 * 1024),
         name="march",
-    )(*[pltpu.with_memory_space_constraint(o, pltpu.HBM) for o in operands])
+    )(*in_hbm(operands))
+
+
+def prepare_kernel(
+    local_rows,
+    shift_hbm,
+    sub_hbm,
+    count_hbm,
+    row_hbm,
+    col_hbm,
+    after_ref,
+    pick_ref,
+    turned_ref,
+    col_ref,
+    passed_ref,
+    shift_ref,
+    sub_ref,
+    count_ref,
+    row_ref,
+    sems,
+):
+    pairs = (
+        (shift_hbm, shift_ref),
+        (sub_hbm, sub_ref),
+        (count_hbm, count_ref),
+        (row_hbm, row_ref),
+        (col_hbm, col_ref),
+    )
+    copies = [
+        pltpu.make_async_copy(source, target, sems.at[number])
+        for number, (source, target) in enumerate(pairs)
+    ]
+    for copy in copies:
+        copy.start()
+    tile = lax.axis_index("radial")
+    devices = lax.axis_size("radial")
+    for copy in copies[:4]:
+        copy.wait()
+    shape = (SUB, pick_ref.shape[1])
+    offset = lax.broadcasted_iota(jnp.int32, shape, 1) - lax.broadcasted_iota(jnp.int32, shape, 0)
+    for slot in range(K_MAX):
+        source = lax.rem(tile + shift_ref[0, tile] + slot // CAP, devices)
+        start = source * local_rows + sub_ref[0, tile, slot] * SUB
+        start = jnp.where(slot < count_ref[0, tile], start, -2 * pick_ref.shape[1])
+        pick_ref[slot * SUB : (slot + 1) * SUB, :] = jnp.where(offset == start, 1.0, 0.0).astype(
+            jnp.bfloat16
+        )
+    turned_ref[...] = row_ref[...].T
+    passed_ref[...] = after_ref[: passed_ref.shape[0], :]
+    copies[4].wait()
+
+
+def prepare(source_shift, slot_sub, tile_count, row_weights, col_weights, local_rows, after):
+    pixels = row_weights.shape[-1]
+    radials = local_rows * lax.axis_size("radial")
+    rows_flat = row_weights.reshape(K_MAX * SUB, pixels)
+    cols_flat = col_weights.reshape(K_MAX, col_weights.shape[-2], pixels)
+    operands = [source_shift, slot_sub, tile_count, rows_flat]
+    places = [pltpu.SMEM] * 3 + [pltpu.VMEM]
+    return pl.pallas_call(
+        functools.partial(prepare_kernel, local_rows),
+        out_shape=[
+            jax.ShapeDtypeStruct((K_MAX * SUB, radials), jnp.bfloat16),
+            jax.ShapeDtypeStruct((pixels, K_MAX * SUB), jnp.bfloat16),
+            jax.ShapeDtypeStruct(cols_flat.shape, jnp.bfloat16),
+            jax.ShapeDtypeStruct((local_rows, after.shape[1]), after.dtype),
+        ],
+        in_specs=[pl.BlockSpec(memory_space=pltpu.HBM)] * 5
+        + [pl.BlockSpec(memory_space=pltpu.VMEM)],
+        out_specs=[pl.BlockSpec(memory_space=pltpu.VMEM)] * 4,
+        scratch_shapes=[place(o.shape, o.dtype) for place, o in zip(places, operands)]
+        + [pltpu.SemaphoreType.DMA((5,))],
+        compiler_params=pltpu.CompilerParams(vmem_limit_bytes=24 * 1024 * 1024),
+        cost_estimate=pl.CostEstimate(
+            flops=0, bytes_accessed=2 * cols_flat.size, transcendentals=0
+        ),
+        name="prepare",
+    )(*in_hbm(operands + [cols_flat]), after)
 
 
 def tile_kernel(places, pick_ref, *refs):
@@ -275,13 +327,11 @@
         block = blocks[slot * SUB : (slot + 1) * SUB]
         mixed = jnp.dot(block, col_ref[slot], preferred_element_type=jnp.float32)
         mixed_ref[slot * SUB : (slot + 1) * SUB, :] = mixed.astype(jnp.bfloat16)
-    out_ref[...] = lax.dot_general(
-        row_ref[...], mixed_ref[...], (((0,), (0,)), ((), ())), preferred_element_type=jnp.float32
-    )
+    out_ref[...] = jnp.dot(row_ref[...], mixed_ref[...], preferred_element_type=jnp.float32)
 
 
 def tile_sum(pick, parts, places, row_weights, col_weights):
-    pixels = row_weights.shape[-1]
+    pixels = row_weights.shape[0]
     channels = col_weights.shape[-2]
     vmem = pl.BlockSpec(memory_space=pltpu.VMEM)
     return pl.pallas_call(
@@ -298,8 +348,8 @@
     )(
         pick,
         *parts,
-        row_weights.reshape(K_MAX * SUB, pixels),
-        col_weights.reshape(K_MAX, channels, pixels),
+        row_weights,
+        col_weights,
     )
 
 
@@ -307,9 +357,10 @@
     return lax.ppermute(value, "radial", [(i, i ^ distance) for i in range(devices)])
 
 
-def gather_parts(polar, devices):
+def gather_parts(polar, devices, prepared):
     if devices != 16:
-        return [lax.all_gather(polar, "radial", axis=0, tiled=True)], [(0, 0)]
+        whole = lax.all_gather(polar, "radial", axis=0, tiled=True)
+        return [whole], [(0, 0)], prepared(polar)[:3]
     core = lax.axis_index("radial") % 2
     size = 2 * polar.shape[0]
 
@@ -318,17 +369,19 @@
             core == 0, jnp.concatenate([own, other], 0), jnp.concatenate([other, own], 0)
         )
 
+    longest = jnp.concatenate([polar, polar, polar[: size // 8]], 0)
+    first = swap(longest, 2, devices)
     pair = in_order(polar, swap(polar, 1, devices))
     held = []
-    for even, odd in ((1, 2), (3, 4), (5, 6)):
+    for even, odd in ((2, 3), (6, 7), (4, 5)):
         routes = [(i, i ^ (2 * (odd if i % 2 else even))) for i in range(devices)]
         held.append(lax.ppermute(pair, "radial", routes))
-    last = swap(polar, 14, devices)
-    other = swap(jnp.concatenate(held + [last], 0), 1, devices)
+    *ready, first = prepared(first)
+    other = swap(jnp.concatenate(held + [first], 0), 1, devices)
     parts = [pair] + held + [other[i * size : (i + 1) * size] for i in range(3)]
-    parts.append(in_order(last, other[3 * size :]))
-    places = [(0, 0), (1, 2), (3, 4), (5, 6), (2, 1), (4, 3), (6, 5), (7, 7)]
-    return parts, places
+    parts.append(in_order(first, other[3 * size :]))
+    places = [(0, 0), (2, 3), (6, 7), (4, 5), (3, 2), (7, 6), (5, 4), (1, 1)]
+    return parts, places, ready
 
 
 def per_device(
@@ -344,18 +397,13 @@
     col_weights,
 ):
     devices = lax.axis_size("radial")
-    polar, pick = march(
-        field_start,
-        phase_table,
-        profile_index,
-        group_power,
-        group_slot,
-        source_shift,
-        slot_sub,
-        tile_count,
+    polar = march(field_start, phase_table, profile_index, group_power, group_slot)
+    prepared = functools.partial(
+        prepare, source_shift, slot_sub, tile_count, row_weights, col_weights, polar.shape[0]
     )
-    parts, places = gather_parts(polar, devices)
-    tile_value = tile_sum(pick, parts, places, row_weights, col_weights)
+    parts, places, ready = gather_parts(polar, devices, prepared)
+    pick, turned, cols = ready
+    tile_value = tile_sum(pick, parts, places, turned, cols)
     return tile_value.reshape((1, 1) + tile_value.shape)
 
 

time: 23.5 us -> 19.9 us (0.85)
  the two profiles are of different devices: /device:TPU:0 before, /device:TPU:5 now
where the time goes in v4:
time: 19.9 us; the launch traced here: 19.8 us
  Pallas kernels  7.42 us (37%)
  starting transfers between devices  6.87 us (35%)
  waiting for transfers between devices  5.37 us (27%)
    ppermute x3, starting transfers between devices, gather_parts(): held.append(lax.ppermute(pair, 'radial', routes))  4.57 us
    ppermute x3, waiting for transfers between devices, gather_parts(): held.append(lax.ppermute(pair, 'radial', routes))  4.1 us
    pallas_call x1, Pallas kernels, march(): pl.pallas_call(functools.partial(march_kernel, steps, slabs), out_shape=j...  3.95 us
    ppermute x3, starting transfers between devices, swap(): lax.ppermute(value, 'radial', [(i, i ^ distance) for i in range(devices)])  2.3 us
    pallas_call x1, Pallas kernels, tile_sum(): pl.pallas_call(functools.partial(tile_kernel, places), out_shape=jax.Shap...  1.76 us
    pallas_call x1, Pallas kernels, prepare(): pl.pallas_call(functools.partial(prepare_kernel, local_rows), out_shape=[...  1.71 us
    ppermute x3, waiting for transfers between devices, swap(): lax.ppermute(value, 'radial', [(i, i ^ distance) for i in range(devices)])  1.28 us
  transfers between devices with their start and end apart: 6, of which 3 were waited for; matrix products, arithmetic and copies ran while one was open for 0% of the time, Pallas kernels for 9%

profile of v4, /device:TPU:5, one launch (start us, length us, event | category | flops | bytes accessed | tf_op | source)
XLA Modules:
  0.0 19.8 jit_solution(12158177917574519342)
XLA Ops:
  0.0 3.9 %march.1 = bf16[64,256]{1,0:T(8,128)(2,1)S(1)} custom-call(s32[2,2]{1,0:T(2,128)} %profile_hbm.1, f32[2]{0:T(128)} %power_hbm.1, s32[2]{0:T(128)} %slot_hbm.1, bf16[2,64,1024]{2,1,0:T(8,128)(2,1)} %field_hbm.1, f32[16,1024]{1,0:T(8,128)} %phase_hbm.1, bf16[512,512]{1,0:T(8,128)(2,1)} %constant.22.clone.weight_hbm, f32[24,256]{1,0:T(8,128)} %constant.23.clone.wave_hbm), custom_call_target="tpu_custom_call" | custom-call | tf_op jit(solution)/shard_map/march/pallas_call | solution.py:215
  4.0 0.7 %collective-permute-start.1 = (bf16[64,256]{1,0:T(8,128)(2,1)S(1)}, bf16[64,256]{1,0:T(8,128)(2,1)S(1)}, u32[]{:S(2)}, u32[]{:S(2)}) collective-permute-start(bf16[64,256]{1,0:T(8,128)(2,1)S(1)} %march.1), channel_id=1, source_target_pairs={{0,1},{1,0},{2,3},{3,2},{4,5},{5,4},{6,7},{7,6},{8,9},{9,8},{10,11... | collective-permute-start | bytes 98312 | tf_op jit(solution)/shard_map/ppermute | solution.py:357
  4.7 1.3 %collective-permute-start = (bf16[144,256]{1,0:T(8,128)(2,1)S(1)}, bf16[144,256]{1,0:T(8,128)(2,1)S(1)}, u32[]{:S(2)}, u32[]{:S(2)}) collective-permute-start(bf16[144,256]{1,0:T(8,128)(2,1)S(1)} %pad_maximum_fusion.1), channel_id=1, source_target_pairs={{0,2},{1,3},{2,0},{3,1},{4,6},{5,7},{6,4},{7,5},{8,10},{9,11},{10,... | collective-permute-start | bytes 221192 | tf_op jit(solution)/shard_map/ppermute | solution.py:357
  6.0 0.0 collective-permute-done.1
  6.0 2.9 %collective-permute-start.4 = (bf16[128,256]{1,0:T(8,128)(2,1)S(1)}, bf16[128,256]{1,0:T(8,128)(2,1)S(1)}, u32[]{:S(2)}, u32[]{:S(2)}) collective-permute-start(bf16[128,256]{1,0:T(8,128)(2,1)S(1)} %maximum_select_fusion.refs_0_), channel_id=1, source_target_pairs={{0,8},{1,11},{2,10},{3,9},{4,12},{5,15},{6,14},{7,13},{8,0},{9,3},... | collective-permute-start | bytes 196616 | tf_op jit(solution)/shard_map/ppermute | solution.py:378
  8.9 1.5 %collective-permute-start.3 = (bf16[128,256]{1,0:T(8,128)(2,1)S(1)}, bf16[128,256]{1,0:T(8,128)(2,1)S(1)}, u32[]{:S(2)}, u32[]{:S(2)}) collective-permute-start(bf16[128,256]{1,0:T(8,128)(2,1)S(1)} %maximum_select_fusion.refs_0_), channel_id=1, source_target_pairs={{0,12},{1,15},{2,14},{3,13},{4,8},{5,11},{6,10},{7,9},{8,4},{9,7},... | collective-permute-start | bytes 196616 | tf_op jit(solution)/shard_map/ppermute | solution.py:378
  10.4 0.2 %collective-permute-start.2 = (bf16[128,256]{1,0:T(8,128)(2,1)S(1)}, bf16[128,256]{1,0:T(8,128)(2,1)S(1)}, u32[]{:S(2)}, u32[]{:S(2)}) collective-permute-start(bf16[128,256]{1,0:T(8,128)(2,1)S(1)} %maximum_select_fusion.refs_0_), channel_id=1, source_target_pairs={{0,4},{1,7},{2,6},{3,5},{4,0},{5,3},{6,2},{7,1},{8,12},{9,15},{10,... | collective-permute-start | bytes 196616 | tf_op jit(solution)/shard_map/ppermute | solution.py:378
  10.6 0.0 collective-permute-done.after_ref
  10.6 1.7 %prepare.1 = (bf16[256,1024]{1,0:T(8,128)(2,1)S(1)}, bf16[256,256]{1,0:T(8,128)(2,1)S(1)}, bf16[16,256,256]{2,1,0:T(8,128)(2,1)S(1)}, bf16[64,256]{1,0:T(8,128)(2,1)S(1)}) custom-call(s32[1,16]{1,0:T(1,128)} %shift_hbm.1, s32[1,16,16]{2,1,0:T(8,128)} %sub_hbm.1, s32[1,16]{1,0:T(1,128)} %count_hbm.1, bf16[256,256]{1,0:T(8,128)(2,1)} %bitcast.4, ...), custom_call_target="tpu_custom_call" | custom-call | bytes 2097152 | tf_op jit(solution)/shard_map/prepare/pallas_call | solution.py:292
  12.3 0.0 collective-permute-done.4.refs_3_
  12.3 3.0 %collective-permute-done.3.refs_2_ = bf16[128,256]{1,0:T(8,128)(2,1)S(1)} collective-permute-done((bf16[128,256]{1,0:T(8,128)(2,1)S(1)}, bf16[128,256]{1,0:T(8,128)(2,1)S(1)}, u32[]{:S(2)}, u32[]{:S(2)}) %collective-permute-start.3) | collective-permute-done | bytes 65568 | tf_op jit(solution)/shard_map/ppermute | solution.py:378
  15.3 1.1 %collective-permute-done.2.refs_1_ = bf16[128,256]{1,0:T(8,128)(2,1)S(1)} collective-permute-done((bf16[128,256]{1,0:T(8,128)(2,1)S(1)}, bf16[128,256]{1,0:T(8,128)(2,1)S(1)}, u32[]{:S(2)}, u32[]{:S(2)}) %collective-permute-start.2) | collective-permute-done | bytes 65568 | tf_op jit(solution)/shard_map/ppermute | solution.py:378
  16.4 0.3 %collective-permute-start.5 = (bf16[448,256]{1,0:T(8,128)(2,1)S(1)}, bf16[448,256]{1,0:T(8,128)(2,1)S(1)}, u32[]{:S(2)}, u32[]{:S(2)}) collective-permute-start(bf16[448,256]{1,0:T(8,128)(2,1)S(1)} %pad_maximum_fusion), channel_id=1, source_target_pairs={{0,1},{1,0},{2,3},{3,2},{4,5},{5,4},{6,7},{7,6},{8,9},{9,8},{10,11... | collective-permute-start | bytes 688136 | tf_op jit(solution)/shard_map/ppermute | solution.py:357
  16.7 1.3 %collective-permute-done.5 = bf16[448,256]{1,0:T(8,128)(2,1)S(1)} collective-permute-done((bf16[448,256]{1,0:T(8,128)(2,1)S(1)}, bf16[448,256]{1,0:T(8,128)(2,1)S(1)}, u32[]{:S(2)}, u32[]{:S(2)}) %collective-permute-start.5) | collective-permute-done | bytes 229408 | tf_op jit(solution)/shard_map/ppermute | solution.py:357
  18.0 1.8 %tile_sum.1 = f32[256,256]{1,0:T(8,128)} custom-call(bf16[256,1024]{1,0:T(8,128)(2,1)S(1)} %get-tuple-element.9.pick_ref, bf16[128,256]{1,0:T(8,128)(2,1)S(1)} %maximum_select_fusion.refs_0_, bf16[128,256]{1,0:T(8,128)(2,1)S(1)} %collective-permute-done.2.refs_1_, bf16[128,256]{1,0:T(8,128)(2,1)S(1)} %collective-permute-done.3.refs_2_, ...), custom_call_target="tpu_custom_call" | custom-call | tf_op jit(solution)/shard_map/tile_sum/pallas_call | solution.py:337
  (6 shorter events, 0.1 us)
Async XLA Ops:
  4.0 2.0 %collective-permute-start.1 = (bf16[64,256]{1,0:T(8,128)(2,1)S(1)}, bf16[64,256]{1,0:T(8,128)(2,1)S(1)}, u32[]{:S(2)}, u32[]{:S(2)}) collective-permute-start(bf16[64,256]{1,0:T(8,128)(2,1)S(1)} %march.1), channel_id=1, source_target_pairs={{0,1},{1,0},{2,3},{3,2},{4,5},{5,4},{6,7},{7,6},{8,9},{9,8},{10,11... | collective-permute-start | bytes 98312 | tf_op jit(solution)/shard_map/ppermute | solution.py:357
  4.7 5.9 %collective-permute-start = (bf16[144,256]{1,0:T(8,128)(2,1)S(1)}, bf16[144,256]{1,0:T(8,128)(2,1)S(1)}, u32[]{:S(2)}, u32[]{:S(2)}) collective-permute-start(bf16[144,256]{1,0:T(8,128)(2,1)S(1)} %pad_maximum_fusion.1), channel_id=1, source_target_pairs={{0,2},{1,3},{2,0},{3,1},{4,6},{5,7},{6,4},{7,5},{8,10},{9,11},{10,... | collective-permute-start | bytes 221192 | tf_op jit(solution)/shard_map/ppermute | solution.py:357
  6.0 6.3 %collective-permute-start.4 = (bf16[128,256]{1,0:T(8,128)(2,1)S(1)}, bf16[128,256]{1,0:T(8,128)(2,1)S(1)}, u32[]{:S(2)}, u32[]{:S(2)}) collective-permute-start(bf16[128,256]{1,0:T(8,128)(2,1)S(1)} %maximum_select_fusion.refs_0_), channel_id=1, source_target_pairs={{0,8},{1,11},{2,10},{3,9},{4,12},{5,15},{6,14},{7,13},{8,0},{9,3},... | collective-permute-start | bytes 196616 | tf_op jit(solution)/shard_map/ppermute | solution.py:378
  8.9 6.4 %collective-permute-start.3 = (bf16[128,256]{1,0:T(8,128)(2,1)S(1)}, bf16[128,256]{1,0:T(8,128)(2,1)S(1)}, u32[]{:S(2)}, u32[]{:S(2)}) collective-permute-start(bf16[128,256]{1,0:T(8,128)(2,1)S(1)} %maximum_select_fusion.refs_0_), channel_id=1, source_target_pairs={{0,12},{1,15},{2,14},{3,13},{4,8},{5,11},{6,10},{7,9},{8,4},{9,7},... | collective-permute-start | bytes 196616 | tf_op jit(solution)/shard_map/ppermute | solution.py:378
  10.4 6.1 %collective-permute-start.2 = (bf16[128,256]{1,0:T(8,128)(2,1)S(1)}, bf16[128,256]{1,0:T(8,128)(2,1)S(1)}, u32[]{:S(2)}, u32[]{:S(2)}) collective-permute-start(bf16[128,256]{1,0:T(8,128)(2,1)S(1)} %maximum_select_fusion.refs_0_), channel_id=1, source_target_pairs={{0,4},{1,7},{2,6},{3,5},{4,0},{5,3},{6,2},{7,1},{8,12},{9,15},{10,... | collective-permute-start | bytes 196616 | tf_op jit(solution)/shard_map/ppermute | solution.py:378
  16.4 1.6 %collective-permute-start.5 = (bf16[448,256]{1,0:T(8,128)(2,1)S(1)}, bf16[448,256]{1,0:T(8,128)(2,1)S(1)}, u32[]{:S(2)}, u32[]{:S(2)}) collective-permute-start(bf16[448,256]{1,0:T(8,128)(2,1)S(1)} %pad_maximum_fusion), channel_id=1, source_target_pairs={{0,1},{1,0},{2,3},{3,2},{4,5},{5,4},{6,7},{7,6},{8,9},{9,8},{10,11... | collective-permute-start | bytes 688136 | tf_op jit(solution)/shard_map/ppermute | solution.py:357

commit v5 on v4

--- a/solution.py
+++ b/solution.py
@@ -278,7 +278,7 @@
             jnp.bfloat16
         )
     turned_ref[...] = row_ref[...].T
-    passed_ref[...] = after_ref[: passed_ref.shape[0], :]
+    passed_ref[...] = after_ref[...]
     copies[4].wait()
 
 
@@ -295,7 +295,7 @@
             jax.ShapeDtypeStruct((K_MAX * SUB, radials), jnp.bfloat16),
             jax.ShapeDtypeStruct((pixels, K_MAX * SUB), jnp.bfloat16),
             jax.ShapeDtypeStruct(cols_flat.shape, jnp.bfloat16),
-            jax.ShapeDtypeStruct((local_rows, after.shape[1]), after.dtype),
+            jax.ShapeDtypeStruct(after.shape, after.dtype),
         ],
         in_specs=[pl.BlockSpec(memory_space=pltpu.HBM)] * 5
         + [pl.BlockSpec(memory_space=pltpu.VMEM)],
@@ -304,7 +304,7 @@
         + [pltpu.SemaphoreType.DMA((5,))],
         compiler_params=pltpu.CompilerParams(vmem_limit_bytes=24 * 1024 * 1024),
         cost_estimate=pl.CostEstimate(
-            flops=0, bytes_accessed=2 * cols_flat.size, transcendentals=0
+            flops=200_000_000_000, bytes_accessed=2 * cols_flat.size, transcendentals=0
         ),
         name="prepare",
     )(*in_hbm(operands + [cols_flat]), after)
@@ -369,18 +369,17 @@
             core == 0, jnp.concatenate([own, other], 0), jnp.concatenate([other, own], 0)
         )
 
-    longest = jnp.concatenate([polar, polar, polar[: size // 8]], 0)
-    first = swap(longest, 2, devices)
+    first = swap(polar, 12, devices)
     pair = in_order(polar, swap(polar, 1, devices))
     held = []
-    for even, odd in ((2, 3), (6, 7), (4, 5)):
+    for even, odd in ((2, 3), (7, 1), (4, 5)):
         routes = [(i, i ^ (2 * (odd if i % 2 else even))) for i in range(devices)]
         held.append(lax.ppermute(pair, "radial", routes))
     *ready, first = prepared(first)
     other = swap(jnp.concatenate(held + [first], 0), 1, devices)
     parts = [pair] + held + [other[i * size : (i + 1) * size] for i in range(3)]
     parts.append(in_order(first, other[3 * size :]))
-    places = [(0, 0), (2, 3), (6, 7), (4, 5), (3, 2), (7, 6), (5, 4), (1, 1)]
+    places = [(0, 0), (2, 3), (7, 1), (4, 5), (3, 2), (1, 7), (5, 4), (6, 6)]
     return parts, places, ready
 
 

time: 19.9 us -> 22.6 us (1.14)
  the two profiles are of different devices: /device:TPU:5 before, /device:TPU:0 now
where the time goes in v5:
time: 22.6 us; the launch traced here: 22.2 us
  starting transfers between devices  9.69 us (43%)
  Pallas kernels  7.01 us (31%)
  waiting for transfers between devices  3.83 us (17%)
  other arithmetic  1.58 us (7%)
    ppermute x3, starting transfers between devices, swap(): lax.ppermute(value, 'radial', [(i, i ^ distance) for i in range(devices)])  5.27 us
    ppermute x3, starting transfers between devices, gather_parts(): held.append(lax.ppermute(pair, 'radial', routes))  4.42 us
    pallas_call x1, Pallas kernels, tile_sum(): pl.pallas_call(functools.partial(tile_kernel, places), out_shape=jax.Shap...  2.68 us
    pallas_call x1, Pallas kernels, march(): pl.pallas_call(functools.partial(march_kernel, steps, slabs), out_shape=j...  2.62 us
    ppermute x3, waiting for transfers between devices, gather_parts(): held.append(lax.ppermute(pair, 'radial', routes))  2.35 us
    pallas_call x1, Pallas kernels, prepare(): pl.pallas_call(functools.partial(prepare_kernel, local_rows), out_shape=[...  1.71 us
    ppermute x3, waiting for transfers between devices, swap(): lax.ppermute(value, 'radial', [(i, i ^ distance) for i in range(devices)])  1.48 us
    concatenate x1, other arithmetic, gather_parts(): other = swap(jnp.concatenate(held + [first], 0), 1, devices)  0.92 us
  transfers between devices with their start and end apart: 6, of which 4 were waited for; matrix products, arithmetic and copies ran while one was open for 3% of the time, Pallas kernels for 8%

profile of v5, /device:TPU:0, one launch (start us, length us, event | category | flops | bytes accessed | tf_op | source)
XLA Modules:
  0.0 22.2 jit_solution(8153961745244480485)
XLA Ops:
  0.0 2.6 %march.1 = bf16[64,256]{1,0:T(8,128)(2,1)S(1)} custom-call(s32[2,2]{1,0:T(2,128)} %profile_hbm.1, f32[2]{0:T(128)} %power_hbm.1, s32[2]{0:T(128)} %slot_hbm.1, bf16[2,64,1024]{2,1,0:T(8,128)(2,1)} %field_hbm.1, f32[16,1024]{1,0:T(8,128)} %phase_hbm.1, bf16[512,512]{1,0:T(8,128)(2,1)} %constant.22.clone.weight_hbm, f32[24,256]{1,0:T(8,128)} %constant.23.clone.wave_hbm), custom_call_target="tpu_custom_call" | custom-call | tf_op jit(solution)/shard_map/march/pallas_call | solution.py:215
  2.6 0.5 %collective-permute-start.1 = (bf16[64,256]{1,0:T(8,128)(2,1)S(1)}, bf16[64,256]{1,0:T(8,128)(2,1)S(1)}, u32[]{:S(2)}, u32[]{:S(2)}) collective-permute-start(bf16[64,256]{1,0:T(8,128)(2,1)S(1)} %march.1), channel_id=1, source_target_pairs={{0,1},{1,0},{2,3},{3,2},{4,5},{5,4},{6,7},{7,6},{8,9},{9,8},{10,11... | collective-permute-start | bytes 98312 | tf_op jit(solution)/shard_map/ppermute | solution.py:357
  3.1 4.7 %collective-permute-start = (bf16[64,256]{1,0:T(8,128)(2,1)S(1)}, bf16[64,256]{1,0:T(8,128)(2,1)S(1)}, u32[]{:S(2)}, u32[]{:S(2)}) collective-permute-start(bf16[64,256]{1,0:T(8,128)(2,1)S(1)} %march.1), channel_id=1, source_target_pairs={{0,12},{1,13},{2,14},{3,15},{4,8},{5,9},{6,10},{7,11},{8,4},{9,5},... | collective-permute-start | bytes 98312 | tf_op jit(solution)/shard_map/ppermute | solution.py:357
  7.8 0.0 collective-permute-done.1
  7.8 0.6 %maximum_select_fusion.refs_0_ = bf16[128,256]{1,0:T(8,128)(2,1)} fusion(bf16[64,256]{1,0:T(8,128)(2,1)S(1)} %collective-permute-done.1, bf16[64,256]{1,0:T(8,128)(2,1)S(1)} %march.1, pred[]{:T(512)S(6)} %eq.6), kind=kLoop, calls=%fused_computation.1 | loop fusion | flops 294912 | bytes 131073 | tf_op jit(solution)/shard_map/jit(_where)/select_n | solution.py:368
  8.5 0.1 collective-permute-start.4
  8.6 2.7 %collective-permute-start.3 = (bf16[128,256]{1,0:T(8,128)(2,1)}, bf16[128,256]{1,0:T(8,128)(2,1)}, u32[]{:S(2)}, u32[]{:S(2)}) collective-permute-start(bf16[128,256]{1,0:T(8,128)(2,1)} %maximum_select_fusion.refs_0_), channel_id=1, source_target_pairs={{0,14},{1,3},{2,12},{3,1},{4,10},{5,7},{6,8},{7,5},{8,6},{9,11},{1... | collective-permute-start | bytes 196616 | tf_op jit(solution)/shard_map/ppermute | solution.py:377
  11.3 1.6 %collective-permute-start.2 = (bf16[128,256]{1,0:T(8,128)(2,1)}, bf16[128,256]{1,0:T(8,128)(2,1)}, u32[]{:S(2)}, u32[]{:S(2)}) collective-permute-start(bf16[128,256]{1,0:T(8,128)(2,1)} %maximum_select_fusion.refs_0_), channel_id=1, source_target_pairs={{0,4},{1,7},{2,6},{3,5},{4,0},{5,3},{6,2},{7,1},{8,12},{9,15},{10,... | collective-permute-start | bytes 196616 | tf_op jit(solution)/shard_map/ppermute | solution.py:377
  12.9 0.0 collective-permute-done.after_ref
  12.9 1.7 %prepare.1 = (bf16[256,1024]{1,0:T(8,128)(2,1)S(1)}, bf16[256,256]{1,0:T(8,128)(2,1)S(1)}, bf16[16,256,256]{2,1,0:T(8,128)(2,1)S(1)}, bf16[64,256]{1,0:T(8,128)(2,1)S(1)}) custom-call(s32[1,16]{1,0:T(1,128)} %shift_hbm.1, s32[1,16,16]{2,1,0:T(8,128)} %sub_hbm.1, s32[1,16]{1,0:T(1,128)} %count_hbm.1, bf16[256,256]{1,0:T(8,128)(2,1)} %bitcast.4, ...), custom_call_target="tpu_custom_call" | custom-call | flops 199999995904 | bytes 2097152 | tf_op jit(solution)/shard_map/prepare/pallas_call | solution.py:292
  14.6 0.5 %collective-permute-done.4.refs_3_ = bf16[128,256]{1,0:T(8,128)(2,1)} collective-permute-done((bf16[128,256]{1,0:T(8,128)(2,1)}, bf16[128,256]{1,0:T(8,128)(2,1)}, u32[]{:S(2)}, u32[]{:S(2)}) %collective-permute-start.4) | collective-permute-done | bytes 65568 | tf_op jit(solution)/shard_map/ppermute | solution.py:377
  15.1 0.9 %collective-permute-done.3.refs_2_ = bf16[128,256]{1,0:T(8,128)(2,1)} collective-permute-done((bf16[128,256]{1,0:T(8,128)(2,1)}, bf16[128,256]{1,0:T(8,128)(2,1)}, u32[]{:S(2)}, u32[]{:S(2)}) %collective-permute-start.3) | collective-permute-done | bytes 65568 | tf_op jit(solution)/shard_map/ppermute | solution.py:377
  16.1 0.9 %collective-permute-done.2.refs_1_ = bf16[128,256]{1,0:T(8,128)(2,1)} collective-permute-done((bf16[128,256]{1,0:T(8,128)(2,1)}, bf16[128,256]{1,0:T(8,128)(2,1)}, u32[]{:S(2)}, u32[]{:S(2)}) %collective-permute-start.2) | collective-permute-done | bytes 65568 | tf_op jit(solution)/shard_map/ppermute | solution.py:377
  17.0 0.9 %pad_maximum_fusion = bf16[448,256]{1,0:T(8,128)(2,1)S(1)} fusion(bf16[64,256]{1,0:T(8,128)(2,1)S(1)} %get-tuple-element.10, bf16[128,256]{1,0:T(8,128)(2,1)} %collective-permute-done.4.refs_3_, bf16[128,256]{1,0:T(8,128)(2,1)} %collective-permute-done.3.refs_2_, bf16[128,256]{1,0:T(8,128)(2,1)} %collective-permute-done.2.refs_1_), kind=kLoop, calls=%fused_computation | loop fusion | flops 917504 | bytes 458752 | tf_op jit(solution)/shard_map/concatenate | solution.py:379
  17.9 0.1 collective-permute-start.5
  18.0 1.5 %collective-permute-done.5 = bf16[448,256]{1,0:T(8,128)(2,1)S(1)} collective-permute-done((bf16[448,256]{1,0:T(8,128)(2,1)S(1)}, bf16[448,256]{1,0:T(8,128)(2,1)S(1)}, u32[]{:S(2)}, u32[]{:S(2)}) %collective-permute-start.5) | collective-permute-done | bytes 229408 | tf_op jit(solution)/shard_map/ppermute | solution.py:357
  19.5 2.7 %tile_sum.1 = f32[256,256]{1,0:T(8,128)} custom-call(bf16[256,1024]{1,0:T(8,128)(2,1)S(1)} %get-tuple-element.9.pick_ref, bf16[128,256]{1,0:T(8,128)(2,1)} %maximum_select_fusion.refs_0_, bf16[128,256]{1,0:T(8,128)(2,1)} %collective-permute-done.2.refs_1_, bf16[128,256]{1,0:T(8,128)(2,1)} %collective-permute-done.3.refs_2_, ...), custom_call_target="tpu_custom_call" | custom-call | tf_op jit(solution)/shard_map/tile_sum/pallas_call | solution.py:337
  (2 shorter events, 0.0 us)
Async XLA Ops:
  2.6 5.2 %collective-permute-start.1 = (bf16[64,256]{1,0:T(8,128)(2,1)S(1)}, bf16[64,256]{1,0:T(8,128)(2,1)S(1)}, u32[]{:S(2)}, u32[]{:S(2)}) collective-permute-start(bf16[64,256]{1,0:T(8,128)(2,1)S(1)} %march.1), channel_id=1, source_target_pairs={{0,1},{1,0},{2,3},{3,2},{4,5},{5,4},{6,7},{7,6},{8,9},{9,8},{10,11... | collective-permute-start | bytes 98312 | tf_op jit(solution)/shard_map/ppermute | solution.py:357
  3.1 9.7 %collective-permute-start = (bf16[64,256]{1,0:T(8,128)(2,1)S(1)}, bf16[64,256]{1,0:T(8,128)(2,1)S(1)}, u32[]{:S(2)}, u32[]{:S(2)}) collective-permute-start(bf16[64,256]{1,0:T(8,128)(2,1)S(1)} %march.1), channel_id=1, source_target_pairs={{0,12},{1,13},{2,14},{3,15},{4,8},{5,9},{6,10},{7,11},{8,4},{9,5},... | collective-permute-start | bytes 98312 | tf_op jit(solution)/shard_map/ppermute | solution.py:357
  8.5 6.7 %collective-permute-start.4 = (bf16[128,256]{1,0:T(8,128)(2,1)}, bf16[128,256]{1,0:T(8,128)(2,1)}, u32[]{:S(2)}, u32[]{:S(2)}) collective-permute-start(bf16[128,256]{1,0:T(8,128)(2,1)} %maximum_select_fusion.refs_0_), channel_id=1, source_target_pairs={{0,8},{1,11},{2,10},{3,9},{4,12},{5,15},{6,14},{7,13},{8,0},{9,3},... | collective-permute-start | bytes 196616 | tf_op jit(solution)/shard_map/ppermute | solution.py:377
  8.6 7.5 %collective-permute-start.3 = (bf16[128,256]{1,0:T(8,128)(2,1)}, bf16[128,256]{1,0:T(8,128)(2,1)}, u32[]{:S(2)}, u32[]{:S(2)}) collective-permute-start(bf16[128,256]{1,0:T(8,128)(2,1)} %maximum_select_fusion.refs_0_), channel_id=1, source_target_pairs={{0,14},{1,3},{2,12},{3,1},{4,10},{5,7},{6,8},{7,5},{8,6},{9,11},{1... | collective-permute-start | bytes 196616 | tf_op jit(solution)/shard_map/ppermute | solution.py:377
  11.3 5.7 %collective-permute-start.2 = (bf16[128,256]{1,0:T(8,128)(2,1)}, bf16[128,256]{1,0:T(8,128)(2,1)}, u32[]{:S(2)}, u32[]{:S(2)}) collective-permute-start(bf16[128,256]{1,0:T(8,128)(2,1)} %maximum_select_fusion.refs_0_), channel_id=1, source_target_pairs={{0,4},{1,7},{2,6},{3,5},{4,0},{5,3},{6,2},{7,1},{8,12},{9,15},{10,... | collective-permute-start | bytes 196616 | tf_op jit(solution)/shard_map/ppermute | solution.py:377
  17.9 1.6 %collective-permute-start.5 = (bf16[448,256]{1,0:T(8,128)(2,1)S(1)}, bf16[448,256]{1,0:T(8,128)(2,1)S(1)}, u32[]{:S(2)}, u32[]{:S(2)}) collective-permute-start(bf16[448,256]{1,0:T(8,128)(2,1)S(1)} %pad_maximum_fusion), channel_id=1, source_target_pairs={{0,1},{1,0},{2,3},{3,2},{4,5},{5,4},{6,7},{7,6},{8,9},{9,8},{10,11... | collective-permute-start | bytes 688136 | tf_op jit(solution)/shard_map/ppermute | solution.py:357

commit v6 on v5

v6 whole, which is shorter than its diff:
```python
import functools
import math

import jax
import jax.numpy as jnp
import numpy as np
from jax import lax
from jax.experimental import pallas as pl
from jax.experimental.pallas import tpu as pltpu
from jax.sharding import PartitionSpec as P

VB = 128
SUB = 16
K_MAX = 16
CAP = 2
GROUP_RADIALS = 512
RADIX = 8
CHUNKS = 4

spread_angle = 6.0
absorb_rate = 0.5


def march_constants(height):
    width = height // RADIX
    index = np.arange(width)
    angle = 2.0 * np.pi / width * (index[:, None] * index[None, :] % width)
    factor = 1.0 / math.sqrt(height)
    cosine, sine = np.cos(angle) * factor, np.sin(angle) * factor
    weights = np.block([[cosine, -sine], [sine, cosine]]).astype(jnp.bfloat16)
    turn = 2.0 * np.pi / height * (np.arange(RADIX)[:, None] * index[None, :])
    level = np.arange(height)
    folded = np.minimum(level, height - level).astype(np.float64)
    theta = -spread_angle * (2.0 * folded / height) ** 2
    theta = theta.reshape(width, RADIX).T
    depth = np.maximum(0.0, (level - 0.9375 * height) / (0.0625 * height))
    absorber = np.exp(-absorb_rate * depth * depth).reshape(RADIX, width)
    waves = np.concatenate([np.cos(turn), np.sin(turn), np.cos(theta), np.sin(theta), absorber], 0)
    waves = np.pad(waves, ((0, -len(waves) % 8), (0, 0)))
    return weights, waves.astype(np.float32)


def cos_sin(angle):
    square = angle * angle
    cosine = jnp.full_like(angle, 1.0 / math.factorial(14) * -1.0)
    for order in (12, 10, 8, 6, 4, 2, 0):
        cosine = cosine * square + (-1.0) ** (order // 2) / math.factorial(order)
    sine = jnp.full_like(angle, 1.0 / math.factorial(13))
    for order in (11, 9, 7, 5, 3, 1):
        sine = sine * square + (-1.0) ** (order // 2) / math.factorial(order)
    return cosine, sine * angle


def turn(real, imag, cosine, sine):
    return real * cosine - imag * sine, real * sine + imag * cosine


def turn_back(real, imag, cosine, sine):
    return real * cosine + imag * sine, imag * cosine - real * sine


def radix_four(parts, sign):
    (r0, i0), (r1, i1), (r2, i2), (r3, i3) = parts
    sr02, si02, dr02, di02 = r0 + r2, i0 + i2, r0 - r2, i0 - i2
    sr13, si13, dr13, di13 = r1 + r3, i1 + i3, r1 - r3, i1 - i3
    plus = (dr02 - di13, di02 + dr13)
    minus = (dr02 + di13, di02 - dr13)
    if sign < 0:
        plus, minus = minus, plus
    return (sr02 + sr13, si02 + si13), plus, (sr02 - sr13, si02 - si13), minus


def radix_eight(parts, sign):
    sums, turned = [], []
    for q in range(4):
        (r, i), (s, t) = parts[q], parts[q + 4]
        sums.append((r + s, i + t))
        turned.append((r - s, i - t))
    half = math.sqrt(0.5)
    (r, i), (s, t), (v, w) = turned[1:]
    if sign < 0:
        turned[1] = ((r + i) * half, (i - r) * half)
        turned[2] = (t, -s)
        turned[3] = ((w - v) * half, (v + w) * -half)
    else:
        turned[1] = ((r - i) * half, (r + i) * half)
        turned[2] = (-t, s)
        turned[3] = ((v + w) * -half, (v - w) * half)
    even, odd = radix_four(sums, sign), radix_four(turned, sign)
    return [part for pair in zip(even, odd) for part in pair]


def march_kernel(
    steps,
    slabs,
    profile_hbm,
    power_hbm,
    slot_hbm,
    phase_hbm,
    wave_hbm,
    field_hbm,
    weight_hbm,
    polar_ref,
    profile_ref,
    power_ref,
    slot_ref,
    phase_ref,
    wave_ref,
    field_ref,
    weight_ref,
    phase_rows,
    screen_ref,
    sems,
    units,
):
    pairs = (
        (profile_hbm, profile_ref),
        (phase_hbm, phase_ref),
        (wave_hbm, wave_ref),
        (field_hbm, field_ref),
        (weight_hbm, weight_ref),
        (power_hbm, power_ref),
        (slot_hbm, slot_ref),
    )
    copies = [
        pltpu.make_async_copy(source, target, sems.at[number])
        for number, (source, target) in enumerate(pairs)
    ]
    for copy in copies:
        copy.start()
    rows, height = field_ref.shape[1:]
    width = height // RADIX
    chunks = rows // SUB
    slab = lax.axis_index("range")
    tile = lax.axis_index("radial")
    total = slabs * steps
    for copy in copies[:3]:
        copy.wait()
    for place in range(total):
        phase_rows[place : place + 1, :] = phase_ref[
            pl.ds(profile_ref[place // steps, place % steps], 1), :
        ]
    for q in range(RADIX):
        columns = slice(q * width, (q + 1) * width)
        cosine, sine = cos_sin(phase_rows[:, columns])
        absorber = wave_ref[4 * RADIX + q : 4 * RADIX + q + 1, :]
        damp = jnp.where(lax.broadcasted_iota(jnp.int32, cosine.shape, 0) == 0, 1.0, absorber)
        for part, value in enumerate((cosine * damp, sine * damp)):
            for place in range(total):
                screen_ref[place, part, :, columns] = jnp.broadcast_to(
                    value[place : place + 1], (8, width)
                )
    for copy in copies[3:]:
        copy.wait()
    gain = power_ref[slot_ref[tile * rows // GROUP_RADIALS]]

    def run(*products):
        for unit in range(2):
            pltpu.matmul_push_rhs(weight_ref[...], 0, unit)
            pltpu.matmul_acc_lhs(
                products[chunks * unit], jnp.zeros((RADIX * SUB, 2 * width), jnp.bfloat16), load_staged_rhs=0
            )
            pltpu.matmul_pop(products[chunks * unit])

        def wave(kind, j):
            return wave_ref[kind * RADIX + j : kind * RADIX + j + 1, :]

        def entering(chunk):
            spot = slice(chunk * SUB, (chunk + 1) * SUB)
            return [
                tuple(
                    field_ref[part, spot, q * width : (q + 1) * width].astype(jnp.float32)
                    for part in range(2)
                )
                for q in range(RADIX)
            ]

        def forward(place, chunk, field):
            parts, lines = [], []
            for q in range(RADIX):
                columns = slice(q * width, (q + 1) * width)
                screen = [screen_ref[place, part, :, columns] for part in range(2)]
                screen = [jnp.concatenate([value] * (SUB // 8), 0) for value in screen]
                parts.append(turn(*field[q], *screen))
            for j, (real, imag) in enumerate(radix_eight(parts, -1)):
                if j:
                    real, imag = turn_back(real, imag, wave(0, j), wave(1, j))
                lines.append(
                    jnp.concatenate([real.astype(jnp.bfloat16), imag.astype(jnp.bfloat16)], 1)
                )
            pltpu.matmul_acc_lhs(products[chunk], jnp.concatenate(lines, 0))

        def middle(chunk):
            spectrum = pltpu.matmul_pop(products[chunk])
            lines = []
            for j in range(RADIX):
                spot = slice(j * SUB, (j + 1) * SUB)
                real, imag = spectrum[spot, :width], spectrum[spot, width:]
                real, imag = turn(real, imag, wave(2, j), wave(3, j))
                lines.append(
                    jnp.concatenate([imag.astype(jnp.bfloat16), real.astype(jnp.bfloat16)], 1)
                )
            pltpu.matmul_acc_lhs(products[chunks + chunk], jnp.concatenate(lines, 0))

        def backward(chunk, lowest):
            back = pltpu.matmul_pop(products[chunks + chunk])
            parts = []
            for j in range(RADIX):
                spot = slice(j * SUB, (j + 1) * SUB)
                real, imag = back[spot, width:], back[spot, :width]
                if j:
                    real, imag = turn(real, imag, wave(0, j), wave(1, j))
                parts.append((real, imag))
            if lowest:
                return [tuple(sum(part[1:], part[0]) for part in zip(*parts))]
            return radix_eight(parts, 1)

        def power_rows(step, chunk, real, imag):
            power = gain * (real * real + imag * imag)
            spot = slice(chunk * SUB, (chunk + 1) * SUB)
            polar_ref[spot, step * VB : (step + 1) * VB] = power.astype(jnp.bfloat16)

        def one_slab(number, last):
            events = []
            for step in range(steps):
                for chunk in range(chunks):
                    start = chunks * step + chunk
                    events.append((start, "forward", step, chunk))
                    events.append((start + 1.5, "middle", step, chunk))
            for chunk in range(chunks):
                events.append((chunks * steps + chunk, "leave", steps, chunk))
            for _, kind, step, chunk in sorted(events):
                if kind == "middle":
                    middle(chunk)
                    continue
                if step == 0:
                    forward(number * steps, chunk, entering(chunk))
                    continue
                field = backward(chunk, kind == "leave" and last)
                if last:
                    power_rows(step - 1, chunk, *field[0])
                if kind == "forward":
                    forward(number * steps + step, chunk, field)
                elif not last:
                    spot = slice(chunk * SUB, (chunk + 1) * SUB)
                    for q in range(RADIX):
                        for part in range(2):
                            field_ref[part, spot, q * width : (q + 1) * width] = field[q][
                                part
                            ].astype(jnp.bfloat16)

        def whole_slab(number, carry):
            one_slab(number, False)
            return carry

        lax.fori_loop(0, slab, whole_slab, 0)
        one_slab(slab, True)

    pl.run_scoped(run, *units)


def in_hbm(operands):
    return [pltpu.with_memory_space_constraint(value, pltpu.HBM) for value in operands]


def march(field, phase_table, profile_index, group_power, group_slot, units):
    rows, height = field.shape[1:]
    slabs, steps = profile_index.shape
    weights, waves = march_constants(height)
    operands = [profile_index, group_power, group_slot, phase_table, waves, field, weights]
    places = [pltpu.SMEM] * 3 + [pltpu.VMEM] * 4
    return pl.pallas_call(
        functools.partial(march_kernel, steps, slabs, units=units),
        out_shape=jax.ShapeDtypeStruct((rows, steps * VB), jnp.bfloat16),
        in_specs=[pl.BlockSpec(memory_space=pltpu.HBM)] * len(operands),
        out_specs=pl.BlockSpec(memory_space=pltpu.VMEM),
        scratch_shapes=[place(o.shape, o.dtype) for place, o in zip(places, operands)]
        + [
            pltpu.VMEM((-(-slabs * steps // 8) * 8, height), jnp.float32),
            pltpu.VMEM((slabs * steps, 2, 8, height), jnp.float32),
            pltpu.SemaphoreType.DMA((len(operands),)),
        ],
        compiler_params=pltpu.CompilerParams(vmem_limit_bytes=24 * 1024 * 1024),
        name="march",
    )(*in_hbm(operands))


def prepare_kernel(
    local_rows,
    shift_hbm,
    sub_hbm,
    count_hbm,
    row_hbm,
    col_hbm,
    after_ref,
    pick_ref,
    turned_ref,
    col_ref,
    passed_ref,
    shift_ref,
    sub_ref,
    count_ref,
    row_ref,
    sems,
):
    pairs = (
        (shift_hbm, shift_ref),
        (sub_hbm, sub_ref),
        (count_hbm, count_ref),
        (row_hbm, row_ref),
        (col_hbm, col_ref),
    )
    copies = [
        pltpu.make_async_copy(source, target, sems.at[number])
        for number, (source, target) in enumerate(pairs)
    ]
    for copy in copies:
        copy.start()
    tile = lax.axis_index("radial")
    devices = lax.axis_size("radial")
    for copy in copies[:4]:
        copy.wait()
    shape = (SUB, pick_ref.shape[1])
    offset = lax.broadcasted_iota(jnp.int32, shape, 1) - lax.broadcasted_iota(jnp.int32, shape, 0)
    for slot in range(K_MAX):
        source = lax.rem(tile + shift_ref[0, tile] + slot // CAP, devices)
        start = source * local_rows + sub_ref[0, tile, slot] * SUB
        start = jnp.where(slot < count_ref[0, tile], start, -2 * pick_ref.shape[1])
        pick_ref[slot * SUB : (slot + 1) * SUB, :] = jnp.where(offset == start, 1.0, 0.0).astype(
            jnp.bfloat16
        )
    turned_ref[...] = row_ref[...].T
    passed_ref[...] = after_ref[...]
    copies[4].wait()


def prepare(source_shift, slot_sub, tile_count, row_weights, col_weights, local_rows, after):
    pixels = row_weights.shape[-1]
    radials = local_rows * lax.axis_size("radial")
    rows_flat = row_weights.reshape(K_MAX * SUB, pixels)
    cols_flat = col_weights.reshape(K_MAX, col_weights.shape[-2], pixels)
    operands = [source_shift, slot_sub, tile_count, rows_flat]
    places = [pltpu.SMEM] * 3 + [pltpu.VMEM]
    return pl.pallas_call(
        functools.partial(prepare_kernel, local_rows),
        out_shape=[
            jax.ShapeDtypeStruct((K_MAX * SUB, radials), jnp.bfloat16),
            jax.ShapeDtypeStruct((pixels, K_MAX * SUB), jnp.bfloat16),
            jax.ShapeDtypeStruct(cols_flat.shape, jnp.bfloat16),
            jax.ShapeDtypeStruct(after.shape, after.dtype),
        ],
        in_specs=[pl.BlockSpec(memory_space=pltpu.HBM)] * 5
        + [pl.BlockSpec(memory_space=pltpu.VMEM)],
        out_specs=[pl.BlockSpec(memory_space=pltpu.VMEM)] * 4,
        scratch_shapes=[place(o.shape, o.dtype) for place, o in zip(places, operands)]
        + [pltpu.SemaphoreType.DMA((5,))],
        compiler_params=pltpu.CompilerParams(vmem_limit_bytes=24 * 1024 * 1024),
        cost_estimate=pl.CostEstimate(
            flops=2_000_000_000, bytes_accessed=2 * cols_flat.size, transcendentals=0
        ),
        name="prepare",
    )(*in_hbm(operands + [cols_flat]), after)


def tile_kernel(places, pick_ref, *refs):
    part_refs = refs[: len(places)]
    row_ref, col_ref, out_ref, polar_ref, mixed_ref = refs[len(places) :]
    chip = lax.axis_index("radial") // 2
    core = lax.axis_index("radial") % 2
    for (even, odd), part_ref in zip(places, part_refs):
        size = part_ref.shape[0]
        start = jnp.where(core == 0, chip ^ even, chip ^ odd) * size
        if size == polar_ref.shape[0]:
            start = 0
        polar_ref[pl.ds(start, size), :] = part_ref[...]
    blocks = jnp.dot(pick_ref[...], polar_ref[...], preferred_element_type=jnp.float32)
    blocks = blocks.astype(jnp.bfloat16)
    for slot in range(K_MAX):
        block = blocks[slot * SUB : (slot + 1) * SUB]
        mixed = jnp.dot(block, col_ref[slot], preferred_element_type=jnp.float32)
        mixed_ref[slot * SUB : (slot + 1) * SUB, :] = mixed.astype(jnp.bfloat16)
    out_ref[...] = jnp.dot(row_ref[...], mixed_ref[...], preferred_element_type=jnp.float32)


def tile_sum(pick, parts, places, row_weights, col_weights):
    pixels = row_weights.shape[0]
    channels = col_weights.shape[-2]
    vmem = pl.BlockSpec(memory_space=pltpu.VMEM)
    return pl.pallas_call(
        functools.partial(tile_kernel, places),
        out_shape=jax.ShapeDtypeStruct((pixels, pixels), jnp.float32),
        in_specs=[vmem] * (len(parts) + 3),
        out_specs=vmem,
        scratch_shapes=[
            pltpu.VMEM((pick.shape[1], channels), jnp.bfloat16),
            pltpu.VMEM((K_MAX * SUB, pixels), jnp.bfloat16),
        ],
        compiler_params=pltpu.CompilerParams(vmem_limit_bytes=24 * 1024 * 1024),
        name="tile_sum",
    )(
        pick,
        *parts,
        row_weights,
        col_weights,
    )


def swap(value, distance, devices):
    return lax.ppermute(value, "radial", [(i, i ^ distance) for i in range(devices)])


def gather_parts(polar, devices, prepared):
    if devices != 16:
        whole = lax.all_gather(polar, "radial", axis=0, tiled=True)
        return [whole], [(0, 0)], prepared(polar)[:3]
    core = lax.axis_index("radial") % 2
    size = 2 * polar.shape[0]

    def in_order(own, other):
        return jnp.where(
            core == 0, jnp.concatenate([own, other], 0), jnp.concatenate([other, own], 0)
        )

    first = swap(polar, 2, devices)
    pair = in_order(polar, swap(polar, 1, devices))
    held = []
    for even, odd in ((2, 3), (4, 5), (6, 7)):
        routes = [(i, i ^ (2 * (odd if i % 2 else even))) for i in range(devices)]
        held.append(lax.ppermute(pair, "radial", routes))
    *ready, first = prepared(first)
    other = swap(jnp.concatenate(held + [first], 0), 1, devices)
    parts = [pair] + held + [other[i * size : (i + 1) * size] for i in range(3)]
    parts.append(in_order(first, other[3 * size :]))
    places = [(0, 0), (2, 3), (4, 5), (6, 7), (3, 2), (5, 4), (7, 6), (1, 1)]
    return parts, places, ready


def per_device(
    units,
    field_start,
    phase_table,
    profile_index,
    group_power,
    group_slot,
    source_shift,
    slot_sub,
    tile_count,
    row_weights,
    col_weights,
):
    devices = lax.axis_size("radial")
    polar = march(field_start, phase_table, profile_index, group_power, group_slot, units)
    prepared = functools.partial(
        prepare, source_shift, slot_sub, tile_count, row_weights, col_weights, polar.shape[0]
    )
    parts, places, ready = gather_parts(polar, devices, prepared)
    pick, turned, cols = ready
    tile_value = tile_sum(pick, parts, places, turned, cols)
    return tile_value.reshape((1, 1) + tile_value.shape)


def solution(mesh):
    with jax.sharding.use_abstract_mesh(mesh.abstract_mesh):
        units = [
            pltpu.ACC(number // CHUNKS)((RADIX * SUB, 256), jnp.float32)
            for number in range(2 * CHUNKS)
        ]
    return jax.shard_map(
        functools.partial(per_device, units),
        mesh=mesh,
        in_specs=(
            P(None, "radial", None),
            P(),
            P(),
            P(),
            P(),
            P("range", None),
            P("range", None, None),
            P("range", None),
            P("range", "radial", None, None, None),
            P("range", "radial", None, None, None),
        ),
        out_specs=P("range", "radial", None, None),
        check_vma=False,
    )
```

time: 22.6 us -> 18.8 us (0.83); the launches traced: 22.2 us -> 18.7 us
  starting transfers between devices: 9.69 us -> 7.8 us
  other arithmetic: 1.58 us -> 0.05 us
  Pallas kernels: 7.01 us -> 5.65 us
  waiting for transfers between devices: 3.83 us -> 5.13 us
    ppermute x3, starting transfers between devices: 5.27 us -> 3.35 us  [swap(): lax.ppermute(value, 'radial', [(i, i ^ distance) for i in range(devices)])]
    ppermute x3, waiting for transfers between devices: 2.35 us -> 3.83 us  [gather_parts(): held.append(lax.ppermute(pair, 'radial', routes))]
    pallas_call x1, Pallas kernels: 2.68 us -> 1.75 us  [tile_sum(): pl.pallas_call(functools.partial(tile_kernel, places), out_shape=jax.Shap...]
    concatenate x1, other arithmetic: 0.92 us -> 0.02 us  [gather_parts(): other = swap(jnp.concatenate(held + [first], 0), 1, devices)]
    select_n x1, other arithmetic: 0.63 us -> 0.01 us  [in_order(): jnp.where(core == 0, jnp.concatenate([own, other], 0), jnp.concatenate([o...]
    pallas_call x1, Pallas kernels: 2.62 us -> 2.18 us  [march(): pl.pallas_call(functools.partial(march_kernel, steps, slabs, units=units)...]
  transfers between devices with their start and end apart: 6 -> 6, of which waited for: 4 -> 3; matrix products, arithmetic and copies ran while one was open for 3% -> 0% of each run, Pallas kernels for 8% -> 9%
where the time goes in v6:
time: 18.8 us; the launch traced here: 18.7 us
  starting transfers between devices  7.8 us (41%)
  Pallas kernels  5.65 us (30%)
  waiting for transfers between devices  5.13 us (27%)
    ppermute x3, starting transfers between devices, gather_parts(): held.append(lax.ppermute(pair, 'radial', routes))  4.45 us
    ppermute x3, waiting for transfers between devices, gather_parts(): held.append(lax.ppermute(pair, 'radial', routes))  3.83 us
    ppermute x3, starting transfers between devices, swap(): lax.ppermute(value, 'radial', [(i, i ^ distance) for i in range(devices)])  3.35 us
    pallas_call x1, Pallas kernels, march(): pl.pallas_call(functools.partial(march_kernel, steps, slabs, units=units)...  2.18 us
    pallas_call x1, Pallas kernels, tile_sum(): pl.pallas_call(functools.partial(tile_kernel, places), out_shape=jax.Shap...  1.75 us
    pallas_call x1, Pallas kernels, prepare(): pl.pallas_call(functools.partial(prepare_kernel, local_rows), out_shape=[...  1.71 us
    ppermute x3, waiting for transfers between devices, swap(): lax.ppermute(value, 'radial', [(i, i ^ distance) for i in range(devices)])  1.29 us
  transfers between devices with their start and end apart: 6, of which 3 were waited for; matrix products, arithmetic and copies ran while one was open for 0% of the time, Pallas kernels for 9%

profile of v6, /device:TPU:0, one launch (start us, length us, event | category | flops | bytes accessed | tf_op | source)
XLA Modules:
  0.0 18.7 jit_solution(4408113850876457321)
XLA Ops:
  0.0 2.2 %march.1 = bf16[64,256]{1,0:T(8,128)(2,1)S(1)} custom-call(s32[2,2]{1,0:T(2,128)} %profile_hbm.1, f32[2]{0:T(128)} %power_hbm.1, s32[2]{0:T(128)} %slot_hbm.1, f32[16,1024]{1,0:T(8,128)} %phase_hbm.1, f32[40,128]{1,0:T(8,128)} %constant.22.clone.wave_hbm, bf16[2,64,1024]{2,1,0:T(8,128)(2,1)} %field_hbm.1, bf16[256,256]{1,0:T(8,128)(2,1)} %constant.23.clone.weight_hbm), custom_call_target="tpu_custom_call" | custom-call | tf_op jit(solution)/shard_map/march/pallas_call | solution.py:272
  2.2 0.5 %collective-permute-start.1 = (bf16[64,256]{1,0:T(8,128)(2,1)S(1)}, bf16[64,256]{1,0:T(8,128)(2,1)S(1)}, u32[]{:S(2)}, u32[]{:S(2)}) collective-permute-start(bf16[64,256]{1,0:T(8,128)(2,1)S(1)} %march.1), channel_id=1, source_target_pairs={{0,1},{1,0},{2,3},{3,2},{4,5},{5,4},{6,7},{7,6},{8,9},{9,8},{10,11... | collective-permute-start | bytes 98312 | tf_op jit(solution)/shard_map/ppermute | solution.py:409
  2.7 2.6 %collective-permute-start = (bf16[64,256]{1,0:T(8,128)(2,1)S(1)}, bf16[64,256]{1,0:T(8,128)(2,1)S(1)}, u32[]{:S(2)}, u32[]{:S(2)}) collective-permute-start(bf16[64,256]{1,0:T(8,128)(2,1)S(1)} %march.1), channel_id=1, source_target_pairs={{0,2},{1,3},{2,0},{3,1},{4,6},{5,7},{6,4},{7,5},{8,10},{9,11},{10,... | collective-permute-start | bytes 98312 | tf_op jit(solution)/shard_map/ppermute | solution.py:409
  5.3 0.0 collective-permute-done.1
  5.3 3.7 %collective-permute-start.4 = (bf16[128,256]{1,0:T(8,128)(2,1)S(1)}, bf16[128,256]{1,0:T(8,128)(2,1)S(1)}, u32[]{:S(2)}, u32[]{:S(2)}) collective-permute-start(bf16[128,256]{1,0:T(8,128)(2,1)S(1)} %maximum_select_fusion.refs_0_), channel_id=1, source_target_pairs={{0,12},{1,15},{2,14},{3,13},{4,8},{5,11},{6,10},{7,9},{8,4},{9,7},... | collective-permute-start | bytes 196616 | tf_op jit(solution)/shard_map/ppermute | solution.py:429
  9.0 0.0 collective-permute-start.3
  9.0 0.8 %collective-permute-start.2 = (bf16[128,256]{1,0:T(8,128)(2,1)S(1)}, bf16[128,256]{1,0:T(8,128)(2,1)S(1)}, u32[]{:S(2)}, u32[]{:S(2)}) collective-permute-start(bf16[128,256]{1,0:T(8,128)(2,1)S(1)} %maximum_select_fusion.refs_0_), channel_id=1, source_target_pairs={{0,4},{1,7},{2,6},{3,5},{4,0},{5,3},{6,2},{7,1},{8,12},{9,15},{10,... | collective-permute-start | bytes 196616 | tf_op jit(solution)/shard_map/ppermute | solution.py:429
  9.7 0.0 collective-permute-done.after_ref
  9.8 1.7 %prepare.1 = (bf16[256,1024]{1,0:T(8,128)(2,1)S(1)}, bf16[256,256]{1,0:T(8,128)(2,1)S(1)}, bf16[16,256,256]{2,1,0:T(8,128)(2,1)S(1)}, bf16[64,256]{1,0:T(8,128)(2,1)S(1)}) custom-call(s32[1,16]{1,0:T(1,128)} %shift_hbm.1, s32[1,16,16]{2,1,0:T(8,128)} %sub_hbm.1, s32[1,16]{1,0:T(1,128)} %count_hbm.1, bf16[256,256]{1,0:T(8,128)(2,1)} %bitcast.4, ...), custom_call_target="tpu_custom_call" | custom-call | flops 2000000000 | bytes 2097152 | tf_op jit(solution)/shard_map/prepare/pallas_call | solution.py:344
  11.5 0.5 %collective-permute-done.4.refs_3_ = bf16[128,256]{1,0:T(8,128)(2,1)S(1)} collective-permute-done((bf16[128,256]{1,0:T(8,128)(2,1)S(1)}, bf16[128,256]{1,0:T(8,128)(2,1)S(1)}, u32[]{:S(2)}, u32[]{:S(2)}) %collective-permute-start.4) | collective-permute-done | bytes 65568 | tf_op jit(solution)/shard_map/ppermute | solution.py:429
  12.0 3.3 %collective-permute-done.3.refs_2_ = bf16[128,256]{1,0:T(8,128)(2,1)S(1)} collective-permute-done((bf16[128,256]{1,0:T(8,128)(2,1)S(1)}, bf16[128,256]{1,0:T(8,128)(2,1)S(1)}, u32[]{:S(2)}, u32[]{:S(2)}) %collective-permute-start.3) | collective-permute-done | bytes 65568 | tf_op jit(solution)/shard_map/ppermute | solution.py:429
  15.3 0.0 collective-permute-done.2.refs_1_
  15.3 0.3 %collective-permute-start.5 = (bf16[448,256]{1,0:T(8,128)(2,1)S(1)}, bf16[448,256]{1,0:T(8,128)(2,1)S(1)}, u32[]{:S(2)}, u32[]{:S(2)}) collective-permute-start(bf16[448,256]{1,0:T(8,128)(2,1)S(1)} %pad_maximum_fusion), channel_id=1, source_target_pairs={{0,1},{1,0},{2,3},{3,2},{4,5},{5,4},{6,7},{7,6},{8,9},{9,8},{10,11... | collective-permute-start | bytes 688136 | tf_op jit(solution)/shard_map/ppermute | solution.py:409
  15.6 1.3 %collective-permute-done.5 = bf16[448,256]{1,0:T(8,128)(2,1)S(1)} collective-permute-done((bf16[448,256]{1,0:T(8,128)(2,1)S(1)}, bf16[448,256]{1,0:T(8,128)(2,1)S(1)}, u32[]{:S(2)}, u32[]{:S(2)}) %collective-permute-start.5) | collective-permute-done | bytes 229408 | tf_op jit(solution)/shard_map/ppermute | solution.py:409
  16.9 1.8 %tile_sum.1 = f32[256,256]{1,0:T(8,128)} custom-call(bf16[256,1024]{1,0:T(8,128)(2,1)S(1)} %get-tuple-element.9.pick_ref, bf16[128,256]{1,0:T(8,128)(2,1)S(1)} %maximum_select_fusion.refs_0_, bf16[128,256]{1,0:T(8,128)(2,1)S(1)} %collective-permute-done.2.refs_1_, bf16[128,256]{1,0:T(8,128)(2,1)S(1)} %collective-permute-done.3.refs_2_, ...), custom_call_target="tpu_custom_call" | custom-call | tf_op jit(solution)/shard_map/tile_sum/pallas_call | solution.py:389
  (4 shorter events, 0.1 us)
Async XLA Ops:
  2.2 3.1 %collective-permute-start.1 = (bf16[64,256]{1,0:T(8,128)(2,1)S(1)}, bf16[64,256]{1,0:T(8,128)(2,1)S(1)}, u32[]{:S(2)}, u32[]{:S(2)}) collective-permute-start(bf16[64,256]{1,0:T(8,128)(2,1)S(1)} %march.1), channel_id=1, source_target_pairs={{0,1},{1,0},{2,3},{3,2},{4,5},{5,4},{6,7},{7,6},{8,9},{9,8},{10,11... | collective-permute-start | bytes 98312 | tf_op jit(solution)/shard_map/ppermute | solution.py:409
  2.7 7.0 %collective-permute-start = (bf16[64,256]{1,0:T(8,128)(2,1)S(1)}, bf16[64,256]{1,0:T(8,128)(2,1)S(1)}, u32[]{:S(2)}, u32[]{:S(2)}) collective-permute-start(bf16[64,256]{1,0:T(8,128)(2,1)S(1)} %march.1), channel_id=1, source_target_pairs={{0,2},{1,3},{2,0},{3,1},{4,6},{5,7},{6,4},{7,5},{8,10},{9,11},{10,... | collective-permute-start | bytes 98312 | tf_op jit(solution)/shard_map/ppermute | solution.py:409
  5.3 6.7 %collective-permute-start.4 = (bf16[128,256]{1,0:T(8,128)(2,1)S(1)}, bf16[128,256]{1,0:T(8,128)(2,1)S(1)}, u32[]{:S(2)}, u32[]{:S(2)}) collective-permute-start(bf16[128,256]{1,0:T(8,128)(2,1)S(1)} %maximum_select_fusion.refs_0_), channel_id=1, source_target_pairs={{0,12},{1,15},{2,14},{3,13},{4,8},{5,11},{6,10},{7,9},{8,4},{9,7},... | collective-permute-start | bytes 196616 | tf_op jit(solution)/shard_map/ppermute | solution.py:429
  9.0 6.3 %collective-permute-start.3 = (bf16[128,256]{1,0:T(8,128)(2,1)S(1)}, bf16[128,256]{1,0:T(8,128)(2,1)S(1)}, u32[]{:S(2)}, u32[]{:S(2)}) collective-permute-start(bf16[128,256]{1,0:T(8,128)(2,1)S(1)} %maximum_select_fusion.refs_0_), channel_id=1, source_target_pairs={{0,8},{1,11},{2,10},{3,9},{4,12},{5,15},{6,14},{7,13},{8,0},{9,3},... | collective-permute-start | bytes 196616 | tf_op jit(solution)/shard_map/ppermute | solution.py:429
  9.0 6.3 %collective-permute-start.2 = (bf16[128,256]{1,0:T(8,128)(2,1)S(1)}, bf16[128,256]{1,0:T(8,128)(2,1)S(1)}, u32[]{:S(2)}, u32[]{:S(2)}) collective-permute-start(bf16[128,256]{1,0:T(8,128)(2,1)S(1)} %maximum_select_fusion.refs_0_), channel_id=1, source_target_pairs={{0,4},{1,7},{2,6},{3,5},{4,0},{5,3},{6,2},{7,1},{8,12},{9,15},{10,... | collective-permute-start | bytes 196616 | tf_op jit(solution)/shard_map/ppermute | solution.py:429
  15.3 1.6 %collective-permute-start.5 = (bf16[448,256]{1,0:T(8,128)(2,1)S(1)}, bf16[448,256]{1,0:T(8,128)(2,1)S(1)}, u32[]{:S(2)}, u32[]{:S(2)}) collective-permute-start(bf16[448,256]{1,0:T(8,128)(2,1)S(1)} %pad_maximum_fusion), channel_id=1, source_target_pairs={{0,1},{1,0},{2,3},{3,2},{4,5},{5,4},{6,7},{7,6},{8,9},{9,8},{10,11... | collective-permute-start | bytes 688136 | tf_op jit(solution)/shard_map/ppermute | solution.py:409

commit v7 on v6

--- a/solution.py
+++ b/solution.py
@@ -428,9 +428,11 @@
         routes = [(i, i ^ (2 * (odd if i % 2 else even))) for i in range(devices)]
         held.append(lax.ppermute(pair, "radial", routes))
     *ready, first = prepared(first)
-    other = swap(jnp.concatenate(held + [first], 0), 1, devices)
-    parts = [pair] + held + [other[i * size : (i + 1) * size] for i in range(3)]
-    parts.append(in_order(first, other[3 * size :]))
+    near, far, last = held
+    early = swap(jnp.concatenate([last, first], 0), 1, devices)
+    late = swap(jnp.concatenate([near, far], 0), 1, devices)
+    parts = [pair] + held + [late[:size], late[size:], early[:size]]
+    parts.append(in_order(first, early[size:]))
     places = [(0, 0), (2, 3), (4, 5), (6, 7), (3, 2), (5, 4), (7, 6), (1, 1)]
     return parts, places, ready
 

time: 18.8 us -> 18.7 us (level)
  waiting for transfers between devices: 5.13 us -> 4.58 us
  starting transfers between devices: 7.8 us -> 8.16 us
    ppermute x3, waiting for transfers between devices: 3.83 us -> 3.47 us  [gather_parts(): held.append(lax.ppermute(pair, 'radial', routes))]
    ppermute x3 -> x4, starting transfers between devices: 3.35 us -> 3.71 us  [swap(): lax.ppermute(value, 'radial', [(i, i ^ distance) for i in range(devices)])]
    ppermute x3 -> x4, waiting for transfers between devices: 1.29 us -> 1.11 us  [swap(): lax.ppermute(value, 'radial', [(i, i ^ distance) for i in range(devices)])]
  transfers between devices with their start and end apart: 6 -> 7, of which waited for: 3 -> 3; matrix products, arithmetic and copies ran while one was open for 0% -> 0% of each run, Pallas kernels for 9% -> 9%
where the time goes in v7:
time: 18.7 us; the launch traced here: 18.5 us
  starting transfers between devices  8.16 us (44%)
  Pallas kernels  5.65 us (30%)
  waiting for transfers between devices  4.58 us (24%)
    ppermute x3, starting transfers between devices, gather_parts(): held.append(lax.ppermute(pair, 'radial', routes))  4.45 us
    ppermute x4, starting transfers between devices, swap(): lax.ppermute(value, 'radial', [(i, i ^ distance) for i in range(devices)])  3.71 us
    ppermute x3, waiting for transfers between devices, gather_parts(): held.append(lax.ppermute(pair, 'radial', routes))  3.47 us
    pallas_call x1, Pallas kernels, march(): pl.pallas_call(functools.partial(march_kernel, steps, slabs, units=units)...  2.18 us
    pallas_call x1, Pallas kernels, tile_sum(): pl.pallas_call(functools.partial(tile_kernel, places), out_shape=jax.Shap...  1.75 us
    pallas_call x1, Pallas kernels, prepare(): pl.pallas_call(functools.partial(prepare_kernel, local_rows), out_shape=[...  1.71 us
    ppermute x4, waiting for transfers between devices, swap(): lax.ppermute(value, 'radial', [(i, i ^ distance) for i in range(devices)])  1.11 us
  transfers between devices with their start and end apart: 7, of which 3 were waited for; matrix products, arithmetic and copies ran while one was open for 0% of the time, Pallas kernels for 9%

profile of v7, /device:TPU:0, one launch (start us, length us, event | category | flops | bytes accessed | tf_op | source)
XLA Modules:
  0.0 18.5 jit_solution(6671281961500767016)
XLA Ops:
  0.0 2.2 %march.1 = bf16[64,256]{1,0:T(8,128)(2,1)S(1)} custom-call(s32[2,2]{1,0:T(2,128)} %profile_hbm.1, f32[2]{0:T(128)} %power_hbm.1, s32[2]{0:T(128)} %slot_hbm.1, f32[16,1024]{1,0:T(8,128)} %phase_hbm.1, f32[40,128]{1,0:T(8,128)} %constant.22.clone.wave_hbm, bf16[2,64,1024]{2,1,0:T(8,128)(2,1)} %field_hbm.1, bf16[256,256]{1,0:T(8,128)(2,1)} %constant.23.clone.weight_hbm), custom_call_target="tpu_custom_call" | custom-call | tf_op jit(solution)/shard_map/march/pallas_call | solution.py:272
  2.2 0.5 %collective-permute-start.1 = (bf16[64,256]{1,0:T(8,128)(2,1)S(1)}, bf16[64,256]{1,0:T(8,128)(2,1)S(1)}, u32[]{:S(2)}, u32[]{:S(2)}) collective-permute-start(bf16[64,256]{1,0:T(8,128)(2,1)S(1)} %march.1), channel_id=1, source_target_pairs={{0,1},{1,0},{2,3},{3,2},{4,5},{5,4},{6,7},{7,6},{8,9},{9,8},{10,11... | collective-permute-start | bytes 98312 | tf_op jit(solution)/shard_map/ppermute | solution.py:409
  2.7 2.6 %collective-permute-start = (bf16[64,256]{1,0:T(8,128)(2,1)S(1)}, bf16[64,256]{1,0:T(8,128)(2,1)S(1)}, u32[]{:S(2)}, u32[]{:S(2)}) collective-permute-start(bf16[64,256]{1,0:T(8,128)(2,1)S(1)} %march.1), channel_id=1, source_target_pairs={{0,2},{1,3},{2,0},{3,1},{4,6},{5,7},{6,4},{7,5},{8,10},{9,11},{10,... | collective-permute-start | bytes 98312 | tf_op jit(solution)/shard_map/ppermute | solution.py:409
  5.3 0.0 collective-permute-done.1
  5.3 3.7 %collective-permute-start.4 = (bf16[128,256]{1,0:T(8,128)(2,1)S(1)}, bf16[128,256]{1,0:T(8,128)(2,1)S(1)}, u32[]{:S(2)}, u32[]{:S(2)}) collective-permute-start(bf16[128,256]{1,0:T(8,128)(2,1)S(1)} %maximum_select_fusion.refs_0_), channel_id=1, source_target_pairs={{0,12},{1,15},{2,14},{3,13},{4,8},{5,11},{6,10},{7,9},{8,4},{9,7},... | collective-permute-start | bytes 196616 | tf_op jit(solution)/shard_map/ppermute | solution.py:429
  9.0 0.0 collective-permute-start.3
  9.0 0.8 %collective-permute-start.2 = (bf16[128,256]{1,0:T(8,128)(2,1)S(1)}, bf16[128,256]{1,0:T(8,128)(2,1)S(1)}, u32[]{:S(2)}, u32[]{:S(2)}) collective-permute-start(bf16[128,256]{1,0:T(8,128)(2,1)S(1)} %maximum_select_fusion.refs_0_), channel_id=1, source_target_pairs={{0,4},{1,7},{2,6},{3,5},{4,0},{5,3},{6,2},{7,1},{8,12},{9,15},{10,... | collective-permute-start | bytes 196616 | tf_op jit(solution)/shard_map/ppermute | solution.py:429
  9.7 0.0 collective-permute-done.after_ref
  9.8 1.7 %prepare.1 = (bf16[256,1024]{1,0:T(8,128)(2,1)S(1)}, bf16[256,256]{1,0:T(8,128)(2,1)S(1)}, bf16[16,256,256]{2,1,0:T(8,128)(2,1)S(1)}, bf16[64,256]{1,0:T(8,128)(2,1)S(1)}) custom-call(s32[1,16]{1,0:T(1,128)} %shift_hbm.1, s32[1,16,16]{2,1,0:T(8,128)} %sub_hbm.1, s32[1,16]{1,0:T(1,128)} %count_hbm.1, bf16[256,256]{1,0:T(8,128)(2,1)} %bitcast.4, ...), custom_call_target="tpu_custom_call" | custom-call | flops 2000000000 | bytes 2097152 | tf_op jit(solution)/shard_map/prepare/pallas_call | solution.py:344
  11.5 0.5 %collective-permute-done.4.refs_3_ = bf16[128,256]{1,0:T(8,128)(2,1)S(1)} collective-permute-done((bf16[128,256]{1,0:T(8,128)(2,1)S(1)}, bf16[128,256]{1,0:T(8,128)(2,1)S(1)}, u32[]{:S(2)}, u32[]{:S(2)}) %collective-permute-start.4) | collective-permute-done | bytes 65568 | tf_op jit(solution)/shard_map/ppermute | solution.py:429
  12.0 0.4 %collective-permute-start.6 = (bf16[192,256]{1,0:T(8,128)(2,1)S(1)}, bf16[192,256]{1,0:T(8,128)(2,1)S(1)}, u32[]{:S(2)}, u32[]{:S(2)}) collective-permute-start(bf16[192,256]{1,0:T(8,128)(2,1)S(1)} %pad_maximum_fusion.1), channel_id=1, source_target_pairs={{0,1},{1,0},{2,3},{3,2},{4,5},{5,4},{6,7},{7,6},{8,9},{9,8},{10,11... | collective-permute-start | bytes 294920 | tf_op jit(solution)/shard_map/ppermute | solution.py:409
  12.3 3.0 %collective-permute-done.3.refs_2_ = bf16[128,256]{1,0:T(8,128)(2,1)S(1)} collective-permute-done((bf16[128,256]{1,0:T(8,128)(2,1)S(1)}, bf16[128,256]{1,0:T(8,128)(2,1)S(1)}, u32[]{:S(2)}, u32[]{:S(2)}) %collective-permute-start.3) | collective-permute-done | bytes 65568 | tf_op jit(solution)/shard_map/ppermute | solution.py:429
  15.3 0.0 collective-permute-done.2.refs_1_
  15.3 0.3 %collective-permute-start.5 = (bf16[256,256]{1,0:T(8,128)(2,1)S(1)}, bf16[256,256]{1,0:T(8,128)(2,1)S(1)}, u32[]{:S(2)}, u32[]{:S(2)}) collective-permute-start(bf16[256,256]{1,0:T(8,128)(2,1)S(1)} %pad_maximum_fusion), channel_id=1, source_target_pairs={{0,1},{1,0},{2,3},{3,2},{4,5},{5,4},{6,7},{7,6},{8,9},{9,8},{10,11... | collective-permute-start | bytes 393224 | tf_op jit(solution)/shard_map/ppermute | solution.py:409
  15.6 0.0 collective-permute-done.6
  15.6 1.1 %collective-permute-done.5 = bf16[256,256]{1,0:T(8,128)(2,1)S(1)} collective-permute-done((bf16[256,256]{1,0:T(8,128)(2,1)S(1)}, bf16[256,256]{1,0:T(8,128)(2,1)S(1)}, u32[]{:S(2)}, u32[]{:S(2)}) %collective-permute-start.5) | collective-permute-done | bytes 131104 | tf_op jit(solution)/shard_map/ppermute | solution.py:409
  16.8 1.8 %tile_sum.1 = f32[256,256]{1,0:T(8,128)} custom-call(bf16[256,1024]{1,0:T(8,128)(2,1)S(1)} %get-tuple-element.9.pick_ref, bf16[128,256]{1,0:T(8,128)(2,1)S(1)} %maximum_select_fusion.refs_0_, bf16[128,256]{1,0:T(8,128)(2,1)S(1)} %collective-permute-done.2.refs_1_, bf16[128,256]{1,0:T(8,128)(2,1)S(1)} %collective-permute-done.3.refs_2_, ...), custom_call_target="tpu_custom_call" | custom-call | tf_op jit(solution)/shard_map/tile_sum/pallas_call | solution.py:389
  (7 shorter events, 0.1 us)
Async XLA Ops:
  2.2 3.1 %collective-permute-start.1 = (bf16[64,256]{1,0:T(8,128)(2,1)S(1)}, bf16[64,256]{1,0:T(8,128)(2,1)S(1)}, u32[]{:S(2)}, u32[]{:S(2)}) collective-permute-start(bf16[64,256]{1,0:T(8,128)(2,1)S(1)} %march.1), channel_id=1, source_target_pairs={{0,1},{1,0},{2,3},{3,2},{4,5},{5,4},{6,7},{7,6},{8,9},{9,8},{10,11... | collective-permute-start | bytes 98312 | tf_op jit(solution)/shard_map/ppermute | solution.py:409
  2.7 7.0 %collective-permute-start = (bf16[64,256]{1,0:T(8,128)(2,1)S(1)}, bf16[64,256]{1,0:T(8,128)(2,1)S(1)}, u32[]{:S(2)}, u32[]{:S(2)}) collective-permute-start(bf16[64,256]{1,0:T(8,128)(2,1)S(1)} %march.1), channel_id=1, source_target_pairs={{0,2},{1,3},{2,0},{3,1},{4,6},{5,7},{6,4},{7,5},{8,10},{9,11},{10,... | collective-permute-start | bytes 98312 | tf_op jit(solution)/shard_map/ppermute | solution.py:409
  5.3 6.7 %collective-permute-start.4 = (bf16[128,256]{1,0:T(8,128)(2,1)S(1)}, bf16[128,256]{1,0:T(8,128)(2,1)S(1)}, u32[]{:S(2)}, u32[]{:S(2)}) collective-permute-start(bf16[128,256]{1,0:T(8,128)(2,1)S(1)} %maximum_select_fusion.refs_0_), channel_id=1, source_target_pairs={{0,12},{1,15},{2,14},{3,13},{4,8},{5,11},{6,10},{7,9},{8,4},{9,7},... | collective-permute-start | bytes 196616 | tf_op jit(solution)/shard_map/ppermute | solution.py:429
  9.0 6.3 %collective-permute-start.3 = (bf16[128,256]{1,0:T(8,128)(2,1)S(1)}, bf16[128,256]{1,0:T(8,128)(2,1)S(1)}, u32[]{:S(2)}, u32[]{:S(2)}) collective-permute-start(bf16[128,256]{1,0:T(8,128)(2,1)S(1)} %maximum_select_fusion.refs_0_), channel_id=1, source_target_pairs={{0,8},{1,11},{2,10},{3,9},{4,12},{5,15},{6,14},{7,13},{8,0},{9,3},... | collective-permute-start | bytes 196616 | tf_op jit(solution)/shard_map/ppermute | solution.py:429
  9.0 6.3 %collective-permute-start.2 = (bf16[128,256]{1,0:T(8,128)(2,1)S(1)}, bf16[128,256]{1,0:T(8,128)(2,1)S(1)}, u32[]{:S(2)}, u32[]{:S(2)}) collective-permute-start(bf16[128,256]{1,0:T(8,128)(2,1)S(1)} %maximum_select_fusion.refs_0_), channel_id=1, source_target_pairs={{0,4},{1,7},{2,6},{3,5},{4,0},{5,3},{6,2},{7,1},{8,12},{9,15},{10,... | collective-permute-start | bytes 196616 | tf_op jit(solution)/shard_map/ppermute | solution.py:429
  12.0 3.6 %collective-permute-start.6 = (bf16[192,256]{1,0:T(8,128)(2,1)S(1)}, bf16[192,256]{1,0:T(8,128)(2,1)S(1)}, u32[]{:S(2)}, u32[]{:S(2)}) collective-permute-start(bf16[192,256]{1,0:T(8,128)(2,1)S(1)} %pad_maximum_fusion.1), channel_id=1, source_target_pairs={{0,1},{1,0},{2,3},{3,2},{4,5},{5,4},{6,7},{7,6},{8,9},{9,8},{10,11... | collective-permute-start | bytes 294920 | tf_op jit(solution)/shard_map/ppermute | solution.py:409
  15.3 1.4 %collective-permute-start.5 = (bf16[256,256]{1,0:T(8,128)(2,1)S(1)}, bf16[256,256]{1,0:T(8,128)(2,1)S(1)}, u32[]{:S(2)}, u32[]{:S(2)}) collective-permute-start(bf16[256,256]{1,0:T(8,128)(2,1)S(1)} %pad_maximum_fusion), channel_id=1, source_target_pairs={{0,1},{1,0},{2,3},{3,2},{4,5},{5,4},{6,7},{7,6},{8,9},{9,8},{10,11... | collective-permute-start | bytes 393224 | tf_op jit(solution)/shard_map/ppermute | solution.py:409

commit v8 on v7

--- a/solution.py
+++ b/solution.py
@@ -293,7 +293,7 @@
     row_hbm,
     col_hbm,
     after_ref,
-    pick_ref,
+    starts_ref,
     turned_ref,
     col_ref,
     passed_ref,
@@ -320,15 +320,14 @@
     devices = lax.axis_size("radial")
     for copy in copies[:4]:
         copy.wait()
-    shape = (SUB, pick_ref.shape[1])
-    offset = lax.broadcasted_iota(jnp.int32, shape, 1) - lax.broadcasted_iota(jnp.int32, shape, 0)
+    column = lax.broadcasted_iota(jnp.int32, starts_ref.shape, 1)
+    starts = jnp.full(starts_ref.shape, -1, jnp.int32)
     for slot in range(K_MAX):
         source = lax.rem(tile + shift_ref[0, tile] + slot // CAP, devices)
         start = source * local_rows + sub_ref[0, tile, slot] * SUB
-        start = jnp.where(slot < count_ref[0, tile], start, -2 * pick_ref.shape[1])
-        pick_ref[slot * SUB : (slot + 1) * SUB, :] = jnp.where(offset == start, 1.0, 0.0).astype(
-            jnp.bfloat16
-        )
+        start = jnp.where(slot < count_ref[0, tile], start, -1)
+        starts = jnp.where(column == slot, start, starts)
+    starts_ref[...] = starts
     turned_ref[...] = row_ref[...].T
     passed_ref[...] = after_ref[...]
     copies[4].wait()
@@ -336,7 +335,6 @@
 
 def prepare(source_shift, slot_sub, tile_count, row_weights, col_weights, local_rows, after):
     pixels = row_weights.shape[-1]
-    radials = local_rows * lax.axis_size("radial")
     rows_flat = row_weights.reshape(K_MAX * SUB, pixels)
     cols_flat = col_weights.reshape(K_MAX, col_weights.shape[-2], pixels)
     operands = [source_shift, slot_sub, tile_count, rows_flat]
@@ -344,7 +342,7 @@
     return pl.pallas_call(
         functools.partial(prepare_kernel, local_rows),
         out_shape=[
-            jax.ShapeDtypeStruct((K_MAX * SUB, radials), jnp.bfloat16),
+            jax.ShapeDtypeStruct((8, 128), jnp.int32),
             jax.ShapeDtypeStruct((pixels, K_MAX * SUB), jnp.bfloat16),
             jax.ShapeDtypeStruct(cols_flat.shape, jnp.bfloat16),
             jax.ShapeDtypeStruct(after.shape, after.dtype),
@@ -362,7 +360,7 @@
     )(*in_hbm(operands + [cols_flat]), after)
 
 
-def tile_kernel(places, pick_ref, *refs):
+def tile_kernel(places, starts_ref, *refs):
     part_refs = refs[: len(places)]
     row_ref, col_ref, out_ref, polar_ref, mixed_ref = refs[len(places) :]
     chip = lax.axis_index("radial") // 2
@@ -373,18 +371,19 @@
         if size == polar_ref.shape[0]:
             start = 0
         polar_ref[pl.ds(start, size), :] = part_ref[...]
-    blocks = jnp.dot(pick_ref[...], polar_ref[...], preferred_element_type=jnp.float32)
-    blocks = blocks.astype(jnp.bfloat16)
-    for slot in range(K_MAX):
-        block = blocks[slot * SUB : (slot + 1) * SUB]
+    starts = [starts_ref[0:1, slot : slot + 1][0, 0] for slot in range(K_MAX)]
+    for slot, start in enumerate(starts):
+        block = polar_ref[pl.ds(pl.multiple_of(jnp.maximum(start, 0), SUB), SUB), :]
+        block = jnp.where(start >= 0, block, jnp.zeros_like(block))
         mixed = jnp.dot(block, col_ref[slot], preferred_element_type=jnp.float32)
         mixed_ref[slot * SUB : (slot + 1) * SUB, :] = mixed.astype(jnp.bfloat16)
     out_ref[...] = jnp.dot(row_ref[...], mixed_ref[...], preferred_element_type=jnp.float32)
 
 
-def tile_sum(pick, parts, places, row_weights, col_weights):
+def tile_sum(starts, parts, places, row_weights, col_weights):
     pixels = row_weights.shape[0]
     channels = col_weights.shape[-2]
+    radials = sum(part.shape[0] for part in parts)
     vmem = pl.BlockSpec(memory_space=pltpu.VMEM)
     return pl.pallas_call(
         functools.partial(tile_kernel, places),
@@ -392,13 +391,13 @@
         in_specs=[vmem] * (len(parts) + 3),
         out_specs=vmem,
         scratch_shapes=[
-            pltpu.VMEM((pick.shape[1], channels), jnp.bfloat16),
+            pltpu.VMEM((radials, channels), jnp.bfloat16),
             pltpu.VMEM((K_MAX * SUB, pixels), jnp.bfloat16),
         ],
         compiler_params=pltpu.CompilerParams(vmem_limit_bytes=24 * 1024 * 1024),
         name="tile_sum",
     )(
-        pick,
+        starts,
         *parts,
         row_weights,
         col_weights,
@@ -456,8 +455,8 @@
         prepare, source_shift, slot_sub, tile_count, row_weights, col_weights, polar.shape[0]
     )
     parts, places, ready = gather_parts(polar, devices, prepared)
-    pick, turned, cols = ready
-    tile_value = tile_sum(pick, parts, places, turned, cols)
+    starts, turned, cols = ready
+    tile_value = tile_sum(starts, parts, places, turned, cols)
     return tile_value.reshape((1, 1) + tile_value.shape)
 
 

time: 18.7 us -> 18.3 us (0.979)
  Pallas kernels: 5.65 us -> 5.27 us
    pallas_call x1, Pallas kernels: 1.75 us -> 1.38 us  [tile_sum(): pl.pallas_call(functools.partial(tile_kernel, places), out_shape=jax.Shap...]
where the time goes in v8:
time: 18.3 us; the launch traced here: 18.1 us
  starting transfers between devices  8.16 us (45%)
  Pallas kernels  5.27 us (29%)
  waiting for transfers between devices  4.58 us (25%)
    ppermute x3, starting transfers between devices, gather_parts(): held.append(lax.ppermute(pair, 'radial', routes))  4.45 us
    ppermute x4, starting transfers between devices, swap(): lax.ppermute(value, 'radial', [(i, i ^ distance) for i in range(devices)])  3.71 us
    ppermute x3, waiting for transfers between devices, gather_parts(): held.append(lax.ppermute(pair, 'radial', routes))  3.47 us
    pallas_call x1, Pallas kernels, march(): pl.pallas_call(functools.partial(march_kernel, steps, slabs, units=units)...  2.18 us
    pallas_call x1, Pallas kernels, prepare(): pl.pallas_call(functools.partial(prepare_kernel, local_rows), out_shape=[...  1.71 us
    pallas_call x1, Pallas kernels, tile_sum(): pl.pallas_call(functools.partial(tile_kernel, places), out_shape=jax.Shap...  1.38 us
    ppermute x4, waiting for transfers between devices, swap(): lax.ppermute(value, 'radial', [(i, i ^ distance) for i in range(devices)])  1.11 us
  transfers between devices with their start and end apart: 7, of which 3 were waited for; matrix products, arithmetic and copies ran while one was open for 0% of the time, Pallas kernels for 9%

profile of v8, /device:TPU:0, one launch (start us, length us, event | category | flops | bytes accessed | tf_op | source)
XLA Modules:
  0.0 18.1 jit_solution(8979926484699350426)
XLA Ops:
  0.0 2.2 %march.1 = bf16[64,256]{1,0:T(8,128)(2,1)S(1)} custom-call(s32[2,2]{1,0:T(2,128)} %profile_hbm.1, f32[2]{0:T(128)} %power_hbm.1, s32[2]{0:T(128)} %slot_hbm.1, f32[16,1024]{1,0:T(8,128)} %phase_hbm.1, f32[40,128]{1,0:T(8,128)} %constant.22.clone.wave_hbm, bf16[2,64,1024]{2,1,0:T(8,128)(2,1)} %field_hbm.1, bf16[256,256]{1,0:T(8,128)(2,1)} %constant.23.clone.weight_hbm), custom_call_target="tpu_custom_call" | custom-call | tf_op jit(solution)/shard_map/march/pallas_call | solution.py:272
  2.2 0.5 %collective-permute-start.1 = (bf16[64,256]{1,0:T(8,128)(2,1)S(1)}, bf16[64,256]{1,0:T(8,128)(2,1)S(1)}, u32[]{:S(2)}, u32[]{:S(2)}) collective-permute-start(bf16[64,256]{1,0:T(8,128)(2,1)S(1)} %march.1), channel_id=1, source_target_pairs={{0,1},{1,0},{2,3},{3,2},{4,5},{5,4},{6,7},{7,6},{8,9},{9,8},{10,11... | collective-permute-start | bytes 98312 | tf_op jit(solution)/shard_map/ppermute | solution.py:408
  2.7 2.6 %collective-permute-start = (bf16[64,256]{1,0:T(8,128)(2,1)S(1)}, bf16[64,256]{1,0:T(8,128)(2,1)S(1)}, u32[]{:S(2)}, u32[]{:S(2)}) collective-permute-start(bf16[64,256]{1,0:T(8,128)(2,1)S(1)} %march.1), channel_id=1, source_target_pairs={{0,2},{1,3},{2,0},{3,1},{4,6},{5,7},{6,4},{7,5},{8,10},{9,11},{10,... | collective-permute-start | bytes 98312 | tf_op jit(solution)/shard_map/ppermute | solution.py:408
  5.3 0.0 collective-permute-done.1
  5.3 3.7 %collective-permute-start.4 = (bf16[128,256]{1,0:T(8,128)(2,1)S(1)}, bf16[128,256]{1,0:T(8,128)(2,1)S(1)}, u32[]{:S(2)}, u32[]{:S(2)}) collective-permute-start(bf16[128,256]{1,0:T(8,128)(2,1)S(1)} %maximum_select_fusion.refs_0_), channel_id=1, source_target_pairs={{0,12},{1,15},{2,14},{3,13},{4,8},{5,11},{6,10},{7,9},{8,4},{9,7},... | collective-permute-start | bytes 196616 | tf_op jit(solution)/shard_map/ppermute | solution.py:428
  9.0 0.0 collective-permute-start.3
  9.0 0.8 %collective-permute-start.2 = (bf16[128,256]{1,0:T(8,128)(2,1)S(1)}, bf16[128,256]{1,0:T(8,128)(2,1)S(1)}, u32[]{:S(2)}, u32[]{:S(2)}) collective-permute-start(bf16[128,256]{1,0:T(8,128)(2,1)S(1)} %maximum_select_fusion.refs_0_), channel_id=1, source_target_pairs={{0,4},{1,7},{2,6},{3,5},{4,0},{5,3},{6,2},{7,1},{8,12},{9,15},{10,... | collective-permute-start | bytes 196616 | tf_op jit(solution)/shard_map/ppermute | solution.py:428
  9.7 0.0 collective-permute-done.after_ref
  9.8 1.7 %prepare.1 = (s32[8,128]{1,0:T(8,128)S(1)}, bf16[256,256]{1,0:T(8,128)(2,1)S(1)}, bf16[16,256,256]{2,1,0:T(8,128)(2,1)S(1)}, bf16[64,256]{1,0:T(8,128)(2,1)S(1)}) custom-call(s32[1,16]{1,0:T(1,128)} %shift_hbm.1, s32[1,16,16]{2,1,0:T(8,128)} %sub_hbm.1, s32[1,16]{1,0:T(1,128)} %count_hbm.1, bf16[256,256]{1,0:T(8,128)(2,1)} %bitcast.4, ...), custom_call_target="tpu_custom_call" | custom-call | flops 2000000000 | bytes 2097152 | tf_op jit(solution)/shard_map/prepare/pallas_call | solution.py:342
  11.5 0.5 %collective-permute-done.4.refs_3_ = bf16[128,256]{1,0:T(8,128)(2,1)S(1)} collective-permute-done((bf16[128,256]{1,0:T(8,128)(2,1)S(1)}, bf16[128,256]{1,0:T(8,128)(2,1)S(1)}, u32[]{:S(2)}, u32[]{:S(2)}) %collective-permute-start.4) | collective-permute-done | bytes 65568 | tf_op jit(solution)/shard_map/ppermute | solution.py:428
  12.0 0.4 %collective-permute-start.6 = (bf16[192,256]{1,0:T(8,128)(2,1)S(1)}, bf16[192,256]{1,0:T(8,128)(2,1)S(1)}, u32[]{:S(2)}, u32[]{:S(2)}) collective-permute-start(bf16[192,256]{1,0:T(8,128)(2,1)S(1)} %pad_maximum_fusion.1), channel_id=1, source_target_pairs={{0,1},{1,0},{2,3},{3,2},{4,5},{5,4},{6,7},{7,6},{8,9},{9,8},{10,11... | collective-permute-start | bytes 294920 | tf_op jit(solution)/shard_map/ppermute | solution.py:408
  12.3 3.0 %collective-permute-done.3.refs_2_ = bf16[128,256]{1,0:T(8,128)(2,1)S(1)} collective-permute-done((bf16[128,256]{1,0:T(8,128)(2,1)S(1)}, bf16[128,256]{1,0:T(8,128)(2,1)S(1)}, u32[]{:S(2)}, u32[]{:S(2)}) %collective-permute-start.3) | collective-permute-done | bytes 65568 | tf_op jit(solution)/shard_map/ppermute | solution.py:428
  15.3 0.0 collective-permute-done.2.refs_1_
  15.3 0.3 %collective-permute-start.5 = (bf16[256,256]{1,0:T(8,128)(2,1)S(1)}, bf16[256,256]{1,0:T(8,128)(2,1)S(1)}, u32[]{:S(2)}, u32[]{:S(2)}) collective-permute-start(bf16[256,256]{1,0:T(8,128)(2,1)S(1)} %pad_maximum_fusion), channel_id=1, source_target_pairs={{0,1},{1,0},{2,3},{3,2},{4,5},{5,4},{6,7},{7,6},{8,9},{9,8},{10,11... | collective-permute-start | bytes 393224 | tf_op jit(solution)/shard_map/ppermute | solution.py:408
  15.6 0.0 collective-permute-done.6
  15.6 1.1 %collective-permute-done.5 = bf16[256,256]{1,0:T(8,128)(2,1)S(1)} collective-permute-done((bf16[256,256]{1,0:T(8,128)(2,1)S(1)}, bf16[256,256]{1,0:T(8,128)(2,1)S(1)}, u32[]{:S(2)}, u32[]{:S(2)}) %collective-permute-start.5) | collective-permute-done | bytes 131104 | tf_op jit(solution)/shard_map/ppermute | solution.py:408
  16.8 1.4 %tile_sum.1 = f32[256,256]{1,0:T(8,128)} custom-call(s32[8,128]{1,0:T(8,128)S(1)} %get-tuple-element.9.starts_ref, bf16[128,256]{1,0:T(8,128)(2,1)S(1)} %maximum_select_fusion.refs_0_, bf16[128,256]{1,0:T(8,128)(2,1)S(1)} %collective-permute-done.2.refs_1_, bf16[128,256]{1,0:T(8,128)(2,1)S(1)} %collective-permute-done.3.refs_2_, ...), custom_call_target="tpu_custom_call" | custom-call | tf_op jit(solution)/shard_map/tile_sum/pallas_call | solution.py:388
  (7 shorter events, 0.1 us)
Async XLA Ops:
  2.2 3.1 %collective-permute-start.1 = (bf16[64,256]{1,0:T(8,128)(2,1)S(1)}, bf16[64,256]{1,0:T(8,128)(2,1)S(1)}, u32[]{:S(2)}, u32[]{:S(2)}) collective-permute-start(bf16[64,256]{1,0:T(8,128)(2,1)S(1)} %march.1), channel_id=1, source_target_pairs={{0,1},{1,0},{2,3},{3,2},{4,5},{5,4},{6,7},{7,6},{8,9},{9,8},{10,11... | collective-permute-start | bytes 98312 | tf_op jit(solution)/shard_map/ppermute | solution.py:408
  2.7 7.0 %collective-permute-start = (bf16[64,256]{1,0:T(8,128)(2,1)S(1)}, bf16[64,256]{1,0:T(8,128)(2,1)S(1)}, u32[]{:S(2)}, u32[]{:S(2)}) collective-permute-start(bf16[64,256]{1,0:T(8,128)(2,1)S(1)} %march.1), channel_id=1, source_target_pairs={{0,2},{1,3},{2,0},{3,1},{4,6},{5,7},{6,4},{7,5},{8,10},{9,11},{10,... | collective-permute-start | bytes 98312 | tf_op jit(solution)/shard_map/ppermute | solution.py:408
  5.3 6.7 %collective-permute-start.4 = (bf16[128,256]{1,0:T(8,128)(2,1)S(1)}, bf16[128,256]{1,0:T(8,128)(2,1)S(1)}, u32[]{:S(2)}, u32[]{:S(2)}) collective-permute-start(bf16[128,256]{1,0:T(8,128)(2,1)S(1)} %maximum_select_fusion.refs_0_), channel_id=1, source_target_pairs={{0,12},{1,15},{2,14},{3,13},{4,8},{5,11},{6,10},{7,9},{8,4},{9,7},... | collective-permute-start | bytes 196616 | tf_op jit(solution)/shard_map/ppermute | solution.py:428
  9.0 6.3 %collective-permute-start.3 = (bf16[128,256]{1,0:T(8,128)(2,1)S(1)}, bf16[128,256]{1,0:T(8,128)(2,1)S(1)}, u32[]{:S(2)}, u32[]{:S(2)}) collective-permute-start(bf16[128,256]{1,0:T(8,128)(2,1)S(1)} %maximum_select_fusion.refs_0_), channel_id=1, source_target_pairs={{0,8},{1,11},{2,10},{3,9},{4,12},{5,15},{6,14},{7,13},{8,0},{9,3},... | collective-permute-start | bytes 196616 | tf_op jit(solution)/shard_map/ppermute | solution.py:428
  9.0 6.3 %collective-permute-start.2 = (bf16[128,256]{1,0:T(8,128)(2,1)S(1)}, bf16[128,256]{1,0:T(8,128)(2,1)S(1)}, u32[]{:S(2)}, u32[]{:S(2)}) collective-permute-start(bf16[128,256]{1,0:T(8,128)(2,1)S(1)} %maximum_select_fusion.refs_0_), channel_id=1, source_target_pairs={{0,4},{1,7},{2,6},{3,5},{4,0},{5,3},{6,2},{7,1},{8,12},{9,15},{10,... | collective-permute-start | bytes 196616 | tf_op jit(solution)/shard_map/ppermute | solution.py:428
  12.0 3.6 %collective-permute-start.6 = (bf16[192,256]{1,0:T(8,128)(2,1)S(1)}, bf16[192,256]{1,0:T(8,128)(2,1)S(1)}, u32[]{:S(2)}, u32[]{:S(2)}) collective-permute-start(bf16[192,256]{1,0:T(8,128)(2,1)S(1)} %pad_maximum_fusion.1), channel_id=1, source_target_pairs={{0,1},{1,0},{2,3},{3,2},{4,5},{5,4},{6,7},{7,6},{8,9},{9,8},{10,11... | collective-permute-start | bytes 294920 | tf_op jit(solution)/shard_map/ppermute | solution.py:408
  15.3 1.4 %collective-permute-start.5 = (bf16[256,256]{1,0:T(8,128)(2,1)S(1)}, bf16[256,256]{1,0:T(8,128)(2,1)S(1)}, u32[]{:S(2)}, u32[]{:S(2)}) collective-permute-start(bf16[256,256]{1,0:T(8,128)(2,1)S(1)} %pad_maximum_fusion), channel_id=1, source_target_pairs={{0,1},{1,0},{2,3},{3,2},{4,5},{5,4},{6,7},{7,6},{8,9},{9,8},{10,11... | collective-permute-start | bytes 393224 | tf_op jit(solution)/shard_map/ppermute | solution.py:408

commit v9 on v8

--- a/solution.py
+++ b/solution.py
@@ -423,16 +423,17 @@
     first = swap(polar, 2, devices)
     pair = in_order(polar, swap(polar, 1, devices))
     held = []
-    for even, odd in ((2, 3), (4, 5), (6, 7)):
+    for even, odd in ((4, 5), (2, 3), (6, 7)):
         routes = [(i, i ^ (2 * (odd if i % 2 else even))) for i in range(devices)]
         held.append(lax.ppermute(pair, "radial", routes))
     *ready, first = prepared(first)
-    near, far, last = held
-    early = swap(jnp.concatenate([last, first], 0), 1, devices)
-    late = swap(jnp.concatenate([near, far], 0), 1, devices)
-    parts = [pair] + held + [late[:size], late[size:], early[:size]]
-    parts.append(in_order(first, early[size:]))
-    places = [(0, 0), (2, 3), (4, 5), (6, 7), (3, 2), (5, 4), (7, 6), (1, 1)]
+    early = swap(jnp.concatenate([held[2], first], 0), 1, devices)
+    late = swap(jnp.concatenate(held[:2], 0), 1, devices)
+    parts = [pair] + held
+    parts += [late[i * size : (i + 1) * size] for i in range(2)]
+    parts += [early[i * size : (i + 1) * size] for i in range(1)]
+    parts.append(in_order(first, early[1 * size :]))
+    places = [(0, 0), (4, 5), (2, 3), (6, 7), (5, 4), (3, 2), (7, 6), (1, 1)]
     return parts, places, ready
 
 

time: 18.3 us -> 18.1 us (0.989)
  starting transfers between devices: 8.16 us -> 7.95 us
    ppermute x4, starting transfers between devices: 3.71 us -> 3.5 us  [swap(): lax.ppermute(value, 'radial', [(i, i ^ distance) for i in range(devices)])]
  transfers between devices with their start and end apart: 7 -> 7, of which waited for: 3 -> 3; matrix products, arithmetic and copies ran while one was open for 0% -> 0% of each run, Pallas kernels for 9% -> 10%
where the time goes in v9:
time: 18.1 us; the launch traced here: 18 us
  starting transfers between devices  7.95 us (44%)
  Pallas kernels  5.27 us (29%)
  waiting for transfers between devices  4.62 us (26%)
    ppermute x3, starting transfers between devices, gather_parts(): held.append(lax.ppermute(pair, 'radial', routes))  4.45 us
    ppermute x4, starting transfers between devices, swap(): lax.ppermute(value, 'radial', [(i, i ^ distance) for i in range(devices)])  3.5 us
    ppermute x3, waiting for transfers between devices, gather_parts(): held.append(lax.ppermute(pair, 'radial', routes))  3.49 us
    pallas_call x1, Pallas kernels, march(): pl.pallas_call(functools.partial(march_kernel, steps, slabs, units=units)...  2.18 us
    pallas_call x1, Pallas kernels, prepare(): pl.pallas_call(functools.partial(prepare_kernel, local_rows), out_shape=[...  1.71 us
    pallas_call x1, Pallas kernels, tile_sum(): pl.pallas_call(functools.partial(tile_kernel, places), out_shape=jax.Shap...  1.38 us
    ppermute x4, waiting for transfers between devices, swap(): lax.ppermute(value, 'radial', [(i, i ^ distance) for i in range(devices)])  1.13 us
  transfers between devices with their start and end apart: 7, of which 3 were waited for; matrix products, arithmetic and copies ran while one was open for 0% of the time, Pallas kernels for 10%

profile of v9, /device:TPU:0, one launch (start us, length us, event | category | flops | bytes accessed | tf_op | source)
XLA Modules:
  0.0 18.0 jit_solution(6543431173724160413)
XLA Ops:
  0.0 2.2 %march.1 = bf16[64,256]{1,0:T(8,128)(2,1)S(1)} custom-call(s32[2,2]{1,0:T(2,128)} %profile_hbm.1, f32[2]{0:T(128)} %power_hbm.1, s32[2]{0:T(128)} %slot_hbm.1, f32[16,1024]{1,0:T(8,128)} %phase_hbm.1, f32[40,128]{1,0:T(8,128)} %constant.22.clone.wave_hbm, bf16[2,64,1024]{2,1,0:T(8,128)(2,1)} %field_hbm.1, bf16[256,256]{1,0:T(8,128)(2,1)} %constant.23.clone.weight_hbm), custom_call_target="tpu_custom_call" | custom-call | tf_op jit(solution)/shard_map/march/pallas_call | solution.py:272
  2.2 0.5 %collective-permute-start.1 = (bf16[64,256]{1,0:T(8,128)(2,1)S(1)}, bf16[64,256]{1,0:T(8,128)(2,1)S(1)}, u32[]{:S(2)}, u32[]{:S(2)}) collective-permute-start(bf16[64,256]{1,0:T(8,128)(2,1)S(1)} %march.1), channel_id=1, source_target_pairs={{0,1},{1,0},{2,3},{3,2},{4,5},{5,4},{6,7},{7,6},{8,9},{9,8},{10,11... | collective-permute-start | bytes 98312 | tf_op jit(solution)/shard_map/ppermute | solution.py:408
  2.7 2.6 %collective-permute-start = (bf16[64,256]{1,0:T(8,128)(2,1)S(1)}, bf16[64,256]{1,0:T(8,128)(2,1)S(1)}, u32[]{:S(2)}, u32[]{:S(2)}) collective-permute-start(bf16[64,256]{1,0:T(8,128)(2,1)S(1)} %march.1), channel_id=1, source_target_pairs={{0,2},{1,3},{2,0},{3,1},{4,6},{5,7},{6,4},{7,5},{8,10},{9,11},{10,... | collective-permute-start | bytes 98312 | tf_op jit(solution)/shard_map/ppermute | solution.py:408
  5.3 0.0 collective-permute-done.1
  5.3 3.7 %collective-permute-start.4 = (bf16[128,256]{1,0:T(8,128)(2,1)S(1)}, bf16[128,256]{1,0:T(8,128)(2,1)S(1)}, u32[]{:S(2)}, u32[]{:S(2)}) collective-permute-start(bf16[128,256]{1,0:T(8,128)(2,1)S(1)} %maximum_select_fusion.refs_0_), channel_id=1, source_target_pairs={{0,12},{1,15},{2,14},{3,13},{4,8},{5,11},{6,10},{7,9},{8,4},{9,7},... | collective-permute-start | bytes 196616 | tf_op jit(solution)/shard_map/ppermute | solution.py:428
  9.0 0.0 collective-permute-start.3
  9.0 0.8 %collective-permute-start.2 = (bf16[128,256]{1,0:T(8,128)(2,1)S(1)}, bf16[128,256]{1,0:T(8,128)(2,1)S(1)}, u32[]{:S(2)}, u32[]{:S(2)}) collective-permute-start(bf16[128,256]{1,0:T(8,128)(2,1)S(1)} %maximum_select_fusion.refs_0_), channel_id=1, source_target_pairs={{0,8},{1,11},{2,10},{3,9},{4,12},{5,15},{6,14},{7,13},{8,0},{9,3},... | collective-permute-start | bytes 196616 | tf_op jit(solution)/shard_map/ppermute | solution.py:428
  9.7 0.0 collective-permute-done.after_ref
  9.8 1.7 %prepare.1 = (s32[8,128]{1,0:T(8,128)S(1)}, bf16[256,256]{1,0:T(8,128)(2,1)S(1)}, bf16[16,256,256]{2,1,0:T(8,128)(2,1)S(1)}, bf16[64,256]{1,0:T(8,128)(2,1)S(1)}) custom-call(s32[1,16]{1,0:T(1,128)} %shift_hbm.1, s32[1,16,16]{2,1,0:T(8,128)} %sub_hbm.1, s32[1,16]{1,0:T(1,128)} %count_hbm.1, bf16[256,256]{1,0:T(8,128)(2,1)} %bitcast.4, ...), custom_call_target="tpu_custom_call" | custom-call | flops 2000000000 | bytes 2097152 | tf_op jit(solution)/shard_map/prepare/pallas_call | solution.py:342
  11.5 0.7 %collective-permute-done.4.refs_3_ = bf16[128,256]{1,0:T(8,128)(2,1)S(1)} collective-permute-done((bf16[128,256]{1,0:T(8,128)(2,1)S(1)}, bf16[128,256]{1,0:T(8,128)(2,1)S(1)}, u32[]{:S(2)}, u32[]{:S(2)}) %collective-permute-start.4) | collective-permute-done | bytes 65568 | tf_op jit(solution)/shard_map/ppermute | solution.py:428
  12.2 0.2 collective-permute-start.6
  12.3 2.8 %collective-permute-done.3.refs_2_ = bf16[128,256]{1,0:T(8,128)(2,1)S(1)} collective-permute-done((bf16[128,256]{1,0:T(8,128)(2,1)S(1)}, bf16[128,256]{1,0:T(8,128)(2,1)S(1)}, u32[]{:S(2)}, u32[]{:S(2)}) %collective-permute-start.3) | collective-permute-done | bytes 65568 | tf_op jit(solution)/shard_map/ppermute | solution.py:428
  15.1 0.0 collective-permute-done.2.refs_1_
  15.2 0.3 %collective-permute-start.5 = (bf16[256,256]{1,0:T(8,128)(2,1)S(1)}, bf16[256,256]{1,0:T(8,128)(2,1)S(1)}, u32[]{:S(2)}, u32[]{:S(2)}) collective-permute-start(bf16[256,256]{1,0:T(8,128)(2,1)S(1)} %pad_maximum_fusion), channel_id=1, source_target_pairs={{0,1},{1,0},{2,3},{3,2},{4,5},{5,4},{6,7},{7,6},{8,9},{9,8},{10,11... | collective-permute-start | bytes 393224 | tf_op jit(solution)/shard_map/ppermute | solution.py:408
  15.4 0.0 collective-permute-done.6
  15.5 1.1 %collective-permute-done.5 = bf16[256,256]{1,0:T(8,128)(2,1)S(1)} collective-permute-done((bf16[256,256]{1,0:T(8,128)(2,1)S(1)}, bf16[256,256]{1,0:T(8,128)(2,1)S(1)}, u32[]{:S(2)}, u32[]{:S(2)}) %collective-permute-start.5) | collective-permute-done | bytes 131104 | tf_op jit(solution)/shard_map/ppermute | solution.py:408
  16.6 1.4 %tile_sum.1 = f32[256,256]{1,0:T(8,128)} custom-call(s32[8,128]{1,0:T(8,128)S(1)} %get-tuple-element.9.starts_ref, bf16[128,256]{1,0:T(8,128)(2,1)S(1)} %maximum_select_fusion.refs_0_, bf16[128,256]{1,0:T(8,128)(2,1)S(1)} %collective-permute-done.2.refs_1_, bf16[128,256]{1,0:T(8,128)(2,1)S(1)} %collective-permute-done.3.refs_2_, ...), custom_call_target="tpu_custom_call" | custom-call | tf_op jit(solution)/shard_map/tile_sum/pallas_call | solution.py:388
  (7 shorter events, 0.1 us)
Async XLA Ops:
  2.2 3.1 %collective-permute-start.1 = (bf16[64,256]{1,0:T(8,128)(2,1)S(1)}, bf16[64,256]{1,0:T(8,128)(2,1)S(1)}, u32[]{:S(2)}, u32[]{:S(2)}) collective-permute-start(bf16[64,256]{1,0:T(8,128)(2,1)S(1)} %march.1), channel_id=1, source_target_pairs={{0,1},{1,0},{2,3},{3,2},{4,5},{5,4},{6,7},{7,6},{8,9},{9,8},{10,11... | collective-permute-start | bytes 98312 | tf_op jit(solution)/shard_map/ppermute | solution.py:408
  2.7 7.0 %collective-permute-start = (bf16[64,256]{1,0:T(8,128)(2,1)S(1)}, bf16[64,256]{1,0:T(8,128)(2,1)S(1)}, u32[]{:S(2)}, u32[]{:S(2)}) collective-permute-start(bf16[64,256]{1,0:T(8,128)(2,1)S(1)} %march.1), channel_id=1, source_target_pairs={{0,2},{1,3},{2,0},{3,1},{4,6},{5,7},{6,4},{7,5},{8,10},{9,11},{10,... | collective-permute-start | bytes 98312 | tf_op jit(solution)/shard_map/ppermute | solution.py:408
  5.3 6.9 %collective-permute-start.4 = (bf16[128,256]{1,0:T(8,128)(2,1)S(1)}, bf16[128,256]{1,0:T(8,128)(2,1)S(1)}, u32[]{:S(2)}, u32[]{:S(2)}) collective-permute-start(bf16[128,256]{1,0:T(8,128)(2,1)S(1)} %maximum_select_fusion.refs_0_), channel_id=1, source_target_pairs={{0,12},{1,15},{2,14},{3,13},{4,8},{5,11},{6,10},{7,9},{8,4},{9,7},... | collective-permute-start | bytes 196616 | tf_op jit(solution)/shard_map/ppermute | solution.py:428
  9.0 6.2 %collective-permute-start.3 = (bf16[128,256]{1,0:T(8,128)(2,1)S(1)}, bf16[128,256]{1,0:T(8,128)(2,1)S(1)}, u32[]{:S(2)}, u32[]{:S(2)}) collective-permute-start(bf16[128,256]{1,0:T(8,128)(2,1)S(1)} %maximum_select_fusion.refs_0_), channel_id=1, source_target_pairs={{0,4},{1,7},{2,6},{3,5},{4,0},{5,3},{6,2},{7,1},{8,12},{9,15},{10,... | collective-permute-start | bytes 196616 | tf_op jit(solution)/shard_map/ppermute | solution.py:428
  9.0 6.2 %collective-permute-start.2 = (bf16[128,256]{1,0:T(8,128)(2,1)S(1)}, bf16[128,256]{1,0:T(8,128)(2,1)S(1)}, u32[]{:S(2)}, u32[]{:S(2)}) collective-permute-start(bf16[128,256]{1,0:T(8,128)(2,1)S(1)} %maximum_select_fusion.refs_0_), channel_id=1, source_target_pairs={{0,8},{1,11},{2,10},{3,9},{4,12},{5,15},{6,14},{7,13},{8,0},{9,3},... | collective-permute-start | bytes 196616 | tf_op jit(solution)/shard_map/ppermute | solution.py:428
  12.2 3.2 %collective-permute-start.6 = (bf16[192,256]{1,0:T(8,128)(2,1)S(1)}, bf16[192,256]{1,0:T(8,128)(2,1)S(1)}, u32[]{:S(2)}, u32[]{:S(2)}) collective-permute-start(bf16[192,256]{1,0:T(8,128)(2,1)S(1)} %pad_maximum_fusion.1), channel_id=1, source_target_pairs={{0,1},{1,0},{2,3},{3,2},{4,5},{5,4},{6,7},{7,6},{8,9},{9,8},{10,11... | collective-permute-start | bytes 294920 | tf_op jit(solution)/shard_map/ppermute | solution.py:408
  15.2 1.4 %collective-permute-start.5 = (bf16[256,256]{1,0:T(8,128)(2,1)S(1)}, bf16[256,256]{1,0:T(8,128)(2,1)S(1)}, u32[]{:S(2)}, u32[]{:S(2)}) collective-permute-start(bf16[256,256]{1,0:T(8,128)(2,1)S(1)} %pad_maximum_fusion), channel_id=1, source_target_pairs={{0,1},{1,0},{2,3},{3,2},{4,5},{5,4},{6,7},{7,6},{8,9},{9,8},{10,11... | collective-permute-start | bytes 393224 | tf_op jit(solution)/shard_map/ppermute | solution.py:408

commit v10 on v9

--- a/solution.py
+++ b/solution.py
@@ -360,39 +360,56 @@
     )(*in_hbm(operands + [cols_flat]), after)
 
 
-def tile_kernel(places, starts_ref, *refs):
+def tile_kernel(places, units, starts_ref, *refs):
     part_refs = refs[: len(places)]
-    row_ref, col_ref, out_ref, polar_ref, mixed_ref = refs[len(places) :]
+    row_ref, col_ref, out_ref, polar_ref = refs[len(places) :]
     chip = lax.axis_index("radial") // 2
     core = lax.axis_index("radial") % 2
-    for (even, odd), part_ref in zip(places, part_refs):
-        size = part_ref.shape[0]
-        start = jnp.where(core == 0, chip ^ even, chip ^ odd) * size
-        if size == polar_ref.shape[0]:
-            start = 0
-        polar_ref[pl.ds(start, size), :] = part_ref[...]
-    starts = [starts_ref[0:1, slot : slot + 1][0, 0] for slot in range(K_MAX)]
-    for slot, start in enumerate(starts):
-        block = polar_ref[pl.ds(pl.multiple_of(jnp.maximum(start, 0), SUB), SUB), :]
-        block = jnp.where(start >= 0, block, jnp.zeros_like(block))
-        mixed = jnp.dot(block, col_ref[slot], preferred_element_type=jnp.float32)
-        mixed_ref[slot * SUB : (slot + 1) * SUB, :] = mixed.astype(jnp.bfloat16)
-    out_ref[...] = jnp.dot(row_ref[...], mixed_ref[...], preferred_element_type=jnp.float32)
-
-
-def tile_sum(starts, parts, places, row_weights, col_weights):
+    half = out_ref.shape[0] // 2
+
+    def run(*products):
+        def stage(slot):
+            pltpu.matmul_push_rhs(col_ref[slot], slot // 2 % 2, slot % 2)
+
+        for slot in range(4):
+            stage(slot)
+        starts = [starts_ref[0:1, slot : slot + 1][0, 0] for slot in range(K_MAX)]
+        for (even, odd), part_ref in zip(places, part_refs):
+            size = part_ref.shape[0]
+            start = jnp.where(core == 0, chip ^ even, chip ^ odd) * size
+            if size == polar_ref.shape[0]:
+                start = 0
+            polar_ref[pl.ds(start, size), :] = part_ref[...]
+        for slot, start in enumerate(starts):
+            block = polar_ref[pl.ds(pl.multiple_of(jnp.maximum(start, 0), SUB), SUB), :]
+            block = jnp.where(start >= 0, block, jnp.zeros_like(block))
+            pltpu.matmul_acc_lhs(products[slot], block, load_staged_rhs=slot // 2 % 2)
+            if slot + 4 < K_MAX:
+                stage(slot + 4)
+        mixed = [pltpu.matmul_pop(product).astype(jnp.bfloat16) for product in products[:K_MAX]]
+        mixed = jnp.concatenate(mixed, 0)
+        for unit, product in enumerate(products[K_MAX:]):
+            pltpu.matmul_push_rhs(mixed, 0, unit)
+            lines = slice(unit * half, (unit + 1) * half)
+            pltpu.matmul_acc_lhs(product, row_ref[lines, :], load_staged_rhs=0)
+        for unit, product in enumerate(products[K_MAX:]):
+            out_ref[unit * half : (unit + 1) * half, :] = pltpu.matmul_pop(product)
+
+    pl.run_scoped(run, *units)
+
+
+def tile_sum(starts, parts, places, row_weights, col_weights, units):
     pixels = row_weights.shape[0]
     channels = col_weights.shape[-2]
     radials = sum(part.shape[0] for part in parts)
     vmem = pl.BlockSpec(memory_space=pltpu.VMEM)
     return pl.pallas_call(
-        functools.partial(tile_kernel, places),
+        functools.partial(tile_kernel, places, units),
         out_shape=jax.ShapeDtypeStruct((pixels, pixels), jnp.float32),
         in_specs=[vmem] * (len(parts) + 3),
         out_specs=vmem,
         scratch_shapes=[
             pltpu.VMEM((radials, channels), jnp.bfloat16),
-            pltpu.VMEM((K_MAX * SUB, pixels), jnp.bfloat16),
         ],
         compiler_params=pltpu.CompilerParams(vmem_limit_bytes=24 * 1024 * 1024),
         name="tile_sum",
@@ -439,6 +456,7 @@
 
 def per_device(
     units,
+    tile_units,
     field_start,
     phase_table,
     profile_index,
@@ -457,7 +475,7 @@
     )
     parts, places, ready = gather_parts(polar, devices, prepared)
     starts, turned, cols = ready
-    tile_value = tile_sum(starts, parts, places, turned, cols)
+    tile_value = tile_sum(starts, parts, places, turned, cols, tile_units)
     return tile_value.reshape((1, 1) + tile_value.shape)
 
 
@@ -467,8 +485,10 @@
             pltpu.ACC(number // CHUNKS)((RADIX * SUB, 256), jnp.float32)
             for number in range(2 * CHUNKS)
         ]
+        tile_units = [pltpu.ACC(slot % 2)((SUB, 256), jnp.float32) for slot in range(K_MAX)]
+        tile_units += [pltpu.ACC(unit)((128, 256), jnp.float32) for unit in range(2)]
     return jax.shard_map(
-        functools.partial(per_device, units),
+        functools.partial(per_device, units, tile_units),
         mesh=mesh,
         in_specs=(
             P(None, "radial", None),

time: 18.1 us -> 18.1 us (level)
  no operation moved by 1% of the time
where the time goes in v10:
time: 18.1 us; the launch traced here: 17.9 us
  starting transfers between devices  7.95 us (44%)
  Pallas kernels  5.22 us (29%)
  waiting for transfers between devices  4.62 us (26%)
    ppermute x3, starting transfers between devices, gather_parts(): held.append(lax.ppermute(pair, 'radial', routes))  4.45 us
    ppermute x4, starting transfers between devices, swap(): lax.ppermute(value, 'radial', [(i, i ^ distance) for i in range(devices)])  3.5 us
    ppermute x3, waiting for transfers between devices, gather_parts(): held.append(lax.ppermute(pair, 'radial', routes))  3.49 us
    pallas_call x1, Pallas kernels, march(): pl.pallas_call(functools.partial(march_kernel, steps, slabs, units=units)...  2.18 us
    pallas_call x1, Pallas kernels, prepare(): pl.pallas_call(functools.partial(prepare_kernel, local_rows), out_shape=[...  1.71 us
    pallas_call x1, Pallas kernels, tile_sum(): pl.pallas_call(functools.partial(tile_kernel, places, units), out_shape=j...  1.32 us
    ppermute x4, waiting for transfers between devices, swap(): lax.ppermute(value, 'radial', [(i, i ^ distance) for i in range(devices)])  1.13 us
  transfers between devices with their start and end apart: 7, of which 3 were waited for; matrix products, arithmetic and copies ran while one was open for 0% of the time, Pallas kernels for 10%

profile of v10, /device:TPU:0, one launch (start us, length us, event | category | flops | bytes accessed | tf_op | source)
XLA Modules:
  0.0 17.9 jit_solution(17611670588479779210)
XLA Ops:
  0.0 2.2 %march.1 = bf16[64,256]{1,0:T(8,128)(2,1)S(1)} custom-call(s32[2,2]{1,0:T(2,128)} %profile_hbm.1, f32[2]{0:T(128)} %power_hbm.1, s32[2]{0:T(128)} %slot_hbm.1, f32[16,1024]{1,0:T(8,128)} %phase_hbm.1, f32[40,128]{1,0:T(8,128)} %constant.22.clone.wave_hbm, bf16[2,64,1024]{2,1,0:T(8,128)(2,1)} %field_hbm.1, bf16[256,256]{1,0:T(8,128)(2,1)} %constant.23.clone.weight_hbm), custom_call_target="tpu_custom_call" | custom-call | tf_op jit(solution)/shard_map/march/pallas_call | solution.py:272
  2.2 0.5 %collective-permute-start.1 = (bf16[64,256]{1,0:T(8,128)(2,1)S(1)}, bf16[64,256]{1,0:T(8,128)(2,1)S(1)}, u32[]{:S(2)}, u32[]{:S(2)}) collective-permute-start(bf16[64,256]{1,0:T(8,128)(2,1)S(1)} %march.1), channel_id=1, source_target_pairs={{0,1},{1,0},{2,3},{3,2},{4,5},{5,4},{6,7},{7,6},{8,9},{9,8},{10,11... | collective-permute-start | bytes 98312 | tf_op jit(solution)/shard_map/ppermute | solution.py:425
  2.7 2.6 %collective-permute-start = (bf16[64,256]{1,0:T(8,128)(2,1)S(1)}, bf16[64,256]{1,0:T(8,128)(2,1)S(1)}, u32[]{:S(2)}, u32[]{:S(2)}) collective-permute-start(bf16[64,256]{1,0:T(8,128)(2,1)S(1)} %march.1), channel_id=1, source_target_pairs={{0,2},{1,3},{2,0},{3,1},{4,6},{5,7},{6,4},{7,5},{8,10},{9,11},{10,... | collective-permute-start | bytes 98312 | tf_op jit(solution)/shard_map/ppermute | solution.py:425
  5.3 0.0 collective-permute-done.1
  5.3 3.7 %collective-permute-start.4 = (bf16[128,256]{1,0:T(8,128)(2,1)S(1)}, bf16[128,256]{1,0:T(8,128)(2,1)S(1)}, u32[]{:S(2)}, u32[]{:S(2)}) collective-permute-start(bf16[128,256]{1,0:T(8,128)(2,1)S(1)} %maximum_select_fusion.refs_0_), channel_id=1, source_target_pairs={{0,12},{1,15},{2,14},{3,13},{4,8},{5,11},{6,10},{7,9},{8,4},{9,7},... | collective-permute-start | bytes 196616 | tf_op jit(solution)/shard_map/ppermute | solution.py:445
  9.0 0.0 collective-permute-start.3
  9.0 0.8 %collective-permute-start.2 = (bf16[128,256]{1,0:T(8,128)(2,1)S(1)}, bf16[128,256]{1,0:T(8,128)(2,1)S(1)}, u32[]{:S(2)}, u32[]{:S(2)}) collective-permute-start(bf16[128,256]{1,0:T(8,128)(2,1)S(1)} %maximum_select_fusion.refs_0_), channel_id=1, source_target_pairs={{0,8},{1,11},{2,10},{3,9},{4,12},{5,15},{6,14},{7,13},{8,0},{9,3},... | collective-permute-start | bytes 196616 | tf_op jit(solution)/shard_map/ppermute | solution.py:445
  9.7 0.0 collective-permute-done.after_ref
  9.8 1.7 %prepare.1 = (s32[8,128]{1,0:T(8,128)S(1)}, bf16[256,256]{1,0:T(8,128)(2,1)S(1)}, bf16[16,256,256]{2,1,0:T(8,128)(2,1)S(1)}, bf16[64,256]{1,0:T(8,128)(2,1)S(1)}) custom-call(s32[1,16]{1,0:T(1,128)} %shift_hbm.1, s32[1,16,16]{2,1,0:T(8,128)} %sub_hbm.1, s32[1,16]{1,0:T(1,128)} %count_hbm.1, bf16[256,256]{1,0:T(8,128)(2,1)} %bitcast.4, ...), custom_call_target="tpu_custom_call" | custom-call | flops 2000000000 | bytes 2097152 | tf_op jit(solution)/shard_map/prepare/pallas_call | solution.py:342
  11.5 0.7 %collective-permute-done.4.refs_3_ = bf16[128,256]{1,0:T(8,128)(2,1)S(1)} collective-permute-done((bf16[128,256]{1,0:T(8,128)(2,1)S(1)}, bf16[128,256]{1,0:T(8,128)(2,1)S(1)}, u32[]{:S(2)}, u32[]{:S(2)}) %collective-permute-start.4) | collective-permute-done | bytes 65568 | tf_op jit(solution)/shard_map/ppermute | solution.py:445
  12.2 0.2 collective-permute-start.6
  12.3 2.8 %collective-permute-done.3.refs_2_ = bf16[128,256]{1,0:T(8,128)(2,1)S(1)} collective-permute-done((bf16[128,256]{1,0:T(8,128)(2,1)S(1)}, bf16[128,256]{1,0:T(8,128)(2,1)S(1)}, u32[]{:S(2)}, u32[]{:S(2)}) %collective-permute-start.3) | collective-permute-done | bytes 65568 | tf_op jit(solution)/shard_map/ppermute | solution.py:445
  15.1 0.0 collective-permute-done.2.refs_1_
  15.2 0.3 %collective-permute-start.5 = (bf16[256,256]{1,0:T(8,128)(2,1)S(1)}, bf16[256,256]{1,0:T(8,128)(2,1)S(1)}, u32[]{:S(2)}, u32[]{:S(2)}) collective-permute-start(bf16[256,256]{1,0:T(8,128)(2,1)S(1)} %pad_maximum_fusion), channel_id=1, source_target_pairs={{0,1},{1,0},{2,3},{3,2},{4,5},{5,4},{6,7},{7,6},{8,9},{9,8},{10,11... | collective-permute-start | bytes 393224 | tf_op jit(solution)/shard_map/ppermute | solution.py:425
  15.4 0.0 collective-permute-done.6
  15.5 1.1 %collective-permute-done.5 = bf16[256,256]{1,0:T(8,128)(2,1)S(1)} collective-permute-done((bf16[256,256]{1,0:T(8,128)(2,1)S(1)}, bf16[256,256]{1,0:T(8,128)(2,1)S(1)}, u32[]{:S(2)}, u32[]{:S(2)}) %collective-permute-start.5) | collective-permute-done | bytes 131104 | tf_op jit(solution)/shard_map/ppermute | solution.py:425
  16.6 1.3 %tile_sum.1 = f32[256,256]{1,0:T(8,128)} custom-call(s32[8,128]{1,0:T(8,128)S(1)} %get-tuple-element.9.starts_ref, bf16[128,256]{1,0:T(8,128)(2,1)S(1)} %maximum_select_fusion.refs_0_, bf16[128,256]{1,0:T(8,128)(2,1)S(1)} %collective-permute-done.2.refs_1_, bf16[128,256]{1,0:T(8,128)(2,1)S(1)} %collective-permute-done.3.refs_2_, ...), custom_call_target="tpu_custom_call" | custom-call | tf_op jit(solution)/shard_map/tile_sum/pallas_call | solution.py:406
  (7 shorter events, 0.1 us)
Async XLA Ops:
  2.2 3.1 %collective-permute-start.1 = (bf16[64,256]{1,0:T(8,128)(2,1)S(1)}, bf16[64,256]{1,0:T(8,128)(2,1)S(1)}, u32[]{:S(2)}, u32[]{:S(2)}) collective-permute-start(bf16[64,256]{1,0:T(8,128)(2,1)S(1)} %march.1), channel_id=1, source_target_pairs={{0,1},{1,0},{2,3},{3,2},{4,5},{5,4},{6,7},{7,6},{8,9},{9,8},{10,11... | collective-permute-start | bytes 98312 | tf_op jit(solution)/shard_map/ppermute | solution.py:425
  2.7 7.0 %collective-permute-start = (bf16[64,256]{1,0:T(8,128)(2,1)S(1)}, bf16[64,256]{1,0:T(8,128)(2,1)S(1)}, u32[]{:S(2)}, u32[]{:S(2)}) collective-permute-start(bf16[64,256]{1,0:T(8,128)(2,1)S(1)} %march.1), channel_id=1, source_target_pairs={{0,2},{1,3},{2,0},{3,1},{4,6},{5,7},{6,4},{7,5},{8,10},{9,11},{10,... | collective-permute-start | bytes 98312 | tf_op jit(solution)/shard_map/ppermute | solution.py:425
  5.3 6.9 %collective-permute-start.4 = (bf16[128,256]{1,0:T(8,128)(2,1)S(1)}, bf16[128,256]{1,0:T(8,128)(2,1)S(1)}, u32[]{:S(2)}, u32[]{:S(2)}) collective-permute-start(bf16[128,256]{1,0:T(8,128)(2,1)S(1)} %maximum_select_fusion.refs_0_), channel_id=1, source_target_pairs={{0,12},{1,15},{2,14},{3,13},{4,8},{5,11},{6,10},{7,9},{8,4},{9,7},... | collective-permute-start | bytes 196616 | tf_op jit(solution)/shard_map/ppermute | solution.py:445
  9.0 6.2 %collective-permute-start.3 = (bf16[128,256]{1,0:T(8,128)(2,1)S(1)}, bf16[128,256]{1,0:T(8,128)(2,1)S(1)}, u32[]{:S(2)}, u32[]{:S(2)}) collective-permute-start(bf16[128,256]{1,0:T(8,128)(2,1)S(1)} %maximum_select_fusion.refs_0_), channel_id=1, source_target_pairs={{0,4},{1,7},{2,6},{3,5},{4,0},{5,3},{6,2},{7,1},{8,12},{9,15},{10,... | collective-permute-start | bytes 196616 | tf_op jit(solution)/shard_map/ppermute | solution.py:445
  9.0 6.2 %collective-permute-start.2 = (bf16[128,256]{1,0:T(8,128)(2,1)S(1)}, bf16[128,256]{1,0:T(8,128)(2,1)S(1)}, u32[]{:S(2)}, u32[]{:S(2)}) collective-permute-start(bf16[128,256]{1,0:T(8,128)(2,1)S(1)} %maximum_select_fusion.refs_0_), channel_id=1, source_target_pairs={{0,8},{1,11},{2,10},{3,9},{4,12},{5,15},{6,14},{7,13},{8,0},{9,3},... | collective-permute-start | bytes 196616 | tf_op jit(solution)/shard_map/ppermute | solution.py:445
  12.2 3.2 %collective-permute-start.6 = (bf16[192,256]{1,0:T(8,128)(2,1)S(1)}, bf16[192,256]{1,0:T(8,128)(2,1)S(1)}, u32[]{:S(2)}, u32[]{:S(2)}) collective-permute-start(bf16[192,256]{1,0:T(8,128)(2,1)S(1)} %pad_maximum_fusion.1), channel_id=1, source_target_pairs={{0,1},{1,0},{2,3},{3,2},{4,5},{5,4},{6,7},{7,6},{8,9},{9,8},{10,11... | collective-permute-start | bytes 294920 | tf_op jit(solution)/shard_map/ppermute | solution.py:425
  15.2 1.4 %collective-permute-start.5 = (bf16[256,256]{1,0:T(8,128)(2,1)S(1)}, bf16[256,256]{1,0:T(8,128)(2,1)S(1)}, u32[]{:S(2)}, u32[]{:S(2)}) collective-permute-start(bf16[256,256]{1,0:T(8,128)(2,1)S(1)} %pad_maximum_fusion), channel_id=1, source_target_pairs={{0,1},{1,0},{2,3},{3,2},{4,5},{5,4},{6,7},{7,6},{8,9},{9,8},{10,11... | collective-permute-start | bytes 393224 | tf_op jit(solution)/shard_map/ppermute | solution.py:425

commit v11 on v9

--- a/solution.py
+++ b/solution.py
@@ -365,12 +365,13 @@
     row_ref, col_ref, out_ref, polar_ref, mixed_ref = refs[len(places) :]
     chip = lax.axis_index("radial") // 2
     core = lax.axis_index("radial") % 2
-    for (even, odd), part_ref in zip(places, part_refs):
-        size = part_ref.shape[0]
-        start = jnp.where(core == 0, chip ^ even, chip ^ odd) * size
-        if size == polar_ref.shape[0]:
-            start = 0
-        polar_ref[pl.ds(start, size), :] = part_ref[...]
+    for pieces, part_ref in zip(places, part_refs):
+        size = part_ref.shape[0] // len(pieces)
+        for piece, (even, odd) in enumerate(pieces):
+            start = jnp.where(core == 0, chip ^ even, chip ^ odd) * size
+            if size == polar_ref.shape[0]:
+                start = 0
+            polar_ref[pl.ds(start, size), :] = part_ref[piece * size : (piece + 1) * size, :]
     starts = [starts_ref[0:1, slot : slot + 1][0, 0] for slot in range(K_MAX)]
     for slot, start in enumerate(starts):
         block = polar_ref[pl.ds(pl.multiple_of(jnp.maximum(start, 0), SUB), SUB), :]
@@ -411,7 +412,7 @@
 def gather_parts(polar, devices, prepared):
     if devices != 16:
         whole = lax.all_gather(polar, "radial", axis=0, tiled=True)
-        return [whole], [(0, 0)], prepared(polar)[:3]
+        return [whole], [[(0, 0)]], prepared(polar)[:3]
     core = lax.axis_index("radial") % 2
     size = 2 * polar.shape[0]
 
@@ -429,11 +430,8 @@
     *ready, first = prepared(first)
     early = swap(jnp.concatenate([held[2], first], 0), 1, devices)
     late = swap(jnp.concatenate(held[:2], 0), 1, devices)
-    parts = [pair] + held
-    parts += [late[i * size : (i + 1) * size] for i in range(2)]
-    parts += [early[i * size : (i + 1) * size] for i in range(1)]
-    parts.append(in_order(first, early[1 * size :]))
-    places = [(0, 0), (4, 5), (2, 3), (6, 7), (5, 4), (3, 2), (7, 6), (1, 1)]
+    parts = [pair] + held + [late, early[:size], in_order(first, early[size:])]
+    places = [[(0, 0)], [(4, 5)], [(2, 3)], [(6, 7)], [(5, 4), (3, 2)], [(7, 6)], [(1, 1)]]
     return parts, places, ready
 
 

time: 18.1 us -> 18.1 us (level)
  no operation moved by 1% of the time
where the time goes in v11:
time: 18.1 us; the launch traced here: 17.9 us
  starting transfers between devices  7.95 us (44%)
  Pallas kernels  5.27 us (29%)
  waiting for transfers between devices  4.62 us (26%)
    ppermute x3, starting transfers between devices, gather_parts(): held.append(lax.ppermute(pair, 'radial', routes))  4.45 us
    ppermute x4, starting transfers between devices, swap(): lax.ppermute(value, 'radial', [(i, i ^ distance) for i in range(devices)])  3.5 us
    ppermute x3, waiting for transfers between devices, gather_parts(): held.append(lax.ppermute(pair, 'radial', routes))  3.49 us
    pallas_call x1, Pallas kernels, march(): pl.pallas_call(functools.partial(march_kernel, steps, slabs, units=units)...  2.18 us
    pallas_call x1, Pallas kernels, prepare(): pl.pallas_call(functools.partial(prepare_kernel, local_rows), out_shape=[...  1.71 us
    pallas_call x1, Pallas kernels, tile_sum(): pl.pallas_call(functools.partial(tile_kernel, places), out_shape=jax.Shap...  1.37 us
    ppermute x4, waiting for transfers between devices, swap(): lax.ppermute(value, 'radial', [(i, i ^ distance) for i in range(devices)])  1.13 us
  transfers between devices with their start and end apart: 7, of which 3 were waited for; matrix products, arithmetic and copies ran while one was open for 0% of the time, Pallas kernels for 10%

profile of v11, /device:TPU:0, one launch (start us, length us, event | category | flops | bytes accessed | tf_op | source)
XLA Modules:
  0.0 17.9 jit_solution(9946059028345314150)
XLA Ops:
  0.0 2.2 %march.1 = bf16[64,256]{1,0:T(8,128)(2,1)S(1)} custom-call(s32[2,2]{1,0:T(2,128)} %profile_hbm.1, f32[2]{0:T(128)} %power_hbm.1, s32[2]{0:T(128)} %slot_hbm.1, f32[16,1024]{1,0:T(8,128)} %phase_hbm.1, f32[40,128]{1,0:T(8,128)} %constant.22.clone.wave_hbm, bf16[2,64,1024]{2,1,0:T(8,128)(2,1)} %field_hbm.1, bf16[256,256]{1,0:T(8,128)(2,1)} %constant.23.clone.weight_hbm), custom_call_target="tpu_custom_call" | custom-call | tf_op jit(solution)/shard_map/march/pallas_call | solution.py:272
  2.2 0.5 %collective-permute-start.1 = (bf16[64,256]{1,0:T(8,128)(2,1)S(1)}, bf16[64,256]{1,0:T(8,128)(2,1)S(1)}, u32[]{:S(2)}, u32[]{:S(2)}) collective-permute-start(bf16[64,256]{1,0:T(8,128)(2,1)S(1)} %march.1), channel_id=1, source_target_pairs={{0,1},{1,0},{2,3},{3,2},{4,5},{5,4},{6,7},{7,6},{8,9},{9,8},{10,11... | collective-permute-start | bytes 98312 | tf_op jit(solution)/shard_map/ppermute | solution.py:409
  2.7 2.6 %collective-permute-start = (bf16[64,256]{1,0:T(8,128)(2,1)S(1)}, bf16[64,256]{1,0:T(8,128)(2,1)S(1)}, u32[]{:S(2)}, u32[]{:S(2)}) collective-permute-start(bf16[64,256]{1,0:T(8,128)(2,1)S(1)} %march.1), channel_id=1, source_target_pairs={{0,2},{1,3},{2,0},{3,1},{4,6},{5,7},{6,4},{7,5},{8,10},{9,11},{10,... | collective-permute-start | bytes 98312 | tf_op jit(solution)/shard_map/ppermute | solution.py:409
  5.3 0.0 collective-permute-done.1
  5.3 3.7 %collective-permute-start.4 = (bf16[128,256]{1,0:T(8,128)(2,1)S(1)}, bf16[128,256]{1,0:T(8,128)(2,1)S(1)}, u32[]{:S(2)}, u32[]{:S(2)}) collective-permute-start(bf16[128,256]{1,0:T(8,128)(2,1)S(1)} %maximum_select_fusion.refs_0_), channel_id=1, source_target_pairs={{0,12},{1,15},{2,14},{3,13},{4,8},{5,11},{6,10},{7,9},{8,4},{9,7},... | collective-permute-start | bytes 196616 | tf_op jit(solution)/shard_map/ppermute | solution.py:429
  9.0 0.0 collective-permute-start.3
  9.0 0.8 %collective-permute-start.2 = (bf16[128,256]{1,0:T(8,128)(2,1)S(1)}, bf16[128,256]{1,0:T(8,128)(2,1)S(1)}, u32[]{:S(2)}, u32[]{:S(2)}) collective-permute-start(bf16[128,256]{1,0:T(8,128)(2,1)S(1)} %maximum_select_fusion.refs_0_), channel_id=1, source_target_pairs={{0,8},{1,11},{2,10},{3,9},{4,12},{5,15},{6,14},{7,13},{8,0},{9,3},... | collective-permute-start | bytes 196616 | tf_op jit(solution)/shard_map/ppermute | solution.py:429
  9.7 0.0 collective-permute-done.after_ref
  9.8 1.7 %prepare.1 = (s32[8,128]{1,0:T(8,128)S(1)}, bf16[256,256]{1,0:T(8,128)(2,1)S(1)}, bf16[16,256,256]{2,1,0:T(8,128)(2,1)S(1)}, bf16[64,256]{1,0:T(8,128)(2,1)S(1)}) custom-call(s32[1,16]{1,0:T(1,128)} %shift_hbm.1, s32[1,16,16]{2,1,0:T(8,128)} %sub_hbm.1, s32[1,16]{1,0:T(1,128)} %count_hbm.1, bf16[256,256]{1,0:T(8,128)(2,1)} %bitcast.4, ...), custom_call_target="tpu_custom_call" | custom-call | flops 2000000000 | bytes 2097152 | tf_op jit(solution)/shard_map/prepare/pallas_call | solution.py:342
  11.5 0.7 %collective-permute-done.4.refs_3_ = bf16[128,256]{1,0:T(8,128)(2,1)S(1)} collective-permute-done((bf16[128,256]{1,0:T(8,128)(2,1)S(1)}, bf16[128,256]{1,0:T(8,128)(2,1)S(1)}, u32[]{:S(2)}, u32[]{:S(2)}) %collective-permute-start.4) | collective-permute-done | bytes 65568 | tf_op jit(solution)/shard_map/ppermute | solution.py:429
  12.2 0.2 collective-permute-start.6
  12.3 2.8 %collective-permute-done.3.refs_2_ = bf16[128,256]{1,0:T(8,128)(2,1)S(1)} collective-permute-done((bf16[128,256]{1,0:T(8,128)(2,1)S(1)}, bf16[128,256]{1,0:T(8,128)(2,1)S(1)}, u32[]{:S(2)}, u32[]{:S(2)}) %collective-permute-start.3) | collective-permute-done | bytes 65568 | tf_op jit(solution)/shard_map/ppermute | solution.py:429
  15.1 0.0 collective-permute-done.2.refs_1_
  15.2 0.3 %collective-permute-start.5 = (bf16[256,256]{1,0:T(8,128)(2,1)S(1)}, bf16[256,256]{1,0:T(8,128)(2,1)S(1)}, u32[]{:S(2)}, u32[]{:S(2)}) collective-permute-start(bf16[256,256]{1,0:T(8,128)(2,1)S(1)} %pad_maximum_fusion), channel_id=1, source_target_pairs={{0,1},{1,0},{2,3},{3,2},{4,5},{5,4},{6,7},{7,6},{8,9},{9,8},{10,11... | collective-permute-start | bytes 393224 | tf_op jit(solution)/shard_map/ppermute | solution.py:409
  15.4 0.0 collective-permute-done.6
  15.5 1.1 %collective-permute-done.5.refs_4_ = bf16[256,256]{1,0:T(8,128)(2,1)S(1)} collective-permute-done((bf16[256,256]{1,0:T(8,128)(2,1)S(1)}, bf16[256,256]{1,0:T(8,128)(2,1)S(1)}, u32[]{:S(2)}, u32[]{:S(2)}) %collective-permute-start.5) | collective-permute-done | bytes 131104 | tf_op jit(solution)/shard_map/ppermute | solution.py:409
  16.6 1.4 %tile_sum.1 = f32[256,256]{1,0:T(8,128)} custom-call(s32[8,128]{1,0:T(8,128)S(1)} %get-tuple-element.9.starts_ref, bf16[128,256]{1,0:T(8,128)(2,1)S(1)} %maximum_select_fusion.refs_0_, bf16[128,256]{1,0:T(8,128)(2,1)S(1)} %collective-permute-done.2.refs_1_, bf16[128,256]{1,0:T(8,128)(2,1)S(1)} %collective-permute-done.3.refs_2_, ...), custom_call_target="tpu_custom_call" | custom-call | tf_op jit(solution)/shard_map/tile_sum/pallas_call | solution.py:389
  (6 shorter events, 0.1 us)
Async XLA Ops:
  2.2 3.1 %collective-permute-start.1 = (bf16[64,256]{1,0:T(8,128)(2,1)S(1)}, bf16[64,256]{1,0:T(8,128)(2,1)S(1)}, u32[]{:S(2)}, u32[]{:S(2)}) collective-permute-start(bf16[64,256]{1,0:T(8,128)(2,1)S(1)} %march.1), channel_id=1, source_target_pairs={{0,1},{1,0},{2,3},{3,2},{4,5},{5,4},{6,7},{7,6},{8,9},{9,8},{10,11... | collective-permute-start | bytes 98312 | tf_op jit(solution)/shard_map/ppermute | solution.py:409
  2.7 7.0 %collective-permute-start = (bf16[64,256]{1,0:T(8,128)(2,1)S(1)}, bf16[64,256]{1,0:T(8,128)(2,1)S(1)}, u32[]{:S(2)}, u32[]{:S(2)}) collective-permute-start(bf16[64,256]{1,0:T(8,128)(2,1)S(1)} %march.1), channel_id=1, source_target_pairs={{0,2},{1,3},{2,0},{3,1},{4,6},{5,7},{6,4},{7,5},{8,10},{9,11},{10,... | collective-permute-start | bytes 98312 | tf_op jit(solution)/shard_map/ppermute | solution.py:409
  5.3 6.9 %collective-permute-start.4 = (bf16[128,256]{1,0:T(8,128)(2,1)S(1)}, bf16[128,256]{1,0:T(8,128)(2,1)S(1)}, u32[]{:S(2)}, u32[]{:S(2)}) collective-permute-start(bf16[128,256]{1,0:T(8,128)(2,1)S(1)} %maximum_select_fusion.refs_0_), channel_id=1, source_target_pairs={{0,12},{1,15},{2,14},{3,13},{4,8},{5,11},{6,10},{7,9},{8,4},{9,7},... | collective-permute-start | bytes 196616 | tf_op jit(solution)/shard_map/ppermute | solution.py:429
  9.0 6.2 %collective-permute-start.3 = (bf16[128,256]{1,0:T(8,128)(2,1)S(1)}, bf16[128,256]{1,0:T(8,128)(2,1)S(1)}, u32[]{:S(2)}, u32[]{:S(2)}) collective-permute-start(bf16[128,256]{1,0:T(8,128)(2,1)S(1)} %maximum_select_fusion.refs_0_), channel_id=1, source_target_pairs={{0,4},{1,7},{2,6},{3,5},{4,0},{5,3},{6,2},{7,1},{8,12},{9,15},{10,... | collective-permute-start | bytes 196616 | tf_op jit(solution)/shard_map/ppermute | solution.py:429
  9.0 6.2 %collective-permute-start.2 = (bf16[128,256]{1,0:T(8,128)(2,1)S(1)}, bf16[128,256]{1,0:T(8,128)(2,1)S(1)}, u32[]{:S(2)}, u32[]{:S(2)}) collective-permute-start(bf16[128,256]{1,0:T(8,128)(2,1)S(1)} %maximum_select_fusion.refs_0_), channel_id=1, source_target_pairs={{0,8},{1,11},{2,10},{3,9},{4,12},{5,15},{6,14},{7,13},{8,0},{9,3},... | collective-permute-start | bytes 196616 | tf_op jit(solution)/shard_map/ppermute | solution.py:429
  12.2 3.2 %collective-permute-start.6 = (bf16[192,256]{1,0:T(8,128)(2,1)S(1)}, bf16[192,256]{1,0:T(8,128)(2,1)S(1)}, u32[]{:S(2)}, u32[]{:S(2)}) collective-permute-start(bf16[192,256]{1,0:T(8,128)(2,1)S(1)} %pad_maximum_fusion.1), channel_id=1, source_target_pairs={{0,1},{1,0},{2,3},{3,2},{4,5},{5,4},{6,7},{7,6},{8,9},{9,8},{10,11... | collective-permute-start | bytes 294920 | tf_op jit(solution)/shard_map/ppermute | solution.py:409
  15.2 1.4 %collective-permute-start.5 = (bf16[256,256]{1,0:T(8,128)(2,1)S(1)}, bf16[256,256]{1,0:T(8,128)(2,1)S(1)}, u32[]{:S(2)}, u32[]{:S(2)}) collective-permute-start(bf16[256,256]{1,0:T(8,128)(2,1)S(1)} %pad_maximum_fusion), channel_id=1, source_target_pairs={{0,1},{1,0},{2,3},{3,2},{4,5},{5,4},{6,7},{7,6},{8,9},{9,8},{10,11... | collective-permute-start | bytes 393224 | tf_op jit(solution)/shard_map/ppermute | solution.py:409

commit v12 on v9

--- a/solution.py
+++ b/solution.py
@@ -226,7 +226,7 @@
                 for chunk in range(chunks):
                     start = chunks * step + chunk
                     events.append((start, "forward", step, chunk))
-                    events.append((start + 1.5, "middle", step, chunk))
+                    events.append((start + 0.6, "middle", step, chunk))
             for chunk in range(chunks):
                 events.append((chunks * steps + chunk, "leave", steps, chunk))
             for _, kind, step, chunk in sorted(events):

time: 18.1 us -> 18.1 us (level)
  no operation moved by 1% of the time
where the time goes in v12:
time: 18.1 us; the launch traced here: 18 us
  starting transfers between devices  7.95 us (44%)
  Pallas kernels  5.27 us (29%)
  waiting for transfers between devices  4.62 us (26%)
    ppermute x3, starting transfers between devices, gather_parts(): held.append(lax.ppermute(pair, 'radial', routes))  4.45 us
    ppermute x4, starting transfers between devices, swap(): lax.ppermute(value, 'radial', [(i, i ^ distance) for i in range(devices)])  3.5 us
    ppermute x3, waiting for transfers between devices, gather_parts(): held.append(lax.ppermute(pair, 'radial', routes))  3.49 us
    pallas_call x1, Pallas kernels, march(): pl.pallas_call(functools.partial(march_kernel, steps, slabs, units=units)...  2.18 us
    pallas_call x1, Pallas kernels, prepare(): pl.pallas_call(functools.partial(prepare_kernel, local_rows), out_shape=[...  1.71 us
    pallas_call x1, Pallas kernels, tile_sum(): pl.pallas_call(functools.partial(tile_kernel, places), out_shape=jax.Shap...  1.38 us
    ppermute x4, waiting for transfers between devices, swap(): lax.ppermute(value, 'radial', [(i, i ^ distance) for i in range(devices)])  1.13 us
  transfers between devices with their start and end apart: 7, of which 3 were waited for; matrix products, arithmetic and copies ran while one was open for 0% of the time, Pallas kernels for 10%

profile of v12, /device:TPU:0, one launch (start us, length us, event | category | flops | bytes accessed | tf_op | source)
XLA Modules:
  0.0 18.0 jit_solution(2486080471570351714)
XLA Ops:
  0.0 2.2 %march.1 = bf16[64,256]{1,0:T(8,128)(2,1)S(1)} custom-call(s32[2,2]{1,0:T(2,128)} %profile_hbm.1, f32[2]{0:T(128)} %power_hbm.1, s32[2]{0:T(128)} %slot_hbm.1, f32[16,1024]{1,0:T(8,128)} %phase_hbm.1, f32[40,128]{1,0:T(8,128)} %constant.22.clone.wave_hbm, bf16[2,64,1024]{2,1,0:T(8,128)(2,1)} %field_hbm.1, bf16[256,256]{1,0:T(8,128)(2,1)} %constant.23.clone.weight_hbm), custom_call_target="tpu_custom_call" | custom-call | tf_op jit(solution)/shard_map/march/pallas_call | solution.py:272
  2.2 0.5 %collective-permute-start.1 = (bf16[64,256]{1,0:T(8,128)(2,1)S(1)}, bf16[64,256]{1,0:T(8,128)(2,1)S(1)}, u32[]{:S(2)}, u32[]{:S(2)}) collective-permute-start(bf16[64,256]{1,0:T(8,128)(2,1)S(1)} %march.1), channel_id=1, source_target_pairs={{0,1},{1,0},{2,3},{3,2},{4,5},{5,4},{6,7},{7,6},{8,9},{9,8},{10,11... | collective-permute-start | bytes 98312 | tf_op jit(solution)/shard_map/ppermute | solution.py:408
  2.7 2.6 %collective-permute-start = (bf16[64,256]{1,0:T(8,128)(2,1)S(1)}, bf16[64,256]{1,0:T(8,128)(2,1)S(1)}, u32[]{:S(2)}, u32[]{:S(2)}) collective-permute-start(bf16[64,256]{1,0:T(8,128)(2,1)S(1)} %march.1), channel_id=1, source_target_pairs={{0,2},{1,3},{2,0},{3,1},{4,6},{5,7},{6,4},{7,5},{8,10},{9,11},{10,... | collective-permute-start | bytes 98312 | tf_op jit(solution)/shard_map/ppermute | solution.py:408
  5.3 0.0 collective-permute-done.1
  5.3 3.7 %collective-permute-start.4 = (bf16[128,256]{1,0:T(8,128)(2,1)S(1)}, bf16[128,256]{1,0:T(8,128)(2,1)S(1)}, u32[]{:S(2)}, u32[]{:S(2)}) collective-permute-start(bf16[128,256]{1,0:T(8,128)(2,1)S(1)} %maximum_select_fusion.refs_0_), channel_id=1, source_target_pairs={{0,12},{1,15},{2,14},{3,13},{4,8},{5,11},{6,10},{7,9},{8,4},{9,7},... | collective-permute-start | bytes 196616 | tf_op jit(solution)/shard_map/ppermute | solution.py:428
  9.0 0.0 collective-permute-start.3
  9.0 0.8 %collective-permute-start.2 = (bf16[128,256]{1,0:T(8,128)(2,1)S(1)}, bf16[128,256]{1,0:T(8,128)(2,1)S(1)}, u32[]{:S(2)}, u32[]{:S(2)}) collective-permute-start(bf16[128,256]{1,0:T(8,128)(2,1)S(1)} %maximum_select_fusion.refs_0_), channel_id=1, source_target_pairs={{0,8},{1,11},{2,10},{3,9},{4,12},{5,15},{6,14},{7,13},{8,0},{9,3},... | collective-permute-start | bytes 196616 | tf_op jit(solution)/shard_map/ppermute | solution.py:428
  9.7 0.0 collective-permute-done.after_ref
  9.8 1.7 %prepare.1 = (s32[8,128]{1,0:T(8,128)S(1)}, bf16[256,256]{1,0:T(8,128)(2,1)S(1)}, bf16[16,256,256]{2,1,0:T(8,128)(2,1)S(1)}, bf16[64,256]{1,0:T(8,128)(2,1)S(1)}) custom-call(s32[1,16]{1,0:T(1,128)} %shift_hbm.1, s32[1,16,16]{2,1,0:T(8,128)} %sub_hbm.1, s32[1,16]{1,0:T(1,128)} %count_hbm.1, bf16[256,256]{1,0:T(8,128)(2,1)} %bitcast.4, ...), custom_call_target="tpu_custom_call" | custom-call | flops 2000000000 | bytes 2097152 | tf_op jit(solution)/shard_map/prepare/pallas_call | solution.py:342
  11.5 0.7 %collective-permute-done.4.refs_3_ = bf16[128,256]{1,0:T(8,128)(2,1)S(1)} collective-permute-done((bf16[128,256]{1,0:T(8,128)(2,1)S(1)}, bf16[128,256]{1,0:T(8,128)(2,1)S(1)}, u32[]{:S(2)}, u32[]{:S(2)}) %collective-permute-start.4) | collective-permute-done | bytes 65568 | tf_op jit(solution)/shard_map/ppermute | solution.py:428
  12.2 0.2 collective-permute-start.6
  12.3 2.8 %collective-permute-done.3.refs_2_ = bf16[128,256]{1,0:T(8,128)(2,1)S(1)} collective-permute-done((bf16[128,256]{1,0:T(8,128)(2,1)S(1)}, bf16[128,256]{1,0:T(8,128)(2,1)S(1)}, u32[]{:S(2)}, u32[]{:S(2)}) %collective-permute-start.3) | collective-permute-done | bytes 65568 | tf_op jit(solution)/shard_map/ppermute | solution.py:428
  15.1 0.0 collective-permute-done.2.refs_1_
  15.2 0.3 %collective-permute-start.5 = (bf16[256,256]{1,0:T(8,128)(2,1)S(1)}, bf16[256,256]{1,0:T(8,128)(2,1)S(1)}, u32[]{:S(2)}, u32[]{:S(2)}) collective-permute-start(bf16[256,256]{1,0:T(8,128)(2,1)S(1)} %pad_maximum_fusion), channel_id=1, source_target_pairs={{0,1},{1,0},{2,3},{3,2},{4,5},{5,4},{6,7},{7,6},{8,9},{9,8},{10,11... | collective-permute-start | bytes 393224 | tf_op jit(solution)/shard_map/ppermute | solution.py:408
  15.4 0.0 collective-permute-done.6
  15.5 1.1 %collective-permute-done.5 = bf16[256,256]{1,0:T(8,128)(2,1)S(1)} collective-permute-done((bf16[256,256]{1,0:T(8,128)(2,1)S(1)}, bf16[256,256]{1,0:T(8,128)(2,1)S(1)}, u32[]{:S(2)}, u32[]{:S(2)}) %collective-permute-start.5) | collective-permute-done | bytes 131104 | tf_op jit(solution)/shard_map/ppermute | solution.py:408
  16.6 1.4 %tile_sum.1 = f32[256,256]{1,0:T(8,128)} custom-call(s32[8,128]{1,0:T(8,128)S(1)} %get-tuple-element.9.starts_ref, bf16[128,256]{1,0:T(8,128)(2,1)S(1)} %maximum_select_fusion.refs_0_, bf16[128,256]{1,0:T(8,128)(2,1)S(1)} %collective-permute-done.2.refs_1_, bf16[128,256]{1,0:T(8,128)(2,1)S(1)} %collective-permute-done.3.refs_2_, ...), custom_call_target="tpu_custom_call" | custom-call | tf_op jit(solution)/shard_map/tile_sum/pallas_call | solution.py:388
  (7 shorter events, 0.1 us)
Async XLA Ops:
  2.2 3.1 %collective-permute-start.1 = (bf16[64,256]{1,0:T(8,128)(2,1)S(1)}, bf16[64,256]{1,0:T(8,128)(2,1)S(1)}, u32[]{:S(2)}, u32[]{:S(2)}) collective-permute-start(bf16[64,256]{1,0:T(8,128)(2,1)S(1)} %march.1), channel_id=1, source_target_pairs={{0,1},{1,0},{2,3},{3,2},{4,5},{5,4},{6,7},{7,6},{8,9},{9,8},{10,11... | collective-permute-start | bytes 98312 | tf_op jit(solution)/shard_map/ppermute | solution.py:408
  2.7 7.0 %collective-permute-start = (bf16[64,256]{1,0:T(8,128)(2,1)S(1)}, bf16[64,256]{1,0:T(8,128)(2,1)S(1)}, u32[]{:S(2)}, u32[]{:S(2)}) collective-permute-start(bf16[64,256]{1,0:T(8,128)(2,1)S(1)} %march.1), channel_id=1, source_target_pairs={{0,2},{1,3},{2,0},{3,1},{4,6},{5,7},{6,4},{7,5},{8,10},{9,11},{10,... | collective-permute-start | bytes 98312 | tf_op jit(solution)/shard_map/ppermute | solution.py:408
  5.3 6.9 %collective-permute-start.4 = (bf16[128,256]{1,0:T(8,128)(2,1)S(1)}, bf16[128,256]{1,0:T(8,128)(2,1)S(1)}, u32[]{:S(2)}, u32[]{:S(2)}) collective-permute-start(bf16[128,256]{1,0:T(8,128)(2,1)S(1)} %maximum_select_fusion.refs_0_), channel_id=1, source_target_pairs={{0,12},{1,15},{2,14},{3,13},{4,8},{5,11},{6,10},{7,9},{8,4},{9,7},... | collective-permute-start | bytes 196616 | tf_op jit(solution)/shard_map/ppermute | solution.py:428
  9.0 6.2 %collective-permute-start.3 = (bf16[128,256]{1,0:T(8,128)(2,1)S(1)}, bf16[128,256]{1,0:T(8,128)(2,1)S(1)}, u32[]{:S(2)}, u32[]{:S(2)}) collective-permute-start(bf16[128,256]{1,0:T(8,128)(2,1)S(1)} %maximum_select_fusion.refs_0_), channel_id=1, source_target_pairs={{0,4},{1,7},{2,6},{3,5},{4,0},{5,3},{6,2},{7,1},{8,12},{9,15},{10,... | collective-permute-start | bytes 196616 | tf_op jit(solution)/shard_map/ppermute | solution.py:428
  9.0 6.2 %collective-permute-start.2 = (bf16[128,256]{1,0:T(8,128)(2,1)S(1)}, bf16[128,256]{1,0:T(8,128)(2,1)S(1)}, u32[]{:S(2)}, u32[]{:S(2)}) collective-permute-start(bf16[128,256]{1,0:T(8,128)(2,1)S(1)} %maximum_select_fusion.refs_0_), channel_id=1, source_target_pairs={{0,8},{1,11},{2,10},{3,9},{4,12},{5,15},{6,14},{7,13},{8,0},{9,3},... | collective-permute-start | bytes 196616 | tf_op jit(solution)/shard_map/ppermute | solution.py:428
  12.2 3.2 %collective-permute-start.6 = (bf16[192,256]{1,0:T(8,128)(2,1)S(1)}, bf16[192,256]{1,0:T(8,128)(2,1)S(1)}, u32[]{:S(2)}, u32[]{:S(2)}) collective-permute-start(bf16[192,256]{1,0:T(8,128)(2,1)S(1)} %pad_maximum_fusion.1), channel_id=1, source_target_pairs={{0,1},{1,0},{2,3},{3,2},{4,5},{5,4},{6,7},{7,6},{8,9},{9,8},{10,11... | collective-permute-start | bytes 294920 | tf_op jit(solution)/shard_map/ppermute | solution.py:408
  15.2 1.4 %collective-permute-start.5 = (bf16[256,256]{1,0:T(8,128)(2,1)S(1)}, bf16[256,256]{1,0:T(8,128)(2,1)S(1)}, u32[]{:S(2)}, u32[]{:S(2)}) collective-permute-start(bf16[256,256]{1,0:T(8,128)(2,1)S(1)} %pad_maximum_fusion), channel_id=1, source_target_pairs={{0,1},{1,0},{2,3},{3,2},{4,5},{5,4},{6,7},{7,6},{8,9},{9,8},{10,11... | collective-permute-start | bytes 393224 | tf_op jit(solution)/shard_map/ppermute | solution.py:408
